TPU v7x, 32 devices: a whole 2x2x4 slice. The times are simulated.
32 devices in a mesh: dp: 2 (over core), row: 4 (over y, x), col: 4 (over z).
Axes of the slice: x: 2, y: 2, z: 4, core: 2. Of those that a mesh axis runs over, the one named last changes fastest.
Arguments:
- states: float32 [5120, 1024], P(('dp', 'row'), 'col'), may hold values from -6 to 6
- teacher: bfloat16 [5120, 1024], P(('dp', 'row'), 'col'), may hold values from -6 to 6
- cotangent: float32 [5120, 1024], P(('dp', 'row'), 'col'), may hold values from -6 to 6
- lengths: int32 [16], P(('dp', 'row')), may hold values from 256 to 320
- norm_gain: float32 [2, 2, 1024], P(None, None, 'col'), may hold values from 0.5 to 1.5
- norm_bias: float32 [2, 2, 1024], P(None, None, 'col'), may hold values from -2 to 2
- in_weight: bfloat16 [2, 1024, 3, 1024], P(None, 'row', None, 'col'), may hold values from -0.1875 to 0.1875
- in_bias: float32 [2, 2, 1024], P(None, None, 'col'), may hold values from -2 to 2
- proj_weight: bfloat16 [2, 1024, 1024], P(None, 'col', 'row'), may hold values from -0.75 to 0.75
- proj_bias: float32 [2, 1024], P(None, 'col'), may hold values from -2 to 2
- up_weight: bfloat16 [2, 1024, 4096], P(None, 'row', 'col'), may hold values from -0.1875 to 0.1875
- up_bias: float32 [2, 4096], P(None, 'col'), may hold values from -2 to 2
- down_weight: bfloat16 [2, 4096, 1024], P(None, 'col', 'row'), may hold values from -0.125 to 0.125
- down_bias: float32 [2, 1024], P(None, 'col'), may hold values from -2 to 2
Outputs:
- loss_value: float32 [], replicated
- output: float32 [5120, 1024], P(('dp', 'row'), 'col')
- input_grad: float32 [5120, 1024], P(('dp', 'row'), 'col')
- norm_gain_grad: float32 [2, 2, 1024], P(None, None, 'col')
- norm_bias_grad: float32 [2, 2, 1024], P(None, None, 'col')
- in_weight_grad: float32 [2, 1024, 3, 1024], P(None, 'row', None, 'col')
- in_bias_grad: float32 [2, 2, 1024], P(None, None, 'col')
- proj_weight_grad: float32 [2, 1024, 1024], P(None, 'col', 'row')
- proj_bias_grad: float32 [2, 1024], P(None, 'col')
- up_weight_grad: float32 [2, 1024, 4096], P(None, 'row', 'col')
- up_bias_grad: float32 [2, 4096], P(None, 'col')
- down_weight_grad: float32 [2, 4096, 1024], P(None, 'col', 'row')
- down_bias_grad: float32 [2, 1024], P(None, 'col')
Inputs may be any that keep to these rules, and one draw needn't show every extreme that they name: `lengths`: number of valid slots of a sequence; slots from that number on are padding.
All inputs are finite; a program needn't handle non-finite values.
Results may differ from a plain program's by a relative error of at most 0.013.
Values may be sent and summed in bfloat16 or wider, within the bound.
No kernel may reach another device: no remote copies, remote signals or barrier semaphores. Data moves between devices by JAX's collectives and lax.ppermute only.
A program may use at most 192 MiB of HBM per device.

v0:
```python
import jax
import jax.numpy as jnp
from jax import lax
from jax.sharding import PartitionSpec as P

HEAD_DIM = 64
LAYERS = 2


epsilon = 1e-06
fill_value = -1e30


def gelu_exact(inputs):
    return jax.nn.gelu(inputs, approximate=False)


def feature_rows(partial_value):
    return lax.psum_scatter(partial_value, "col", scatter_dimension=1, tiled=True)


def gradient_rows(partial_value):
    return lax.psum_scatter(
        partial_value.astype(jnp.bfloat16), "col", scatter_dimension=1, tiled=True
    ).astype(jnp.float32)


def gather_gradient(gradient):
    return lax.all_gather(gradient, "col", axis=1, tiled=True)


def norm_shares(inputs, gains, shifts, model_width):
    totals = lax.psum((jnp.sum(inputs, axis=1), jnp.sum(inputs * inputs, axis=1)), "col")
    centre = (totals[0] / model_width)[:, None]
    rscale = lax.rsqrt((totals[1] / model_width)[:, None] - centre * centre + epsilon)
    standard = (inputs - centre) * rscale
    normed = lax.all_gather(
        (standard * gains + shifts).astype(jnp.bfloat16), "col", axis=1, tiled=True
    )
    return (normed, standard, rscale)


def norm_backward(grad_share, standard, rscale, gains, model_width):
    scaled = grad_share * gains
    sums = lax.psum((jnp.sum(scaled, axis=1), jnp.sum(scaled * standard, axis=1)), "col")
    grad_input = rscale * (
        scaled - sums[0][:, None] / model_width - standard * sums[1][:, None] / model_width
    )
    return (grad_input, jnp.sum(grad_share * standard, axis=0), jnp.sum(grad_share, axis=0))


def split_heads(flat_rows, seq_here):
    return flat_rows.reshape(
        seq_here, flat_rows.shape[0] // seq_here, flat_rows.shape[1] // HEAD_DIM, HEAD_DIM
    )


def attention_scores(queries, key_block, validity, score_scale):
    scores = (
        jnp.einsum("sqhe,skhe->shqk", queries, key_block, preferred_element_type=jnp.float32)
        * score_scale
    )
    return jnp.where(validity[:, None, None, :], scores, fill_value)


def attend(queries, key_block, values, validity, score_scale):
    scores = attention_scores(queries, key_block, validity, score_scale)
    maximum = jnp.max(scores, axis=-1, keepdims=True)
    exponent = jnp.exp(scores - maximum)
    total_mass = jnp.sum(exponent, axis=-1, keepdims=True)
    attention = (exponent / total_mass).astype(jnp.bfloat16)
    mixture = jnp.einsum("shqk,skhe->sqhe", attention, values, preferred_element_type=jnp.float32)
    return (mixture, maximum + jnp.log(total_mass))


def attend_back(queries, key_block, values, validity, score_scale, logsum, grad_mixture):
    scores = attention_scores(queries, key_block, validity, score_scale)
    chance = jnp.exp(scores - logsum)
    grad_values = jnp.einsum(
        "shqk,sqhe->skhe",
        chance.astype(jnp.bfloat16),
        grad_mixture,
        preferred_element_type=jnp.float32,
    )
    grad_chance = jnp.einsum(
        "sqhe,skhe->shqk", grad_mixture, values, preferred_element_type=jnp.float32
    )
    grad_scores = (
        chance * (grad_chance - jnp.sum(grad_chance * chance, axis=-1, keepdims=True))
    ).astype(jnp.bfloat16)
    grad_queries = (
        jnp.einsum("shqk,skhe->sqhe", grad_scores, key_block, preferred_element_type=jnp.float32)
        * score_scale
    )
    grad_keys = (
        jnp.einsum("shqk,sqhe->skhe", grad_scores, queries, preferred_element_type=jnp.float32)
        * score_scale
    )
    return (grad_queries, grad_keys, grad_values)


def body(
    states,
    teacher,
    cotangent,
    lengths,
    norm_gain,
    norm_bias,
    in_weight,
    in_bias,
    proj_weight,
    proj_bias,
    up_weight,
    up_bias,
    down_weight,
    down_bias,
):
    token_rows = states.shape[0]
    share_width = states.shape[1]
    model_width = share_width * lax.axis_size("col")
    seq_here = lengths.shape[0]
    slot_count = token_rows // seq_here
    score_scale = HEAD_DIM ** (-0.5)
    positions = jnp.arange(slot_count, dtype=jnp.int32)
    validity = positions[None, :] < lengths[:, None]
    row_mask = validity.reshape(token_rows, 1).astype(jnp.float32)
    current = states
    records = []
    for layer_index in range(LAYERS):
        fetched = (
            lax.all_gather(in_weight[layer_index], "row", axis=0, tiled=True),
            lax.all_gather(proj_weight[layer_index], "row", axis=1, tiled=True),
            lax.all_gather(up_weight[layer_index], "row", axis=0, tiled=True),
            lax.all_gather(down_weight[layer_index], "row", axis=1, tiled=True),
        )
        in_full, proj_full, up_full, down_full = fetched
        normed_one, standard_one, rscale_one = norm_shares(
            current, norm_gain[layer_index, 0], norm_bias[layer_index, 0], model_width
        )
        projected = jnp.einsum(
            "td,dpe->tpe", normed_one, in_full, preferred_element_type=jnp.float32
        )
        queries = split_heads(
            (projected[:, 0] + in_bias[layer_index, 0]).astype(jnp.bfloat16), seq_here
        )
        key_block = split_heads(projected[:, 1].astype(jnp.bfloat16), seq_here)
        values = split_heads(
            (projected[:, 2] + in_bias[layer_index, 1]).astype(jnp.bfloat16), seq_here
        )
        mixture, logsum = attend(queries, key_block, values, validity, score_scale)
        attended = mixture.reshape(token_rows, share_width).astype(jnp.bfloat16)
        attn_partial = jnp.dot(attended, proj_full, preferred_element_type=jnp.float32)
        middle = current + feature_rows(attn_partial) + proj_bias[layer_index]
        normed_two, standard_two, rscale_two = norm_shares(
            middle, norm_gain[layer_index, 1], norm_bias[layer_index, 1], model_width
        )
        hidden_pre = (
            jnp.dot(normed_two, up_full, preferred_element_type=jnp.float32) + up_bias[layer_index]
        )
        hidden = gelu_exact(hidden_pre).astype(jnp.bfloat16)
        down_partial = jnp.dot(hidden, down_full, preferred_element_type=jnp.float32)
        records.append(
            (
                fetched,
                normed_one,
                standard_one,
                rscale_one,
                queries,
                key_block,
                values,
                logsum,
                attended,
                normed_two,
                standard_two,
                rscale_two,
                hidden_pre,
                hidden,
            )
        )
        branch = feature_rows(down_partial) + down_bias[layer_index]
        current = (middle + branch) * row_mask
    residue = current - teacher.astype(jnp.float32)
    local_squared = jnp.sum(residue * residue * row_mask)
    local_count = jnp.where(lax.axis_index("col") == 0, jnp.sum(row_mask), 0.0)
    token_total, squared_total = lax.psum((local_count, local_squared), ("dp", "row", "col"))
    loss_value = squared_total / (token_total * model_width)
    factor = token_rows * lax.axis_size("dp") * lax.axis_size("row") / token_total
    grad_current = cotangent + 2.0 * factor * residue * row_mask
    results = [None] * LAYERS
    for layer_index in reversed(range(LAYERS)):
        (
            fetched,
            normed_one,
            standard_one,
            rscale_one,
            queries,
            key_block,
            values,
            logsum,
            attended,
            normed_two,
            standard_two,
            rscale_two,
            hidden_pre,
            hidden,
        ) = records[layer_index]
        in_full, proj_full, up_full, down_full = fetched
        grad_two = grad_current * row_mask
        grad_two_low = grad_two.astype(jnp.bfloat16)
        down_bias_part = jnp.sum(grad_two_low.astype(jnp.float32), axis=0)
        grad_two_rows = gather_gradient(grad_two_low)
        down_part = jnp.einsum(
            "tf,td->fd", hidden, grad_two_rows, preferred_element_type=jnp.float32
        )
        grad_hidden = jnp.einsum(
            "td,fd->tf", grad_two_rows, down_full, preferred_element_type=jnp.float32
        )
        ignored, gelu_pull = jax.vjp(gelu_exact, hidden_pre)
        grad_pre_low = gelu_pull(grad_hidden)[0].astype(jnp.bfloat16)
        up_bias_part = jnp.sum(grad_pre_low.astype(jnp.float32), axis=0)
        up_part = jnp.einsum(
            "td,tf->df", normed_two, grad_pre_low, preferred_element_type=jnp.float32
        )
        grad_normed_two = gradient_rows(
            jnp.einsum("tf,df->td", grad_pre_low, up_full, preferred_element_type=jnp.float32)
        )
        grad_norm_two, gain_part_two, shift_part_two = norm_backward(
            grad_normed_two, standard_two, rscale_two, norm_gain[layer_index, 1], model_width
        )
        grad_middle = grad_two + grad_norm_two
        grad_one_low = grad_middle.astype(jnp.bfloat16)
        proj_bias_part = jnp.sum(grad_one_low.astype(jnp.float32), axis=0)
        grad_one_rows = gather_gradient(grad_one_low)
        proj_part = jnp.einsum(
            "te,td->ed", attended, grad_one_rows, preferred_element_type=jnp.float32
        )
        grad_attended = jnp.einsum(
            "td,ed->te", grad_one_rows, proj_full, preferred_element_type=jnp.float32
        ).astype(jnp.bfloat16)
        grad_queries, grad_keys, grad_values = attend_back(
            queries,
            key_block,
            values,
            validity,
            score_scale,
            logsum,
            split_heads(grad_attended, seq_here),
        )
        grad_triple = jnp.stack(
            [
                grad_queries.reshape(token_rows, share_width),
                grad_keys.reshape(token_rows, share_width),
                grad_values.reshape(token_rows, share_width),
            ],
            axis=1,
        ).astype(jnp.bfloat16)
        in_part = jnp.einsum(
            "td,tpe->dpe", normed_one, grad_triple, preferred_element_type=jnp.float32
        )
        in_bias_part = jnp.stack(
            [
                jnp.sum(grad_triple[:, 0].astype(jnp.float32), axis=0),
                jnp.sum(grad_triple[:, 2].astype(jnp.float32), axis=0),
            ]
        )
        grad_normed_one = gradient_rows(
            jnp.einsum("tpe,dpe->td", grad_triple, in_full, preferred_element_type=jnp.float32)
        )
        grad_norm_one, gain_part_one, shift_part_one = norm_backward(
            grad_normed_one, standard_one, rscale_one, norm_gain[layer_index, 0], model_width
        )
        grad_current = grad_middle + grad_norm_one
        blocks = (
            lax.psum_scatter(
                in_part.astype(jnp.bfloat16), "row", scatter_dimension=0, tiled=True
            ).astype(jnp.float32),
            lax.psum_scatter(
                proj_part.astype(jnp.bfloat16), "row", scatter_dimension=1, tiled=True
            ).astype(jnp.float32),
            lax.psum_scatter(
                up_part.astype(jnp.bfloat16), "row", scatter_dimension=0, tiled=True
            ).astype(jnp.float32),
            lax.psum_scatter(
                down_part.astype(jnp.bfloat16), "row", scatter_dimension=1, tiled=True
            ).astype(jnp.float32),
        )
        blocks = (
            lax.psum(blocks[0].astype(jnp.bfloat16), "dp").astype(jnp.float32),
            lax.psum(blocks[1].astype(jnp.bfloat16), "dp").astype(jnp.float32),
            lax.psum(blocks[2].astype(jnp.bfloat16), "dp").astype(jnp.float32),
            lax.psum(blocks[3].astype(jnp.bfloat16), "dp").astype(jnp.float32),
        )
        vectors = lax.psum(
            (
                jnp.stack([gain_part_one, gain_part_two]),
                jnp.stack([shift_part_one, shift_part_two]),
                in_bias_part,
                proj_bias_part,
                up_bias_part,
                down_bias_part,
            ),
            ("dp", "row"),
        )
        results[layer_index] = (
            vectors[0],
            vectors[1],
            blocks[0],
            vectors[2],
            blocks[1],
            vectors[3],
            blocks[2],
            vectors[4],
            blocks[3],
            vectors[5],
        )
    stacked = [
        jnp.stack([results[layer_index][member] for layer_index in range(LAYERS)])
        for member in range(10)
    ]
    return (
        loss_value,
        current,
        grad_current,
        stacked[0],
        stacked[1],
        stacked[2],
        stacked[3],
        stacked[4],
        stacked[5],
        stacked[6],
        stacked[7],
        stacked[8],
        stacked[9],
    )


def solution(mesh):
    in_specs = (
        P(("dp", "row"), "col"),
        P(("dp", "row"), "col"),
        P(("dp", "row"), "col"),
        P(("dp", "row")),
        P(None, None, "col"),
        P(None, None, "col"),
        P(None, "row", None, "col"),
        P(None, None, "col"),
        P(None, "col", "row"),
        P(None, "col"),
        P(None, "row", "col"),
        P(None, "col"),
        P(None, "col", "row"),
        P(None, "col"),
    )
    out_specs = (
        P(),
        P(("dp", "row"), "col"),
        P(("dp", "row"), "col"),
        P(None, None, "col"),
        P(None, None, "col"),
        P(None, "row", None, "col"),
        P(None, None, "col"),
        P(None, "col", "row"),
        P(None, "col"),
        P(None, "row", "col"),
        P(None, "col"),
        P(None, "col", "row"),
        P(None, "col"),
    )
    return jax.shard_map(body, mesh=mesh, in_specs=in_specs, out_specs=out_specs, check_vma=False)
```

profile of v0, /device:TPU:1, one launch (start us, length us, event | category | flops | bytes accessed | tf_op | source)
XLA Modules:
  0.0 1358.8 jit_solution(17156937366289661022)
XLA Ops:
  11.2 10.9 all-reduce.9
  27.9 11.4 all-gather.1
  40.0 17.0 %all-gather.23.cloned.1.call-done = bf16[640,1024]{1,0:T(8,128)(2,1)} async-done(((bf16[640,256]{1,0:T(8,128)(2,1)}), bf16[640,1024]{1,0:T(8,128)(2,1)}) %all-gather.23.cloned.1.call-update) | async-done | bytes 1310736 | tf_op jit(solution)/shard_map/all_gather | solution.py:37
  57.0 33.2 %all-gather.39.cloned.1.call-done = bf16[1,1024,3,256]{3,1,2,0:T(8,128)(2,1)} async-done(((bf16[1,256,3,256]{3,1,2,0:T(8,128)(2,1)}), bf16[1,1024,3,256]{3,1,2,0:T(8,128)(2,1)}) %all-gather.39.cloned.1.call-update) | async-done | bytes 1572880 | tf_op jit(solution)/shard_map/all_gather | solution.py:131
  107.1 50.3 %reduce-scatter.17.cloned.1.call-done = f32[640,256]{1,0:T(8,128)} async-done(((f32[640,1024]{1,0:T(8,128)}), f32[640,256]{1,0:T(8,128)}) %reduce-scatter.17.cloned.1.call-update) | async-done | bytes 655376 | tf_op jit(solution)/shard_map/reduce_scatter | solution.py:19
  158.8 8.6 all-reduce.8
  171.7 23.2 %all-gather.41.cloned.1.call-done = bf16[1,1024,1024]{2,1,0:T(8,128)(2,1)} async-done(((bf16[1,256,1024]{2,1,0:T(8,128)(2,1)}), bf16[1,1024,1024]{2,1,0:T(8,128)(2,1)}) %all-gather.41.cloned.1.call-update) | async-done | bytes 2097168 | tf_op jit(solution)/shard_map/all_gather | solution.py:133
  194.9 34.2 %all-gather.25.cloned.1.call-done = bf16[640,1024]{1,0:T(8,128)(2,1)} async-done(((bf16[640,256]{1,0:T(8,128)(2,1)}), bf16[640,1024]{1,0:T(8,128)(2,1)}) %all-gather.25.cloned.1.call-update) | async-done | bytes 1310736 | tf_op jit(solution)/shard_map/all_gather | solution.py:37
  229.1 10.3 multiply_convert_fusion.3
  239.4 26.9 %all-gather.43.cloned.1.call-done = bf16[1,1024,1024]{2,1,0:T(8,128)(2,1)} async-done(((bf16[1,1024,256]{2,1,0:T(8,128)(2,1)}), bf16[1,1024,1024]{2,1,0:T(8,128)(2,1)}) %all-gather.43.cloned.1.call-update) | async-done | bytes 2097168 | tf_op jit(solution)/shard_map/all_gather | solution.py:134
  266.4 5.1 fusion.26
  273.0 50.7 %reduce-scatter.19.cloned.1.call-done = f32[640,256]{1,0:T(8,128)} async-done(((f32[640,1024]{1,0:T(8,128)}), f32[640,256]{1,0:T(8,128)}) %reduce-scatter.19.cloned.1.call-update) | async-done | bytes 655376 | tf_op jit(solution)/shard_map/reduce_scatter | solution.py:19
  325.1 8.6 all-reduce.7
  336.1 11.4 all-gather.5
  347.5 12.6 all-gather.45.cloned.1.call-done
  360.1 33.3 %all-gather.27.cloned.1.call-done = bf16[640,1024]{1,0:T(8,128)(2,1)} async-done(((bf16[640,256]{1,0:T(8,128)(2,1)}), bf16[640,1024]{1,0:T(8,128)(2,1)}) %all-gather.27.cloned.1.call-update) | async-done | bytes 1310736 | tf_op jit(solution)/shard_map/all_gather | solution.py:37
  420.3 51.1 %reduce-scatter.21.cloned.1.call-done = f32[640,256]{1,0:T(8,128)} async-done(((f32[640,1024]{1,0:T(8,128)}), f32[640,256]{1,0:T(8,128)}) %reduce-scatter.21.cloned.1.call-update) | async-done | bytes 655376 | tf_op jit(solution)/shard_map/reduce_scatter | solution.py:19
  472.8 8.6 all-reduce.6
  483.7 25.4 %all-gather.47.cloned.1.call-done = bf16[1,1024,1024]{2,1,0:T(8,128)(2,1)} async-done(((bf16[1,256,1024]{2,1,0:T(8,128)(2,1)}), bf16[1,1024,1024]{2,1,0:T(8,128)(2,1)}) %all-gather.47.cloned.1.call-update) | async-done | bytes 2097168 | tf_op jit(solution)/shard_map/all_gather | solution.py:133
  509.0 34.2 %all-gather.29.cloned.1.call-done = bf16[640,1024]{1,0:T(8,128)(2,1)} async-done(((bf16[640,256]{1,0:T(8,128)(2,1)}), bf16[640,1024]{1,0:T(8,128)(2,1)}) %all-gather.29.cloned.1.call-update) | async-done | bytes 1310736 | tf_op jit(solution)/shard_map/all_gather | solution.py:37
  543.3 10.3 multiply_convert_fusion.2
  553.5 27.1 %all-gather.49.cloned.1.call-done = bf16[1,1024,1024]{2,1,0:T(8,128)(2,1)} async-done(((bf16[1,1024,256]{2,1,0:T(8,128)(2,1)}), bf16[1,1024,1024]{2,1,0:T(8,128)(2,1)}) %all-gather.49.cloned.1.call-update) | async-done | bytes 2097168 | tf_op jit(solution)/shard_map/all_gather | solution.py:134
  587.6 50.1 %reduce-scatter.23.cloned.1.call-done = f32[640,256]{1,0:T(8,128)} async-done(((f32[640,1024]{1,0:T(8,128)}), f32[640,256]{1,0:T(8,128)}) %reduce-scatter.23.cloned.1.call-update) | async-done | bytes 655376 | tf_op jit(solution)/shard_map/reduce_scatter | solution.py:19
  640.6 39.7 %all-reduce = (f32[]{:T(128)}, f32[]{:T(128)}) all-reduce(f32[]{:T(128)} %get-tuple-element.90, f32[]{:T(128)S(6)} %select_n.15), channel_id=1, replica_groups=mesh['dp'=2,'row'=4,'col'=4] {'dp','row','col'}, use_global_device_ids=true, to_apply=%region_25.26 | all-reduce | flops 2 | bytes 16 | tf_op jit(solution)/shard_map/psum | solution.py:185
  683.3 32.9 %all-gather.31.cloned.1.call-done = bf16[640,1024]{1,0:T(8,128)(2,1)} async-done(((bf16[640,256]{1,0:T(8,128)(2,1)}), bf16[640,1024]{1,0:T(8,128)(2,1)}) %all-gather.31.cloned.1.call-update) | async-done | bytes 1310736 | tf_op jit(solution)/shard_map/all_gather | solution.py:29
  716.2 6.1 convert_reduce_fusion
  726.0 30.9 %reduce-scatter.25.cloned.1.call-done = bf16[640,256]{1,0:T(8,128)(2,1)} async-done(((bf16[640,1024]{1,0:T(8,128)(2,1)}), bf16[640,256]{1,0:T(8,128)(2,1)}) %reduce-scatter.25.cloned.1.call-update) | async-done | bytes 327696 | tf_op jit(solution)/shard_map/reduce_scatter | solution.py:23
  758.4 7.8 all-reduce.5
  769.4 32.6 %all-gather.33.cloned.1.call-done = bf16[640,1024]{1,0:T(8,128)(2,1)} async-done(((bf16[640,256]{1,0:T(8,128)(2,1)}), bf16[640,1024]{1,0:T(8,128)(2,1)}) %all-gather.33.cloned.1.call-update) | async-done | bytes 1310736 | tf_op jit(solution)/shard_map/all_gather | solution.py:29
  829.4 30.9 %reduce-scatter.27.cloned.1.call-done = bf16[640,256]{1,0:T(8,128)(2,1)} async-done(((bf16[640,1024]{1,0:T(8,128)(2,1)}), bf16[640,256]{1,0:T(8,128)(2,1)}) %reduce-scatter.27.cloned.1.call-update) | async-done | bytes 327696 | tf_op jit(solution)/shard_map/reduce_scatter | solution.py:23
  861.7 7.8 all-reduce.4
  872.2 32.6 %all-gather.35.cloned.1.call-done = bf16[640,1024]{1,0:T(8,128)(2,1)} async-done(((bf16[640,256]{1,0:T(8,128)(2,1)}), bf16[640,1024]{1,0:T(8,128)(2,1)}) %all-gather.35.cloned.1.call-update) | async-done | bytes 1310736 | tf_op jit(solution)/shard_map/all_gather | solution.py:29
  904.8 6.1 convert_reduce_fusion.1
  914.7 31.0 %reduce-scatter.29.cloned.1.call-done = bf16[640,256]{1,0:T(8,128)(2,1)} async-done(((bf16[640,1024]{1,0:T(8,128)(2,1)}), bf16[640,256]{1,0:T(8,128)(2,1)}) %reduce-scatter.29.cloned.1.call-update) | async-done | bytes 327696 | tf_op jit(solution)/shard_map/reduce_scatter | solution.py:23
  947.1 7.8 all-reduce.3
  962.3 5.0 convolution_convert_fusion.2
  973.0 5.0 convolution_convert_fusion.1
  982.9 7.2 all-gather.37.cloned.1.call-done
  1028.1 39.0 %reduce-scatter.43.cloned.1.call-done = bf16[256,1024]{1,0:T(8,128)(2,1)} async-done(((bf16[1024,1024]{1,0:T(8,128)(2,1)}), bf16[256,1024]{1,0:T(8,128)(2,1)}) %reduce-scatter.43.cloned.1.call-update) | async-done | bytes 524304 | tf_op jit(solution)/shard_map/reduce_scatter | solution.py:280
  1067.2 27.9 %reduce-scatter.39.cloned.1.call-done = bf16[256,256]{1,0:T(8,128)(2,1)} async-done(((bf16[256,1024]{1,0:T(8,128)(2,1)}), bf16[256,256]{1,0:T(8,128)(2,1)}) %reduce-scatter.39.cloned.1.call-update) | async-done | bytes 131088 | tf_op jit(solution)/shard_map/reduce_scatter | solution.py:277
  1095.1 34.9 %reduce-scatter.35.cloned.1.call-done = bf16[256,3,256]{2,0,1:T(8,128)(2,1)} async-done(((bf16[1024,3,256]{2,0,1:T(8,128)(2,1)}), bf16[256,3,256]{2,0,1:T(8,128)(2,1)}) %reduce-scatter.35.cloned.1.call-update) | async-done | bytes 393232 | tf_op jit(solution)/shard_map/reduce_scatter | solution.py:274
  1130.0 38.3 %reduce-scatter.45.cloned.1.call-done = bf16[1024,256]{1,0:T(8,128)(2,1)} async-done(((bf16[1024,1024]{1,0:T(8,128)(2,1)}), bf16[1024,256]{1,0:T(8,128)(2,1)}) %reduce-scatter.45.cloned.1.call-update) | async-done | bytes 524304 | tf_op jit(solution)/shard_map/reduce_scatter | solution.py:283
  1168.3 38.6 %reduce-scatter.41.cloned.1.call-done = bf16[256,1024]{1,0:T(8,128)(2,1)} async-done(((bf16[1024,1024]{1,0:T(8,128)(2,1)}), bf16[256,1024]{1,0:T(8,128)(2,1)}) %reduce-scatter.41.cloned.1.call-update) | async-done | bytes 524304 | tf_op jit(solution)/shard_map/reduce_scatter | solution.py:280
  1206.9 27.7 %reduce-scatter.37.cloned.1.call-done = bf16[256,256]{1,0:T(8,128)(2,1)} async-done(((bf16[256,1024]{1,0:T(8,128)(2,1)}), bf16[256,256]{1,0:T(8,128)(2,1)}) %reduce-scatter.37.cloned.1.call-update) | async-done | bytes 131088 | tf_op jit(solution)/shard_map/reduce_scatter | solution.py:277
  1234.6 34.1 %reduce-scatter.33.cloned.1.call-done = bf16[256,3,256]{2,0,1:T(8,128)(2,1)} async-done(((bf16[1024,3,256]{2,0,1:T(8,128)(2,1)}), bf16[256,3,256]{2,0,1:T(8,128)(2,1)}) %reduce-scatter.33.cloned.1.call-update) | async-done | bytes 393232 | tf_op jit(solution)/shard_map/reduce_scatter | solution.py:274
  1270.7 31.3 %reduce-scatter.31.cloned.1.call-done = bf16[640,256]{1,0:T(8,128)(2,1)} async-done(((bf16[640,1024]{1,0:T(8,128)(2,1)}), bf16[640,256]{1,0:T(8,128)(2,1)}) %reduce-scatter.31.cloned.1.call-update) | async-done | bytes 327696 | tf_op jit(solution)/shard_map/reduce_scatter | solution.py:23
  1303.4 27.4 %all-reduce.1 = (f32[1,2,256]{2,1,0:T(2,128)S(1)}, f32[1,2,256]{2,1,0:T(2,128)S(1)}, f32[1,2,256]{2,1,0:T(2,128)S(1)}, f32[1,2,256]{2,1,0:T(2,128)S(1)}, f32[1,2...) all-reduce(f32[1,2,256]{2,1,0:T(2,128)S(1)} %maximum_bitcast_fusion, ...), channel_id=1, replica_groups=mesh['dp'=2,'row'=4,'col'=4] {'dp','row'}, use_global_device_ids=true, to_apply=%region_55.56 | all-reduce | flops 6144 | bytes 49152 | tf_op jit(solution)/shard_map/psum | solution.py:293
  1330.8 7.7 all-reduce.2
  (394 shorter events, 193.9 us)
Async XLA Ops:
  7.2 49.8 %all-gather.23.cloned.1.call-start = ((), (), s32[]{:S(2)}) async-start(), calls=%async_computation.16 | async-start | bytes 1638400 | tf_op jit(solution)/shard_map/all_gather | solution.py:37
  24.3 65.9 %all-gather.39.cloned.1.call-start = ((), (), s32[]{:S(2)}) async-start(), calls=%async_computation.40 | async-start | bytes 1966080 | tf_op jit(solution)/shard_map/all_gather | solution.py:131
  26.4 131.0 %reduce-scatter.17.cloned.1.call-start = ((), (), s32[]{:S(2)}) async-start(), calls=%async_computation.17 | async-start | bytes 3276800 | tf_op jit(solution)/shard_map/reduce_scatter | solution.py:19
  27.2 71.6 %copy-start.63 = (f32[4,64]{1,0:T(4,128)}, f32[4,64]{1,0:T(4,128)S(1)}, u32[]{:S(2)}) copy-start(f32[4,64]{1,0:T(4,128)S(1)} %add.318) | copy-start | bytes 3076
  27.3 73.2 %copy-start.59 = (f32[4,64]{1,0:T(4,128)}, f32[4,64]{1,0:T(4,128)S(1)}, u32[]{:S(2)}) copy-start(f32[4,64]{1,0:T(4,128)S(1)} %add.315) | copy-start | bytes 3076
  105.4 89.5 %all-gather.41.cloned.1.call-start = ((), (), s32[]{:S(2)}) async-start(), calls=%async_computation.41 | async-start | bytes 2621440 | tf_op jit(solution)/shard_map/all_gather | solution.py:133
  106.5 122.6 %all-gather.25.cloned.1.call-start = ((), (), s32[]{:S(2)}) async-start(), calls=%async_computation.18 | async-start | bytes 1638400 | tf_op jit(solution)/shard_map/all_gather | solution.py:37
  167.5 71.9 %copy-start.47 = (f32[640]{0:T(1024)}, f32[640]{0:T(1024)S(1)}, u32[]{:S(2)}) copy-start(f32[640]{0:T(1024)S(1)} %get-tuple-element.125) | copy-start | bytes 7684
  167.5 71.9 %copy-start.49 = (f32[640]{0:T(1024)}, f32[640]{0:T(1024)S(1)}, u32[]{:S(2)}) copy-start(f32[640]{0:T(1024)S(1)} %get-tuple-element.126) | copy-start | bytes 7684
  168.5 97.8 %all-gather.43.cloned.1.call-start = ((), (), s32[]{:S(2)}) async-start(), calls=%async_computation.42 | async-start | bytes 2621440 | tf_op jit(solution)/shard_map/all_gather | solution.py:134
  170.8 152.8 %reduce-scatter.19.cloned.1.call-start = ((), (), s32[]{:S(2)}) async-start(), calls=%async_computation.19 | async-start | bytes 3276800 | tf_op jit(solution)/shard_map/reduce_scatter | solution.py:19
  171.7 67.7 %copy-start.79 = (f32[1,1024]{1,0:T(1,128)}, f32[1,1024]{1,0:T(1,128)S(1)}, u32[]{:S(2)}) copy-start(f32[1,1024]{1,0:T(1,128)S(1)} %get-tuple-element.112) | copy-start | bytes 12292
  271.4 64.0 %copy-start.82 = (f32[256]{0:T(256)S(1)}, f32[256]{0:T(256)}, u32[]{:S(2)}) copy-start(f32[256]{0:T(256)} %get-tuple-element.40) | copy-start | bytes 3076
  271.4 64.7 %copy-start.32 = (bf16[1,256,256]{2,1,0:T(8,128)(2,1)S(1)}, bf16[1,256,256]{2,1,0:T(8,128)(2,1)}, u32[]{:S(2)}) copy-start(bf16[1,256,256]{2,1,0:T(8,128)(2,1)} %get-tuple-element.109) | copy-start | bytes 393220
  271.5 88.6 %all-gather.45.cloned.1.call-start = ((), (), s32[]{:S(2)}) async-start(), calls=%async_computation.43 | async-start | bytes 1966080 | tf_op jit(solution)/shard_map/all_gather | solution.py:131
  272.2 121.1 %all-gather.27.cloned.1.call-start = ((), (), s32[]{:S(2)}) async-start(), calls=%async_computation.20 | async-start | bytes 1638400 | tf_op jit(solution)/shard_map/all_gather | solution.py:37
  334.7 136.7 %reduce-scatter.21.cloned.1.call-start = ((), (), s32[]{:S(2)}) async-start(), calls=%async_computation.21 | async-start | bytes 3276800 | tf_op jit(solution)/shard_map/reduce_scatter | solution.py:19
  419.5 123.7 %copy-start.81 = (f32[1,1024]{1,0:T(1,128)S(1)}, f32[1,1024]{1,0:T(1,128)}, u32[]{:S(2)}) copy-start(f32[1,1024]{1,0:T(1,128)} %get-tuple-element.111) | copy-start | bytes 12292
  419.6 89.5 %all-gather.47.cloned.1.call-start = ((), (), s32[]{:S(2)}) async-start(), calls=%async_computation.44 | async-start | bytes 2621440 | tf_op jit(solution)/shard_map/all_gather | solution.py:133
  420.3 123.0 %all-gather.29.cloned.1.call-start = ((), (), s32[]{:S(2)}) async-start(), calls=%async_computation.22 | async-start | bytes 1638400 | tf_op jit(solution)/shard_map/all_gather | solution.py:37
  482.4 98.2 %all-gather.49.cloned.1.call-start = ((), (), s32[]{:S(2)}) async-start(), calls=%async_computation.45 | async-start | bytes 2621440 | tf_op jit(solution)/shard_map/all_gather | solution.py:134
  483.2 154.6 %reduce-scatter.23.cloned.1.call-start = ((), (), s32[]{:S(2)}) async-start(), calls=%async_computation.23 | async-start | bytes 3276800 | tf_op jit(solution)/shard_map/reduce_scatter | solution.py:19
  585.6 130.6 %all-gather.31.cloned.1.call-start = ((), (), s32[]{:S(2)}) async-start(), calls=%async_computation.24 | async-start | bytes 1638400 | tf_op jit(solution)/shard_map/all_gather | solution.py:29
  683.3 73.7 %reduce-scatter.25.cloned.1.call-start = ((), (), s32[]{:S(2)}) async-start(), calls=%async_computation.25 | async-start | bytes 1638400 | tf_op jit(solution)/shard_map/reduce_scatter | solution.py:23
  726.0 76.0 %all-gather.33.cloned.1.call-start = ((), (), s32[]{:S(2)}) async-start(), calls=%async_computation.26 | async-start | bytes 1638400 | tf_op jit(solution)/shard_map/all_gather | solution.py:29
  769.1 91.2 %reduce-scatter.27.cloned.1.call-start = ((), (), s32[]{:S(2)}) async-start(), calls=%async_computation.27 | async-start | bytes 1638400 | tf_op jit(solution)/shard_map/reduce_scatter | solution.py:23
  829.3 75.6 %copy-start.80 = (f32[1,1024]{1,0:T(1,128)S(1)}, f32[1,1024]{1,0:T(1,128)}, u32[]{:S(2)}) copy-start(f32[1,1024]{1,0:T(1,128)} %copy-done.79) | copy-start | bytes 12292
  829.3 75.5 %all-gather.35.cloned.1.call-start = ((), (), s32[]{:S(2)}) async-start(), calls=%async_computation.28 | async-start | bytes 1638400 | tf_op jit(solution)/shard_map/all_gather | solution.py:29
  872.0 73.7 %reduce-scatter.29.cloned.1.call-start = ((), (), s32[]{:S(2)}) async-start(), calls=%async_computation.29 | async-start | bytes 1638400 | tf_op jit(solution)/shard_map/reduce_scatter | solution.py:23
  914.7 75.5 %all-gather.37.cloned.1.call-start = ((), (), s32[]{:S(2)}) async-start(), calls=%async_computation.30 | async-start | bytes 1638400 | tf_op jit(solution)/shard_map/all_gather | solution.py:29
  957.3 70.8 %reduce-scatter.47.cloned.1.call-start = ((), (), s32[]{:S(2)}) async-start(), calls=%async_computation.39 | async-start | bytes 2621440 | tf_op jit(solution)/shard_map/reduce_scatter | solution.py:283
  962.3 104.9 %reduce-scatter.43.cloned.1.call-start = ((), (), s32[]{:S(2)}) async-start(), calls=%async_computation.37 | async-start | bytes 2621440 | tf_op jit(solution)/shard_map/reduce_scatter | solution.py:280
  967.3 127.8 %reduce-scatter.39.cloned.1.call-start = ((), (), s32[]{:S(2)}) async-start(), calls=%async_computation.35 | async-start | bytes 655360 | tf_op jit(solution)/shard_map/reduce_scatter | solution.py:277
  968.8 161.2 %reduce-scatter.35.cloned.1.call-start = ((), (), s32[]{:S(2)}) async-start(), calls=%async_computation.33 | async-start | bytes 1966080 | tf_op jit(solution)/shard_map/reduce_scatter | solution.py:274
  972.9 195.4 %reduce-scatter.45.cloned.1.call-start = ((), (), s32[]{:S(2)}) async-start(), calls=%async_computation.38 | async-start | bytes 2621440 | tf_op jit(solution)/shard_map/reduce_scatter | solution.py:283
  978.0 228.8 %reduce-scatter.41.cloned.1.call-start = ((), (), s32[]{:S(2)}) async-start(), calls=%async_computation.36 | async-start | bytes 2621440 | tf_op jit(solution)/shard_map/reduce_scatter | solution.py:280
  982.9 251.8 %reduce-scatter.37.cloned.1.call-start = ((), (), s32[]{:S(2)}) async-start(), calls=%async_computation.34 | async-start | bytes 655360 | tf_op jit(solution)/shard_map/reduce_scatter | solution.py:277
  997.5 271.2 %reduce-scatter.33.cloned.1.call-start = ((), (), s32[]{:S(2)}) async-start(), calls=%async_computation.32 | async-start | bytes 1966080 | tf_op jit(solution)/shard_map/reduce_scatter | solution.py:274
  1022.2 279.7 %reduce-scatter.31.cloned.1.call-start = ((), (), s32[]{:S(2)}) async-start(), calls=%async_computation.31 | async-start | bytes 1638400 | tf_op jit(solution)/shard_map/reduce_scatter | solution.py:23
  1024.6 245.5 %copy-start.16 = (bf16[640,1,256]{0,2,1:T(8,128)(2,1)S(1)}, bf16[640,1,256]{0,2,1:T(8,128)(2,1)}, u32[]{:S(2)}) copy-start(bf16[640,1,256]{0,2,1:T(8,128)(2,1)} %copy-done.15) | copy-start | bytes 983044
  1024.6 245.7 %copy-start.18 = (bf16[640,1,256]{0,2,1:T(8,128)(2,1)S(1)}, bf16[640,1,256]{0,2,1:T(8,128)(2,1)}, u32[]{:S(2)}) copy-start(bf16[640,1,256]{0,2,1:T(8,128)(2,1)} %copy-done.17) | copy-start | bytes 983044
  1024.6 245.8 %copy-start.19 = (bf16[640,1,256]{0,2,1:T(8,128)(2,1)S(1)}, bf16[640,1,256]{0,2,1:T(8,128)(2,1)}, u32[]{:S(2)}) copy-start(bf16[640,1,256]{0,2,1:T(8,128)(2,1)} %stack_reshape.29) | copy-start | bytes 983044
  1024.6 246.0 %copy-start.20 = (bf16[640,1,256]{0,2,1:T(8,128)(2,1)S(1)}, bf16[640,1,256]{0,2,1:T(8,128)(2,1)}, u32[]{:S(2)}) copy-start(bf16[640,1,256]{0,2,1:T(8,128)(2,1)} %stack_reshape.27) | copy-start | bytes 983044
  1024.6 277.4 %copy-start.44 = (f32[640]{0:T(1024)S(1)}, f32[640]{0:T(1024)}, u32[]{:S(2)}) copy-start(f32[640]{0:T(1024)} %copy-done.43) | copy-start | bytes 7684
  1024.6 277.3 %copy-start.46 = (f32[640]{0:T(1024)S(1)}, f32[640]{0:T(1024)}, u32[]{:S(2)}) copy-start(f32[640]{0:T(1024)} %copy-done.45) | copy-start | bytes 7684
  1024.6 277.3 %copy-start.67 = (f32[1,1,256]{2,1,0:T(1,128)S(1)}, f32[1,1,256]{2,1,0:T(1,128)}, u32[]{:S(2)}) copy-start(f32[1,1,256]{2,1,0:T(1,128)} %copy-done.66) | copy-start | bytes 3076
  1024.6 318.5 %all-reduce.13.cloned.1.call-start = ((), (), s32[]{:S(2)}) async-start(), calls=%async_computation.46 | async-start | bytes 6291456 | tf_op jit(solution)/shard_map/psum | solution.py:288
  1268.7 72.2 %copy-start.25 = (f32[640,256]{1,0:T(8,128)S(1)}, f32[640,256]{1,0:T(8,128)}, u32[]{:S(2)}) copy-start(f32[640,256]{1,0:T(8,128)} %get-tuple-element.86) | copy-start | bytes 1966084
  (80 other events, 1461.4 us)
Sparse Core Ops, SparseCore 0:
  24.4 32.5 all-gather.22
  59.4 30.7 all-gather.38
  105.5 51.9 reduce-scatter.16
  159.7 35.1 all-gather.40
  196.9 32.1 all-gather.24
  231.4 34.9 all-gather.42
  271.6 51.9 reduce-scatter.18
  326.1 34.0 all-gather.44
  362.2 31.0 all-gather.26
  419.7 51.7 reduce-scatter.20
  473.9 35.1 all-gather.46
  511.0 32.1 all-gather.28
  545.7 34.9 all-gather.48
  585.7 51.9 reduce-scatter.22
  683.4 32.7 all-gather.30
  726.1 30.8 reduce-scatter.24
  769.2 32.6 all-gather.32
  829.4 30.8 reduce-scatter.26
  872.1 32.6 all-gather.34
  914.8 30.8 reduce-scatter.28
  957.4 32.6 all-gather.36
  993.1 34.9 reduce-scatter.46
  1031.9 35.1 reduce-scatter.42
  1070.4 24.6 reduce-scatter.38
  1098.9 31.0 reduce-scatter.34
  1133.1 35.1 reduce-scatter.44
  1171.7 35.1 reduce-scatter.40
  1209.9 24.6 reduce-scatter.36
  1237.6 31.0 reduce-scatter.32
  1270.8 31.0 reduce-scatter.30
  1304.8 22.9 all-reduce.12
where the time goes:
time: 1370 us; the launch traced here: 1360 us
  waiting for transfers between devices  945 us (69%)
  blocking collectives  158 us (12%)
  matrix products  120 us (9%)
  local copies, waits for them, and re-layouts  67.4 us (5%)
  other arithmetic  45.5 us (3%)
  between operations  20.2 us (1%)
    reduce_scatter x4, waiting for transfers between devices, feature_rows(): lax.psum_scatter(partial_value, 'col', scatter_dimension=1, tiled=True)  202 us
    reduce_scatter x4, waiting for transfers between devices, gradient_rows(): lax.psum_scatter(partial_value.astype(jnp.bfloat16), 'col', scatter_dimen...  124 us
    all_gather x4, waiting for transfers between devices, norm_shares(): lax.all_gather((standard * gains + shifts).astype(jnp.bfloat16), 'col', a...  119 us
    all_gather x4, waiting for transfers between devices, gather_gradient(): return lax.all_gather(gradient, 'col', axis=1, tiled=True)  105 us
    reduce_scatter x2, waiting for transfers between devices, body(): lax.psum_scatter(up_part.astype(jnp.bfloat16), 'row', scatter_dimension=0...  77.6 us
    reduce_scatter x2, waiting for transfers between devices, body(): lax.psum_scatter(in_part.astype(jnp.bfloat16), 'row', scatter_dimension=0...  69 us
    reduce_scatter x2, waiting for transfers between devices, body(): lax.psum_scatter(proj_part.astype(jnp.bfloat16), 'row', scatter_dimension...  55.7 us
    all_gather x2, waiting for transfers between devices, body(): lax.all_gather(down_weight[layer_index], 'row', axis=1, tiled=True)  54 us
  transfers between devices with their start and end apart: 31, of which 30 were waited for; matrix products, arithmetic and copies ran while one was open for 8% of the time, Pallas kernels for 0%

commit v1 on v0

v1 whole, which is shorter than its diff:
```python
import jax
import jax.numpy as jnp
from jax import lax
from jax.sharding import PartitionSpec as P

HEAD_DIM = 64
LAYERS = 2

epsilon = 1e-06
fill_value = -1e30
low_type = jnp.bfloat16


def gelu_exact(inputs):
    return jax.nn.gelu(inputs, approximate=False)


def flip_col(value):
    count = lax.axis_size("col")
    return lax.ppermute(value, "col", [(i, count - 1 - i) for i in range(count)])


def swap_core(value):
    count = lax.axis_size("dp")
    return lax.ppermute(value, "dp", [(i, count - 1 - i) for i in range(count)])


def group_shift(value, step):
    count = lax.axis_size("col")
    half = count // 2
    pairs = [(i, i // half * half + (i % half + step) % half) for i in range(count)]
    return lax.ppermute(value, "col", pairs)


def group_sum(partial_value):
    low = partial_value.astype(low_type)
    total = partial_value
    for step in range(1, lax.axis_size("col") // 2):
        total = total + group_shift(low, step).astype(jnp.float32)
    return total


def butterfly_sum(value, axes):
    for axis in axes:
        count = lax.axis_size(axis)
        step = 1
        while step < count:
            value = value + lax.ppermute(value, axis, [(i, i ^ step) for i in range(count)])
            step *= 2
    return value


def gather_row_direct(shard):
    count = lax.axis_size("row")
    if count > 4:
        return lax.all_gather(shard, "row", axis=0, tiled=False)
    mine = lax.axis_index("row")
    whole = jnp.zeros((count,) + shard.shape, shard.dtype)
    whole = lax.dynamic_update_index_in_dim(whole, shard, mine, 0)
    for step in range(1, count):
        piece = lax.ppermute(shard, "row", [(i, i ^ step) for i in range(count)])
        whole = lax.dynamic_update_index_in_dim(whole, piece, mine ^ step, 0)
    return whole


def gather_row(shard):
    return lax.all_gather(shard, "row", axis=0, tiled=False)


def scatter_row(blocks):
    return lax.psum_scatter(blocks, "row", scatter_dimension=0, tiled=False)


def place_blocks(pair, mine_first):
    count = lax.axis_size("col")
    half = count // 2
    col_index = lax.axis_index("col")
    base = col_index // half * half
    whole = jnp.zeros((count,) + pair.shape[1:], pair.dtype)
    for step in range(half):
        piece = pair if step == 0 else group_shift(pair, step)
        source = base + (col_index - base + half - step) % half
        whole = lax.dynamic_update_index_in_dim(whole, piece[0], source, 0)
        whole = lax.dynamic_update_index_in_dim(whole, piece[1], count - 1 - source, 0)
    return whole


def norm_rows(inputs, gains, shifts, model_width):
    centre = jnp.sum(inputs, axis=1, keepdims=True) / model_width
    centred = inputs - centre
    spread = jnp.sum(centred * centred, axis=1, keepdims=True) / model_width
    rscale = lax.rsqrt(spread + epsilon)
    standard = centred * rscale
    return ((standard * gains + shifts).astype(low_type), standard, rscale)


def norm_backward(grad_rows, standard, rscale, gains, model_width):
    scaled = grad_rows * gains
    first = jnp.sum(scaled, axis=1, keepdims=True) / model_width
    second = jnp.sum(scaled * standard, axis=1, keepdims=True) / model_width
    grad_input = rscale * (scaled - first - standard * second)
    return (grad_input, jnp.sum(grad_rows * standard, axis=0), jnp.sum(grad_rows, axis=0))


def dot(left, right, spec):
    return jnp.einsum(spec, left, right, preferred_element_type=jnp.float32)


def split_heads(flat_rows, seqs):
    return flat_rows.reshape(
        seqs, flat_rows.shape[0] // seqs, flat_rows.shape[1] // HEAD_DIM, HEAD_DIM
    )


def attention_scores(queries, key_block, validity, score_scale):
    scores = dot(queries, key_block, "sqhe,skhe->shqk") * score_scale
    return jnp.where(validity[:, None, None, :], scores, fill_value)


def attend(queries, key_block, values, validity, score_scale):
    scores = attention_scores(queries, key_block, validity, score_scale)
    maximum = jnp.max(scores, axis=-1, keepdims=True)
    exponent = jnp.exp(scores - maximum)
    total_mass = jnp.sum(exponent, axis=-1, keepdims=True)
    attention = (exponent / total_mass).astype(low_type)
    mixture = dot(attention, values, "shqk,skhe->sqhe")
    return (mixture, maximum + jnp.log(total_mass))


def attend_back(queries, key_block, values, validity, score_scale, logsum, grad_mixture):
    scores = attention_scores(queries, key_block, validity, score_scale)
    chance = jnp.exp(scores - logsum)
    grad_values = dot(chance.astype(low_type), grad_mixture, "shqk,sqhe->skhe")
    grad_chance = dot(grad_mixture, values, "sqhe,skhe->shqk")
    grad_scores = (
        chance * (grad_chance - jnp.sum(grad_chance * chance, axis=-1, keepdims=True))
    ).astype(low_type)
    grad_queries = dot(grad_scores, key_block, "shqk,skhe->sqhe") * score_scale
    grad_keys = dot(grad_scores, queries, "shqk,sqhe->skhe") * score_scale
    return (grad_queries, grad_keys, grad_values)


def body(
    states,
    teacher,
    cotangent,
    lengths,
    norm_gain,
    norm_bias,
    in_weight,
    in_bias,
    proj_weight,
    proj_bias,
    up_weight,
    up_bias,
    down_weight,
    down_bias,
):
    col_count = lax.axis_size("col")
    row_count = lax.axis_size("row")
    core_count = lax.axis_size("dp")
    half_group = col_count // 2
    col_index = lax.axis_index("col")
    core_index = lax.axis_index("dp")
    group_index = col_index // half_group
    first_core = core_index == 0
    token_rows, width = states.shape
    model_width = width * col_count
    seqs = lengths.shape[0] // 2
    rows = token_rows // 2
    slot_count = rows // seqs
    hidden_width = up_bias.shape[1]
    score_scale = HEAD_DIM ** (-0.5)

    weight_pairs = [
        (d * col_count + i, d * col_count + (i if d == 0 else col_count - 1 - i))
        for d in range(core_count)
        for i in range(col_count)
    ]

    def fetch(shard, gather):
        moved = lax.ppermute(shard, ("dp", "col"), weight_pairs)
        whole = gather(moved)
        return (whole, swap_core(whole))

    in_full = [None] * LAYERS
    proj_full = [None] * LAYERS
    up_full = [None] * LAYERS
    down_full = [None] * LAYERS
    for layer in range(LAYERS):
        in_full[layer] = fetch(in_weight[layer], gather_row_direct)
        proj_full[layer] = fetch(proj_weight[layer], gather_row_direct)
        up_full[layer] = fetch(up_weight[layer], gather_row)
        down_full[layer] = fetch(down_weight[layer], gather_row)

    feature_pack = jnp.concatenate(
        [norm_gain.reshape(-1, width), norm_bias.reshape(-1, width), proj_bias, down_bias]
    )
    hidden_pack = jnp.concatenate([in_bias.reshape(-1, width), up_bias.reshape(-1, width)])
    feature_rows = feature_pack.shape[0]
    small = jnp.concatenate([feature_pack, hidden_pack])
    small_pair = jnp.stack([small, flip_col(small)])
    feature_all = place_blocks(small_pair[:, :feature_rows], True)
    feature_all = jnp.transpose(feature_all, (1, 0, 2)).reshape(feature_rows, model_width)
    gains = feature_all[: 2 * LAYERS].reshape(LAYERS, 2, model_width)
    shifts = feature_all[2 * LAYERS : 4 * LAYERS].reshape(LAYERS, 2, model_width)
    proj_shift = feature_all[4 * LAYERS : 5 * LAYERS]
    down_shift = feature_all[5 * LAYERS :]
    hidden_pair = small_pair[:, feature_rows:]
    hidden_pair = jnp.where(first_core, hidden_pair, hidden_pair[::-1])
    in_shift = hidden_pair[:, : 2 * LAYERS].reshape(2, LAYERS, 2, width)
    up_shift = hidden_pair[:, 2 * LAYERS :].reshape(2, LAYERS, hidden_width)

    def own_half(value):
        return lax.dynamic_slice_in_dim(value, group_index * rows, rows, 0)

    def other_half(value):
        return lax.dynamic_slice_in_dim(value, (1 - group_index) * rows, rows, 0)

    def whole_rows(value):
        pair = jnp.stack([own_half(value), flip_col(other_half(value))])
        blocks = place_blocks(pair, True)
        return jnp.transpose(blocks, (1, 0, 2)).reshape(rows, model_width)

    def share_rows(value):
        own = lax.dynamic_slice_in_dim(value, col_index * width, width, 1)
        other = lax.dynamic_slice_in_dim(value, (col_count - 1 - col_index) * width, width, 1)
        received = flip_col(other)
        lower = jnp.where(group_index == 0, own, received)
        upper = jnp.where(group_index == 0, received, own)
        return jnp.concatenate([lower, upper])

    current = whole_rows(states)
    token_total = butterfly_sum(jnp.sum(lengths), ("dp", "row")).astype(jnp.float32)
    factor = token_rows * core_count * row_count / token_total

    positions = jnp.arange(slot_count, dtype=jnp.int32)
    all_validity = positions[None, :] < lengths[:, None]
    all_mask = all_validity.reshape(token_rows, 1).astype(jnp.float32)
    own_lengths = lax.dynamic_slice_in_dim(lengths, group_index * seqs, seqs, 0)
    validity = positions[None, :] < own_lengths[:, None]
    row_mask = validity.reshape(rows, 1).astype(jnp.float32)

    teacher_wide = teacher.astype(jnp.float32)
    seed_share = cotangent - 2.0 * factor * all_mask * teacher_wide
    seeds = whole_rows(seed_share)

    records = []
    for layer in range(LAYERS):
        normed_one, standard_one, rscale_one = norm_rows(
            current, gains[layer, 0], shifts[layer, 0], model_width
        )
        queries, key_block, values = [], [], []
        for side in range(2):
            weight = in_full[layer][side].reshape(model_width, 3, width)
            projected = dot(normed_one, weight, "td,dpe->tpe")
            queries.append((projected[:, 0] + in_shift[side, layer, 0]).astype(low_type))
            key_block.append(projected[:, 1].astype(low_type))
            values.append((projected[:, 2] + in_shift[side, layer, 1]).astype(low_type))
        queries = split_heads(jnp.concatenate(queries, 1), seqs)
        key_block = split_heads(jnp.concatenate(key_block, 1), seqs)
        values = split_heads(jnp.concatenate(values, 1), seqs)
        mixture, logsum = attend(queries, key_block, values, validity, score_scale)
        attended = mixture.reshape(rows, 2 * width).astype(low_type)
        attn_partial = 0.0
        for side in range(2):
            attn_partial = attn_partial + dot(
                attended[:, side * width : (side + 1) * width],
                proj_full[layer][side],
                "te,red->trd",
            ).reshape(rows, model_width)
        middle = current + group_sum(attn_partial) + proj_shift[layer]
        normed_two, standard_two, rscale_two = norm_rows(
            middle, gains[layer, 1], shifts[layer, 1], model_width
        )
        hidden_pre, hidden = [], []
        down_partial = 0.0
        for side in range(2):
            weight = up_full[layer][side].reshape(model_width, hidden_width)
            pre = dot(normed_two, weight, "td,df->tf") + up_shift[side, layer]
            hid = gelu_exact(pre).astype(low_type)
            hidden_pre.append(pre)
            hidden.append(hid)
            down_partial = down_partial + dot(
                hid, down_full[layer][side], "tf,rfd->trd"
            ).reshape(rows, model_width)
        records.append(
            (
                normed_one,
                standard_one,
                rscale_one,
                queries,
                key_block,
                values,
                logsum,
                attended,
                normed_two,
                standard_two,
                rscale_two,
                hidden_pre,
                hidden,
            )
        )
        current = (middle + group_sum(down_partial) + down_shift[layer]) * row_mask

    output_share = share_rows(current)
    residue = (output_share - teacher_wide) * all_mask
    squared = jnp.sum(residue * residue)
    grad_current = seeds + 2.0 * factor * current * row_mask

    in_blocks, proj_blocks, up_blocks, down_blocks = [], [], [], []
    feature_grads = {}
    hidden_grads = {}

    def send_back(pair):
        low = [piece.astype(low_type) for piece in pair]
        both = (low[0].astype(jnp.float32) + swap_core(low[1]).astype(jnp.float32)).astype(low_type)
        return scatter_row(both)

    def finish(block):
        pairs = [(col_count + i, col_count - 1 - i) for i in range(col_count)]
        arrived = lax.ppermute(block, ("dp", "col"), pairs)
        total = (block.astype(jnp.float32) + arrived.astype(jnp.float32)).astype(low_type)
        copied = lax.ppermute(total, "dp", [(0, 1)])
        return jnp.where(first_core, total, copied).astype(jnp.float32)

    def row_blocks(value):
        return value.reshape((row_count, value.shape[0] // row_count) + value.shape[1:])

    for layer in reversed(range(LAYERS)):
        (
            normed_one,
            standard_one,
            rscale_one,
            queries,
            key_block,
            values,
            logsum,
            attended,
            normed_two,
            standard_two,
            rscale_two,
            hidden_pre,
            hidden,
        ) = records[layer]
        grad_two = grad_current * row_mask
        grad_two_low = grad_two.astype(low_type)
        down_bias_part = jnp.sum(grad_two_low.astype(jnp.float32), axis=0)
        grad_two_blocks = grad_two_low.reshape(rows, row_count, model_width // row_count)
        grad_pre, up_bias_part, down_pair, up_pair = [], [], [], []
        normed_two_grad = 0.0
        for side in range(2):
            grad_hidden = dot(grad_two_blocks, down_full[layer][side], "trd,rfd->tf")
            ignored, gelu_pull = jax.vjp(gelu_exact, hidden_pre[side])
            pre_low = gelu_pull(grad_hidden)[0].astype(low_type)
            grad_pre.append(pre_low)
            up_bias_part.append(jnp.sum(pre_low.astype(jnp.float32), axis=0))
            weight = up_full[layer][side].reshape(model_width, hidden_width)
            normed_two_grad = normed_two_grad + dot(pre_low, weight, "tf,df->td")
        normed_two_grad = group_sum(normed_two_grad)
        for side in range(2):
            down_pair.append(dot(hidden[side], grad_two_blocks, "tf,trd->rfd"))
            up_pair.append(row_blocks(dot(normed_two, grad_pre[side], "td,tf->df")))
        down_blocks.append(send_back(down_pair))
        up_blocks.append(send_back(up_pair))
        grad_norm_two, gain_part_two, shift_part_two = norm_backward(
            normed_two_grad, standard_two, rscale_two, gains[layer, 1], model_width
        )
        grad_middle = grad_two + grad_norm_two
        grad_one_low = grad_middle.astype(low_type)
        proj_bias_part = jnp.sum(grad_one_low.astype(jnp.float32), axis=0)
        grad_one_blocks = grad_one_low.reshape(rows, row_count, model_width // row_count)
        grad_attended, proj_pair = [], []
        for side in range(2):
            grad_attended.append(
                dot(grad_one_blocks, proj_full[layer][side], "trd,red->te").astype(low_type)
            )
            proj_pair.append(
                dot(attended[:, side * width : (side + 1) * width], grad_one_blocks, "te,trd->red")
            )
        proj_blocks.append(send_back(proj_pair))
        grad_queries, grad_keys, grad_values = attend_back(
            queries,
            key_block,
            values,
            validity,
            score_scale,
            logsum,
            split_heads(jnp.concatenate(grad_attended, 1), seqs),
        )
        grad_triple = jnp.stack(
            [
                grad_queries.reshape(rows, 2, width),
                grad_keys.reshape(rows, 2, width),
                grad_values.reshape(rows, 2, width),
            ],
            axis=2,
        ).astype(low_type)
        in_bias_part = jnp.sum(grad_triple.astype(jnp.float32), axis=0)[:, ::2]
        in_pair = []
        normed_one_grad = 0.0
        for side in range(2):
            weight = in_full[layer][side].reshape(model_width, 3, width)
            normed_one_grad = normed_one_grad + dot(grad_triple[:, side], weight, "tpe,dpe->td")
        normed_one_grad = group_sum(normed_one_grad)
        for side in range(2):
            in_pair.append(row_blocks(dot(normed_one, grad_triple[:, side], "td,tpe->dpe")))
        in_blocks.append(send_back(in_pair))
        grad_norm_one, gain_part_one, shift_part_one = norm_backward(
            normed_one_grad, standard_one, rscale_one, gains[layer, 0], model_width
        )
        grad_current = grad_middle + grad_norm_one
        feature_grads[layer] = (
            gain_part_one,
            gain_part_two,
            shift_part_one,
            shift_part_two,
            proj_bias_part,
            down_bias_part,
        )
        hidden_grads[layer] = jnp.concatenate(
            [in_bias_part, jnp.stack(up_bias_part).reshape(2, -1, width)], axis=1
        )

    input_share = share_rows(grad_current)

    def together(blocks):
        return jnp.stack([finish(block) for block in blocks[::-1]])

    in_grad = together(in_blocks)
    proj_grad = together(proj_blocks)
    up_grad = together(up_blocks)
    down_grad = together(down_blocks)

    feature_parts = jnp.stack([part for layer in range(LAYERS) for part in feature_grads[layer]])
    feature_parts = feature_parts.reshape(-1, col_count, width)
    own_parts = lax.dynamic_index_in_dim(feature_parts, col_index, 1, False)
    other_parts = lax.dynamic_index_in_dim(feature_parts, col_count - 1 - col_index, 1, False)
    hidden_parts = jnp.concatenate([hidden_grads[layer] for layer in range(LAYERS)], axis=1)
    hidden_parts = jnp.where(first_core, hidden_parts, hidden_parts[::-1])
    extra = jnp.zeros((1, width), jnp.float32).at[0, 0].set(squared)
    packed = jnp.concatenate(
        [jnp.stack([own_parts, other_parts]), hidden_parts, jnp.stack([extra, extra])], axis=1
    )
    packed = butterfly_sum(packed, ("dp", "row"))
    vectors = packed[0] + flip_col(packed[1])
    squared_total = packed[0, -1, 0]
    squared_total = butterfly_sum(squared_total, ("col",))
    loss_value = squared_total / (token_total * model_width)
    per_layer = len(feature_grads[0])
    features = vectors[: LAYERS * per_layer].reshape(LAYERS, per_layer, width)
    hiddens = vectors[LAYERS * per_layer : -1].reshape(LAYERS, -1, width)
    return (
        loss_value,
        output_share,
        input_share,
        features[:, 0:2],
        features[:, 2:4],
        in_grad,
        hiddens[:, 0:2],
        proj_grad,
        features[:, 4],
        up_grad,
        hiddens[:, 2:].reshape(LAYERS, hidden_width),
        down_grad,
        features[:, 5],
    )


def solution(mesh):
    in_specs = (
        P(("dp", "row"), "col"),
        P(("dp", "row"), "col"),
        P(("dp", "row"), "col"),
        P(("dp", "row")),
        P(None, None, "col"),
        P(None, None, "col"),
        P(None, "row", None, "col"),
        P(None, None, "col"),
        P(None, "col", "row"),
        P(None, "col"),
        P(None, "row", "col"),
        P(None, "col"),
        P(None, "col", "row"),
        P(None, "col"),
    )
    out_specs = (
        P(),
        P(("dp", "row"), "col"),
        P(("dp", "row"), "col"),
        P(None, None, "col"),
        P(None, None, "col"),
        P(None, "row", None, "col"),
        P(None, None, "col"),
        P(None, "col", "row"),
        P(None, "col"),
        P(None, "row", "col"),
        P(None, "col"),
        P(None, "col", "row"),
        P(None, "col"),
    )
    return jax.shard_map(body, mesh=mesh, in_specs=in_specs, out_specs=out_specs, check_vma=False)
```

time: 1370 us -> 720 us (0.53)
  waiting for transfers between devices: 945 us -> 250 us
  blocking collectives: 158 us -> 0 us
  starting transfers between devices: 2.89 us -> 148 us
  local copies, waits for them, and re-layouts: 67.4 us -> 109 us
  other arithmetic: 45.5 us -> 73.3 us
  matrix products: 120 us -> 104 us
    reduce_scatter x16 -> x0, waiting for transfers between devices: 570 us -> none  [the longest x4 202 us: feature_rows(): lax.psum_scatter(partial_value, 'col', scatter_dimension=1, tiled=True)]
    all_gather x14 -> x4, waiting for transfers between devices: 372 us -> 0.04 us  [gather_row(): return lax.all_gather(shard, 'row', axis=0, tiled=False)]
    ppermute x0 -> x77, waiting for transfers between devices: none -> 180 us  [the longest x11 69.7 us: group_shift(): return lax.ppermute(value, 'col', pairs)]
    ppermute x0 -> x77, starting transfers between devices: none -> 146 us  [the longest x8 35.9 us: finish(): arrived = lax.ppermute(block, ('dp', 'col'), pairs)]
    psum x10 -> x0, blocking collectives: 135 us -> none  [the longest x1 39.7 us: body(): lax.psum((local_count, local_squared), ('dp', 'row', 'col'))]
    unnamed x31 -> x20, waiting for transfers between devices: 2.53 us -> 69.6 us
    convert_element_type x4 -> x30, other arithmetic: 4.95 us -> 34.9 us  [the longest x4 13.5 us: body(): hid = gelu_exact(pre).astype(low_type)]
    dynamic_update_slice x0 -> x28, local copies, waits for them, and re-layouts: none -> 24.6 us  [the longest x12 8.31 us: gather_row_direct(): whole = lax.dynamic_update_index_in_dim(whole, piece, mine ^ step, 0)]
  transfers between devices with their start and end apart: 31 -> 89, of which waited for: 30 -> 34; matrix products, arithmetic and copies ran while one was open for 8% -> 33% of each run, Pallas kernels for 0% -> 0%
where the time goes in v1:
time: 720 us; the launch traced here: 709 us
  waiting for transfers between devices  250 us (35%)
  starting transfers between devices  148 us (21%)
  local copies, waits for them, and re-layouts  109 us (15%)
  matrix products  104 us (14%)
  other arithmetic  73.3 us (10%)
  between operations  24.7 us (3%)
    dot_general x60, matrix products, dot(): return jnp.einsum(spec, left, right, preferred_element_type=jnp.float32)  104 us
    ppermute x11, waiting for transfers between devices, group_shift(): return lax.ppermute(value, 'col', pairs)  69.7 us
    unnamed x20, waiting for transfers between devices  69.6 us
    ppermute x8, starting transfers between devices, finish(): arrived = lax.ppermute(block, ('dp', 'col'), pairs)  35.9 us
    ppermute x12, waiting for transfers between devices, gather_row_direct(): piece = lax.ppermute(shard, 'row', [(i, i ^ step) for i in range(count)])  35.2 us
    ppermute x8, starting transfers between devices, fetch(): moved = lax.ppermute(shard, ('dp', 'col'), weight_pairs)  34.1 us
    unnamed x335, local copies, waits for them, and re-layouts  29.5 us
    ppermute x6, waiting for transfers between devices, flip_col(): lax.ppermute(value, 'col', [(i, count - 1 - i) for i in range(count)])  27.6 us
  transfers between devices with their start and end apart: 89, of which 34 were waited for; matrix products, arithmetic and copies ran while one was open for 33% of the time, Pallas kernels for 0%

profile of v1, /device:TPU:1, one launch (start us, length us, event | category | flops | bytes accessed | tf_op | source)
XLA Modules:
  0.0 708.6 jit_solution(2780963273082035638)
XLA Ops:
  9.5 6.2 collective-permute-start.20
  15.6 6.7 collective-permute-done.20
  25.8 3.3 collective-permute-start.2
  30.5 5.2 collective-permute-start.14
  51.7 5.1 collective-permute-start.21
  63.7 8.8 %collective-permute-start.3 = (f32[2,12,256]{2,1,0:T(8,128)S(1)}, f32[2,12,256]{2,1,0:T(8,128)S(1)}, u32[]{:S(2)}, u32[]{:S(2)}) collective-permute-start(f32[2,12,256]{2,1,0:T(8,128)S(1)} %get-tuple-element.149), channel_id=1, source_target_pairs={{0,1},{1,0},{2,3},{3,2},{4,5},{5,4},{6,7},{7,6},{8,9},{9,8},{10,11... | collective-permute-start | bytes 73736 | tf_op jit(solution)/shard_map/ppermute | solution.py:32
  91.4 4.5 collective-permute-start.36
  98.1 5.9 collective-permute-done.15
  105.3 3.3 collective-permute-done.16
  110.3 3.3 collective-permute-done.17
  113.5 6.6 collective-permute-start.37
  127.4 5.5 collective-permute-done.5
  136.0 14.3 %collective-permute-done.7 = bf16[256,3,256]{2,0,1:T(8,128)(2,1)S(1)} collective-permute-done((bf16[256,3,256]{2,0,1:T(8,128)(2,1)}, bf16[256,3,256]{2,0,1:T(8,128)(2,1)S(1)}, u32[]{:S(2)}, u32[]{:S(2)}) %collective-permute-start.7) | collective-permute-done | bytes 393248 | tf_op jit(solution)/shard_map/ppermute | solution.py:61
  189.5 7.6 %collective-permute-done.19 = bf16[320,1024]{1,0:T(8,128)(2,1)S(1)} collective-permute-done((bf16[320,1024]{1,0:T(8,128)(2,1)S(1)}, bf16[320,1024]{1,0:T(8,128)(2,1)S(1)}, u32[]{:S(2)}, u32[]{:S(2)}) %collective-permute-start.19) | collective-permute-done | bytes 655392 | tf_op jit(solution)/shard_map/ppermute | solution.py:32
  203.3 3.9 fusion.73
  210.0 3.7 fusion.74
  221.9 11.1 %collective-permute-done.24 = bf16[320,1024]{1,0:T(8,128)(2,1)S(1)} collective-permute-done((bf16[320,1024]{1,0:T(8,128)(2,1)S(1)}, bf16[320,1024]{1,0:T(8,128)(2,1)S(1)}, u32[]{:S(2)}, u32[]{:S(2)}) %collective-permute-start.24) | collective-permute-done | bytes 655392 | tf_op jit(solution)/shard_map/ppermute | solution.py:32
  268.5 18.1 %collective-permute-done.12 = f32[320,256]{1,0:T(8,128)S(1)} collective-permute-done((f32[320,256]{1,0:T(8,128)S(1)}, f32[320,256]{1,0:T(8,128)S(1)}, u32[]{:S(2)}, u32[]{:S(2)}) %collective-permute-start.12) | collective-permute-done | bytes 327712 | tf_op jit(solution)/shard_map/ppermute | solution.py:20
  312.8 9.4 %collective-permute-done.40 = bf16[320,1024]{1,0:T(8,128)(2,1)S(1)} collective-permute-done((bf16[320,1024]{1,0:T(8,128)(2,1)S(1)}, bf16[320,1024]{1,0:T(8,128)(2,1)S(1)}, u32[]{:S(2)}, u32[]{:S(2)}) %collective-permute-start.40) | collective-permute-done | bytes 655392 | tf_op jit(solution)/shard_map/ppermute | solution.py:32
  330.3 14.4 %collective-permute-done.41 = bf16[320,1024]{1,0:T(8,128)(2,1)S(1)} collective-permute-done((bf16[320,1024]{1,0:T(8,128)(2,1)S(1)}, bf16[320,1024]{1,0:T(8,128)(2,1)S(1)}, u32[]{:S(2)}, u32[]{:S(2)}) %collective-permute-start.41) | collective-permute-done | bytes 655392 | tf_op jit(solution)/shard_map/ppermute | solution.py:32
  349.3 3.8 fusion.57
  370.2 10.5 %collective-permute-done.42 = bf16[320,1024]{1,0:T(8,128)(2,1)S(1)} collective-permute-done((bf16[320,1024]{1,0:T(8,128)(2,1)S(1)}, bf16[320,1024]{1,0:T(8,128)(2,1)S(1)}, u32[]{:S(2)}, u32[]{:S(2)}) %collective-permute-start.42) | collective-permute-done | bytes 655392 | tf_op jit(solution)/shard_map/ppermute | solution.py:32
  398.5 3.3 convolution_convert_fusion.4
  411.4 3.4 collective-permute-start.59
  418.1 3.6 add_convert_fusion
  441.3 3.3 multiply_reduce_fusion
  450.2 4.2 fusion.2
  458.5 15.7 %collective-permute-done.44 = bf16[320,1024]{1,0:T(8,128)(2,1)S(1)} collective-permute-done((bf16[320,1024]{1,0:T(8,128)(2,1)S(1)}, bf16[320,1024]{1,0:T(8,128)(2,1)S(1)}, u32[]{:S(2)}, u32[]{:S(2)}) %collective-permute-start.44) | collective-permute-done | bytes 655392 | tf_op jit(solution)/shard_map/ppermute | solution.py:32
  480.5 3.0 collective-permute-done.53
  488.7 3.8 collective-permute-done.71
  496.3 3.7 convolution_convert_fusion.2
  502.1 9.4 %collective-permute-done.45 = f32[320,256]{1,0:T(8,128)} collective-permute-done((f32[320,256]{1,0:T(8,128)S(1)}, f32[320,256]{1,0:T(8,128)}, u32[]{:S(2)}, u32[]{:S(2)}) %collective-permute-start.45) | collective-permute-done | bytes 327712 | tf_op jit(solution)/shard_map/ppermute | solution.py:20
  518.3 3.7 collective-permute-start.63
  526.6 3.4 collective-permute-start.46
  530.1 4.6 fusion.1
  534.8 3.6 collective-permute-done.47
  545.6 3.9 collective-permute-start.49
  554.6 7.3 %collective-permute-done.50 = f32[]{:T(128)} collective-permute-done((f32[]{:T(128)}, f32[]{:T(128)}, u32[]{:S(2)}, u32[]{:S(2)}) %collective-permute-start.50) | collective-permute-done | bytes 36 | tf_op jit(solution)/shard_map/ppermute | solution.py:48
  563.2 5.1 collective-permute-start.60
  572.9 6.9 collective-permute-start.57
  586.9 3.3 collective-permute-done.69
  591.7 4.1 collective-permute-done.75
  598.5 5.3 reduce-scatter.25.cloned.1.call-done
  603.8 6.2 collective-permute-start.54
  610.0 32.0 %reduce-scatter.37.cloned.1.call-done = bf16[1,1024,256]{1,2,0:T(8,128)(2,1)} async-done(((bf16[4,1024,256]{1,2,0:T(8,128)(2,1)}), bf16[1,1024,256]{1,2,0:T(8,128)(2,1)}) %reduce-scatter.37.cloned.1.call-update) | async-done | bytes 524304
  642.0 5.7 collective-permute-start.72
  648.8 32.1 %reduce-scatter.33.cloned.1.call-done = bf16[1,256,1024]{2,1,0:T(8,128)(2,1)} async-done(((bf16[4,256,1024]{2,1,0:T(8,128)(2,1)}), bf16[1,256,1024]{2,1,0:T(8,128)(2,1)}) %reduce-scatter.33.cloned.1.call-update) | async-done | bytes 524304
  680.9 5.7 collective-permute-start.66
  (774 shorter events, 336.4 us)
Async XLA Ops:
  7.3 190.2 %all-gather.9.cloned.1.call-start = ((), (), s32[]{:S(2)}) async-start(), calls=%async_computation.8 | async-start | bytes 2621440 | tf_op jit(solution)/shard_map/all_gather | solution.py:67
  23.1 178.2 %all-gather.11.cloned.1.call-start = ((), (), s32[]{:S(2)}) async-start(), calls=%async_computation.9 | async-start | bytes 2621440 | tf_op jit(solution)/shard_map/all_gather | solution.py:67
  23.8 20.4 %collective-permute-start.9 = (s32[]{:T(128)}, s32[]{:T(128)}, u32[]{:S(2)}, u32[]{:S(2)}) collective-permute-start(s32[]{:T(128)} %reduce_sum.363), channel_id=1, source_target_pairs={{0,16},{16,0},{1,17},{17,1},{2,18},{18,2},{3,19},{19,3},{4,20},{20... | collective-permute-start | bytes 20 | tf_op jit(solution)/shard_map/ppermute | solution.py:48
  25.8 32.6 %collective-permute-start.2 = (f32[24,256]{1,0:T(8,128)}, f32[24,256]{1,0:T(8,128)}, u32[]{:S(2)}, u32[]{:S(2)}) collective-permute-start(f32[24,256]{1,0:T(8,128)} %concatenate.52), channel_id=1, source_target_pairs={{0,3},{1,2},{2,1},{3,0},{4,7},{5,6},{6,5},{7,4},{8,11},{9,10},{10,... | collective-permute-start | bytes 73736 | tf_op jit(solution)/shard_map/ppermute | solution.py:20
  29.8 90.4 %collective-permute-start = (f32[320,256]{1,0:T(8,128)}, f32[320,256]{1,0:T(8,128)S(1)}, u32[]{:S(2)}, u32[]{:S(2)}) collective-permute-start(f32[320,256]{1,0:T(8,128)} %constant_dynamic-slice_fusion.3), channel_id=1, source_target_pairs={{0,3},{1,2},{2,1},{3,0},{4,7},{5,6},{6,5},{7,4},{8,11},{9,10},{10,... | collective-permute-start | bytes 983048 | tf_op jit(solution)/shard_map/ppermute | solution.py:20
  30.5 60.9 %collective-permute-start.14 = (bf16[256,256]{1,0:T(8,128)(2,1)}, bf16[256,256]{1,0:T(8,128)(2,1)}, u32[]{:S(2)}, u32[]{:S(2)}) collective-permute-start(bf16[256,256]{1,0:T(8,128)(2,1)} %get-tuple-element.145), channel_id=1, source_target_pairs={{0,0},{1,1},{2,2},{3,3},{16,19},{17,18},{18,17},{19,16},{4,4},{5,5... | collective-permute-start | bytes 393224 | tf_op jit(solution)/shard_map/ppermute | solution.py:182
  36.6 85.8 %collective-permute-start.4 = (bf16[256,3,256]{2,0,1:T(8,128)(2,1)}, bf16[256,3,256]{2,0,1:T(8,128)(2,1)}, u32[]{:S(2)}, u32[]{:S(2)}) collective-permute-start(bf16[256,3,256]{2,0,1:T(8,128)(2,1)} %get-tuple-element.143), channel_id=1, source_target_pairs={{0,0},{1,1},{2,2},{3,3},{16,19},{17,18},{18,17},{19,16},{4,4},{5,5... | collective-permute-start | bytes 1179656 | tf_op jit(solution)/shard_map/ppermute | solution.py:182
  58.3 38.5 %collective-permute-start.30 = (bf16[256,256]{1,0:T(8,128)(2,1)}, bf16[256,256]{1,0:T(8,128)(2,1)S(1)}, u32[]{:S(2)}, u32[]{:S(2)}) collective-permute-start(bf16[256,256]{1,0:T(8,128)(2,1)} %get-tuple-element.144), channel_id=1, source_target_pairs={{0,0},{1,1},{2,2},{3,3},{16,19},{17,18},{18,17},{19,16},{4,4},{5,5... | collective-permute-start | bytes 393224 | tf_op jit(solution)/shard_map/ppermute | solution.py:182
  63.7 16.9 %collective-permute-start.3 = (f32[2,12,256]{2,1,0:T(8,128)S(1)}, f32[2,12,256]{2,1,0:T(8,128)S(1)}, u32[]{:S(2)}, u32[]{:S(2)}) collective-permute-start(f32[2,12,256]{2,1,0:T(8,128)S(1)} %get-tuple-element.149), channel_id=1, source_target_pairs={{0,1},{1,0},{2,3},{3,2},{4,5},{5,4},{6,7},{7,6},{8,9},{9,8},{10,11... | collective-permute-start | bytes 73736 | tf_op jit(solution)/shard_map/ppermute | solution.py:32
  72.5 149.3 %all-gather.13.cloned.1.call-start = ((), (), s32[]{:S(2)}) async-start(), calls=%async_computation.10 | async-start | bytes 2621440 | tf_op jit(solution)/shard_map/all_gather | solution.py:67
  80.6 43.2 %collective-permute-start.25 = (bf16[256,3,256]{2,0,1:T(8,128)(2,1)}, bf16[256,3,256]{2,0,1:T(8,128)(2,1)}, u32[]{:S(2)}, u32[]{:S(2)}) collective-permute-start(bf16[256,3,256]{2,0,1:T(8,128)(2,1)} %get-tuple-element.142), channel_id=1, source_target_pairs={{0,0},{1,1},{2,2},{3,3},{16,19},{17,18},{18,17},{19,16},{4,4},{5,5... | collective-permute-start | bytes 1179656 | tf_op jit(solution)/shard_map/ppermute | solution.py:182
  91.4 35.8 %collective-permute-start.36 = (bf16[256,1024]{1,0:T(8,128)(2,1)}, bf16[256,1024]{1,0:T(8,128)(2,1)}, u32[]{:S(2)}, u32[]{:S(2)}) collective-permute-start(bf16[256,1024]{1,0:T(8,128)(2,1)} %get-tuple-element.132), channel_id=1, source_target_pairs={{0,0},{1,1},{2,2},{3,3},{16,19},{17,18},{18,17},{19,16},{4,4},{5,5... | collective-permute-start | bytes 1572872 | tf_op jit(solution)/shard_map/ppermute | solution.py:182
  113.5 107.8 %collective-permute-start.37 = (bf16[1024,256]{1,0:T(8,128)(2,1)}, bf16[1024,256]{1,0:T(8,128)(2,1)}, u32[]{:S(2)}, u32[]{:S(2)}) collective-permute-start(bf16[1024,256]{1,0:T(8,128)(2,1)} %get-tuple-element.130), channel_id=1, source_target_pairs={{0,0},{1,1},{2,2},{3,3},{16,19},{17,18},{18,17},{19,16},{4,4},{5,5... | collective-permute-start | bytes 1572872 | tf_op jit(solution)/shard_map/ppermute | solution.py:182
  120.2 97.2 %collective-permute-start.31 = (bf16[256,256]{1,0:T(8,128)(2,1)S(1)}, bf16[256,256]{1,0:T(8,128)(2,1)}, u32[]{:S(2)}, u32[]{:S(2)}) collective-permute-start(bf16[256,256]{1,0:T(8,128)(2,1)S(1)} %collective-permute-done.30), channel_id=1, source_target_pairs={{0,4},{4,0},{8,12},{12,8},{1,5},{5,1},{9,13},{13,9},{2,6},{6,2},{1... | collective-permute-start | bytes 393224 | tf_op jit(solution)/shard_map/ppermute | solution.py:61
  127.1 23.2 %collective-permute-start.1 = (f32[2,320,256]{2,1,0:T(8,128)}, f32[2,320,256]{2,1,0:T(8,128)}, u32[]{:S(2)}, u32[]{:S(2)}) collective-permute-start(f32[2,320,256]{2,1,0:T(8,128)} %pad_maximum_fusion.2), channel_id=1, source_target_pairs={{0,1},{1,0},{2,3},{3,2},{4,5},{5,4},{6,7},{7,6},{8,9},{9,8},{10,11... | collective-permute-start | bytes 1966088 | tf_op jit(solution)/shard_map/ppermute | solution.py:32
  127.2 160.4 %all-gather.15.cloned.1.call-start = ((), (), s32[]{:S(2)}) async-start(), calls=%async_computation.11 | async-start | bytes 2621440 | tf_op jit(solution)/shard_map/all_gather | solution.py:67
  132.9 17.4 %collective-permute-start.7 = (bf16[256,3,256]{2,0,1:T(8,128)(2,1)}, bf16[256,3,256]{2,0,1:T(8,128)(2,1)S(1)}, u32[]{:S(2)}, u32[]{:S(2)}) collective-permute-start(bf16[256,3,256]{2,0,1:T(8,128)(2,1)} %collective-permute-done.4), channel_id=1, source_target_pairs={{0,12},{4,8},{8,4},{12,0},{1,13},{5,9},{9,5},{13,1},{2,14},{6,10},... | collective-permute-start | bytes 1179656 | tf_op jit(solution)/shard_map/ppermute | solution.py:61
  134.9 42.4 %collective-permute-start.18 = (bf16[4,256,256]{2,1,0:T(8,128)(2,1)S(1)}, bf16[4,256,256]{2,1,0:T(8,128)(2,1)}, u32[]{:S(2)}, u32[]{:S(2)}) collective-permute-start(bf16[4,256,256]{2,1,0:T(8,128)(2,1)S(1)} %bitcast_dynamic-update-slice_fusion.12), channel_id=1, source_target_pairs={{0,16},{16,0},{1,17},{17,1},{2,18},{18,2},{3,19},{19,3},{4,20},{20... | collective-permute-start | bytes 1572872 | tf_op jit(solution)/shard_map/ppermute | solution.py:25
  150.3 31.3 %collective-permute-start.26 = (bf16[256,3,256]{2,0,1:T(8,128)(2,1)}, bf16[256,3,256]{2,0,1:T(8,128)(2,1)}, u32[]{:S(2)}, u32[]{:S(2)}) collective-permute-start(bf16[256,3,256]{2,0,1:T(8,128)(2,1)} %collective-permute-done.25), channel_id=1, source_target_pairs={{0,4},{4,0},{8,12},{12,8},{1,5},{5,1},{9,13},{13,9},{2,6},{6,2},{1... | collective-permute-start | bytes 1179656 | tf_op jit(solution)/shard_map/ppermute | solution.py:61
  150.4 17.7 %collective-permute-start.8 = (bf16[4,256,3,256]{3,1,0,2:T(8,128)(2,1)S(1)}, bf16[4,256,3,256]{3,1,0,2:T(8,128)(2,1)}, u32[]{:S(2)}, u32[]{:S(2)}) collective-permute-start(bf16[4,256,3,256]{3,1,0,2:T(8,128)(2,1)S(1)} %bitcast_dynamic-update-slice_fusion.7), channel_id=1, source_target_pairs={{0,16},{16,0},{1,17},{17,1},{2,18},{18,2},{3,19},{19,3},{4,20},{20... | collective-permute-start | bytes 4718600 | tf_op jit(solution)/shard_map/ppermute | solution.py:25
  183.5 36.0 %collective-permute-start.32 = (bf16[256,256]{1,0:T(8,128)(2,1)S(1)}, bf16[256,256]{1,0:T(8,128)(2,1)}, u32[]{:S(2)}, u32[]{:S(2)}) collective-permute-start(bf16[256,256]{1,0:T(8,128)(2,1)S(1)} %collective-permute-done.30), channel_id=1, source_target_pairs={{0,8},{4,12},{8,0},{12,4},{1,9},{5,13},{9,1},{13,5},{2,10},{6,14},... | collective-permute-start | bytes 393224 | tf_op jit(solution)/shard_map/ppermute | solution.py:61
  213.7 22.4 %collective-permute-start.29 = (bf16[4,256,3,256]{3,1,0,2:T(8,128)(2,1)}, bf16[4,256,3,256]{3,1,0,2:T(8,128)(2,1)}, u32[]{:S(2)}, u32[]{:S(2)}) collective-permute-start(bf16[4,256,3,256]{3,1,0,2:T(8,128)(2,1)} %bitcast_dynamic-update-slice_fusion.6), channel_id=1, source_target_pairs={{0,16},{16,0},{1,17},{17,1},{2,18},{18,2},{3,19},{19,3},{4,20},{20... | collective-permute-start | bytes 4718600 | tf_op jit(solution)/shard_map/ppermute | solution.py:25
  217.4 15.7 %collective-permute-start.24 = (bf16[320,1024]{1,0:T(8,128)(2,1)S(1)}, bf16[320,1024]{1,0:T(8,128)(2,1)S(1)}, u32[]{:S(2)}, u32[]{:S(2)}) collective-permute-start(bf16[320,1024]{1,0:T(8,128)(2,1)S(1)} %convert_element_type.534), channel_id=1, source_target_pairs={{0,1},{1,0},{2,3},{3,2},{4,5},{5,4},{6,7},{7,6},{8,9},{9,8},{10,11... | collective-permute-start | bytes 1966088 | tf_op jit(solution)/shard_map/ppermute | solution.py:32
  220.5 40.2 %collective-permute-start.34 = (bf16[4,256,256]{2,1,0:T(8,128)(2,1)S(1)}, bf16[4,256,256]{2,1,0:T(8,128)(2,1)}, u32[]{:S(2)}, u32[]{:S(2)}) collective-permute-start(bf16[4,256,256]{2,1,0:T(8,128)(2,1)S(1)} %bitcast_dynamic-update-slice_fusion.8), channel_id=1, source_target_pairs={{0,16},{16,0},{1,17},{17,1},{2,18},{18,2},{3,19},{19,3},{4,20},{20... | collective-permute-start | bytes 1572872 | tf_op jit(solution)/shard_map/ppermute | solution.py:25
  221.3 296.9 %reduce-scatter.31.cloned.1.call-start = ((), (), s32[]{:S(2)}) async-start(), calls=%async_computation.15 | async-start | bytes 655360
  221.8 71.0 %collective-permute-start.38 = (bf16[4,256,1024]{2,1,0:T(8,128)(2,1)}, bf16[4,256,1024]{2,1,0:T(8,128)(2,1)}, u32[]{:S(2)}, u32[]{:S(2)}) collective-permute-start(bf16[4,256,1024]{2,1,0:T(8,128)(2,1)} %bitcast.552), channel_id=1, source_target_pairs={{0,16},{16,0},{1,17},{17,1},{2,18},{18,2},{3,19},{19,3},{4,20},{20... | collective-permute-start | bytes 6291464 | tf_op jit(solution)/shard_map/ppermute | solution.py:25
  263.8 26.3 %collective-permute-start.35 = (bf16[320,1024]{1,0:T(8,128)(2,1)}, bf16[320,1024]{1,0:T(8,128)(2,1)}, u32[]{:S(2)}, u32[]{:S(2)}) collective-permute-start(bf16[320,1024]{1,0:T(8,128)(2,1)} %convert_element_type.549), channel_id=1, source_target_pairs={{0,1},{1,0},{2,3},{3,2},{4,5},{5,4},{6,7},{7,6},{8,9},{9,8},{10,11... | collective-permute-start | bytes 1966088 | tf_op jit(solution)/shard_map/ppermute | solution.py:32
  264.9 21.7 %collective-permute-start.12 = (f32[320,256]{1,0:T(8,128)S(1)}, f32[320,256]{1,0:T(8,128)S(1)}, u32[]{:S(2)}, u32[]{:S(2)}) collective-permute-start(f32[320,256]{1,0:T(8,128)S(1)} %constant_dynamic-slice_fusion.2), channel_id=1, source_target_pairs={{0,3},{1,2},{2,1},{3,0},{4,7},{5,6},{6,5},{7,4},{8,11},{9,10},{10,... | collective-permute-start | bytes 983048 | tf_op jit(solution)/shard_map/ppermute | solution.py:20
  287.5 20.3 %collective-permute-start.13 = (f32[2,320,256]{2,1,0:T(8,128)}, f32[2,320,256]{2,1,0:T(8,128)}, u32[]{:S(2)}, u32[]{:S(2)}) collective-permute-start(f32[2,320,256]{2,1,0:T(8,128)} %pad_maximum_fusion.3), channel_id=1, source_target_pairs={{0,1},{1,0},{2,3},{3,2},{4,5},{5,4},{6,7},{7,6},{8,9},{9,8},{10,11... | collective-permute-start | bytes 1966088 | tf_op jit(solution)/shard_map/ppermute | solution.py:32
  305.3 16.9 %collective-permute-start.40 = (bf16[320,1024]{1,0:T(8,128)(2,1)S(1)}, bf16[320,1024]{1,0:T(8,128)(2,1)S(1)}, u32[]{:S(2)}, u32[]{:S(2)}) collective-permute-start(bf16[320,1024]{1,0:T(8,128)(2,1)S(1)} %convert_element_type.554), channel_id=1, source_target_pairs={{0,1},{1,0},{2,3},{3,2},{4,5},{5,4},{6,7},{7,6},{8,9},{9,8},{10,11... | collective-permute-start | bytes 1966088 | tf_op jit(solution)/shard_map/ppermute | solution.py:32
  329.0 15.7 %collective-permute-start.41 = (bf16[320,1024]{1,0:T(8,128)(2,1)S(1)}, bf16[320,1024]{1,0:T(8,128)(2,1)S(1)}, u32[]{:S(2)}, u32[]{:S(2)}) collective-permute-start(bf16[320,1024]{1,0:T(8,128)(2,1)S(1)} %get-tuple-element.186), channel_id=1, source_target_pairs={{0,1},{1,0},{2,3},{3,2},{4,5},{5,4},{6,7},{7,6},{8,9},{9,8},{10,11... | collective-permute-start | bytes 1966088 | tf_op jit(solution)/shard_map/ppermute | solution.py:32
  368.2 36.4 %collective-permute-start.62 = (bf16[4,256,256]{1,2,0:T(8,128)(2,1)}, bf16[4,256,256]{1,2,0:T(8,128)(2,1)}, u32[]{:S(2)}, u32[]{:S(2)}) collective-permute-start(bf16[4,256,256]{1,2,0:T(8,128)(2,1)} %fusion.63), channel_id=1, source_target_pairs={{0,16},{16,0},{1,17},{17,1},{2,18},{18,2},{3,19},{19,3},{4,20},{20... | collective-permute-start | bytes 1572872 | tf_op jit(solution)/shard_map/ppermute | solution.py:25
  401.8 16.3 %collective-permute-start.56 = (bf16[4,256,3,256]{3,1,2,0:T(8,128)(2,1)}, bf16[4,256,3,256]{3,1,2,0:T(8,128)(2,1)}, u32[]{:S(2)}, u32[]{:S(2)}) collective-permute-start(bf16[4,256,3,256]{3,1,2,0:T(8,128)(2,1)} %convolution_convert_fusion.4), channel_id=1, source_target_pairs={{0,16},{16,0},{1,17},{17,1},{2,18},{18,2},{3,19},{19,3},{4,20},{20... | collective-permute-start | bytes 4718600 | tf_op jit(solution)/shard_map/ppermute | solution.py:25
  407.0 156.2 %reduce-scatter.29.cloned.1.call-start = ((), (), s32[]{:S(2)}) async-start(), calls=%async_computation.14 | async-start | bytes 655360
  417.6 155.3 %reduce-scatter.27.cloned.1.call-start = ((), (), s32[]{:S(2)}) async-start(), calls=%async_computation.13 | async-start | bytes 1966080
  421.7 159.1 %reduce-scatter.35.cloned.1.call-start = ((), (), s32[]{:S(2)}) async-start(), calls=%async_computation.17 | async-start | bytes 2621440
  431.8 151.3 %reduce-scatter.39.cloned.1.call-start = ((), (), s32[]{:S(2)}) async-start(), calls=%async_computation.19 | async-start | bytes 2621440
  454.5 149.3 %reduce-scatter.25.cloned.1.call-start = ((), (), s32[]{:S(2)}) async-start(), calls=%async_computation.12 | async-start | bytes 1966080
  457.7 16.5 %collective-permute-start.44 = (bf16[320,1024]{1,0:T(8,128)(2,1)S(1)}, bf16[320,1024]{1,0:T(8,128)(2,1)S(1)}, u32[]{:S(2)}, u32[]{:S(2)}) collective-permute-start(bf16[320,1024]{1,0:T(8,128)(2,1)S(1)} %get-tuple-element.200), channel_id=1, source_target_pairs={{0,1},{1,0},{2,3},{3,2},{4,5},{5,4},{6,7},{7,6},{8,9},{9,8},{10,11... | collective-permute-start | bytes 1966088 | tf_op jit(solution)/shard_map/ppermute | solution.py:32
  485.7 156.2 %reduce-scatter.37.cloned.1.call-start = ((), (), s32[]{:S(2)}) async-start(), calls=%async_computation.18 | async-start | bytes 2621440
  495.2 185.6 %reduce-scatter.33.cloned.1.call-start = ((), (), s32[]{:S(2)}) async-start(), calls=%async_computation.16 | async-start | bytes 2621440
  500.0 30.1 %collective-permute-start.65 = (bf16[4,256,1024]{2,1,0:T(8,128)(2,1)}, bf16[4,256,1024]{2,1,0:T(8,128)(2,1)}, u32[]{:S(2)}, u32[]{:S(2)}) collective-permute-start(bf16[4,256,1024]{2,1,0:T(8,128)(2,1)} %bitcast.175), channel_id=1, source_target_pairs={{0,16},{16,0},{1,17},{17,1},{2,18},{18,2},{3,19},{19,3},{4,20},{20... | collective-permute-start | bytes 6291464 | tf_op jit(solution)/shard_map/ppermute | solution.py:25
  541.7 20.8 %collective-permute-start.52 = (f32[25,256]{1,0:T(8,128)S(1)}, f32[25,256]{1,0:T(8,128)S(1)}, u32[]{:S(2)}, u32[]{:S(2)}) collective-permute-start(f32[25,256]{1,0:T(8,128)S(1)} %slice_bitcast_fusion.20), channel_id=1, source_target_pairs={{0,3},{1,2},{2,1},{3,0},{4,7},{5,6},{6,5},{7,4},{8,11},{9,10},{10,... | collective-permute-start | bytes 76808 | tf_op jit(solution)/shard_map/ppermute | solution.py:20
  542.7 37.1 %collective-permute-start.51 = (f32[320,256]{1,0:T(8,128)S(1)}, f32[320,256]{1,0:T(8,128)}, u32[]{:S(2)}, u32[]{:S(2)}) collective-permute-start(f32[320,256]{1,0:T(8,128)S(1)} %constant_dynamic-slice_fusion), channel_id=1, source_target_pairs={{0,3},{1,2},{2,1},{3,0},{4,7},{5,6},{6,5},{7,4},{8,11},{9,10},{10,... | collective-permute-start | bytes 983048 | tf_op jit(solution)/shard_map/ppermute | solution.py:20
  590.4 57.2 %collective-permute-start.70 = (bf16[256,1024]{1,0:T(8,128)(2,1)S(1)}, bf16[256,1024]{1,0:T(8,128)(2,1)}, u32[]{:S(2)}, u32[]{:S(2)}) collective-permute-start(bf16[256,1024]{1,0:T(8,128)(2,1)S(1)} %add_convert_fusion.13), channel_id=1, source_target_pairs={{0,16},{1,17},{2,18},{3,19},{4,20},{5,21},{6,22},{7,23},{8,24},{9,... | collective-permute-start | bytes 1572872 | tf_op jit(solution)/shard_map/ppermute | solution.py:324
  596.1 90.5 %collective-permute-start.76 = (bf16[1024,256]{0,1:T(8,128)(2,1)S(1)}, bf16[1024,256]{0,1:T(8,128)(2,1)}, u32[]{:S(2)}, u32[]{:S(2)}) collective-permute-start(bf16[1024,256]{0,1:T(8,128)(2,1)S(1)} %add_convert_fusion.11), channel_id=1, source_target_pairs={{0,16},{1,17},{2,18},{3,19},{4,20},{5,21},{6,22},{7,23},{8,24},{9,... | collective-permute-start | bytes 1572872 | tf_op jit(solution)/shard_map/ppermute | solution.py:324
  603.8 83.9 %collective-permute-start.54 = (bf16[256,3,256]{2,0,1:T(8,128)(2,1)}, bf16[256,3,256]{2,0,1:T(8,128)(2,1)}, u32[]{:S(2)}, u32[]{:S(2)}) collective-permute-start(bf16[256,3,256]{2,0,1:T(8,128)(2,1)} %bitcast.610), channel_id=1, source_target_pairs={{16,3},{17,2},{18,1},{19,0},{20,7},{21,6},{22,5},{23,4},{24,11},{2... | collective-permute-start | bytes 1179656 | tf_op jit(solution)/shard_map/ppermute | solution.py:322
  642.0 48.2 %collective-permute-start.72 = (bf16[1024,256]{0,1:T(8,128)(2,1)}, bf16[1024,256]{0,1:T(8,128)(2,1)S(1)}, u32[]{:S(2)}, u32[]{:S(2)}) collective-permute-start(bf16[1024,256]{0,1:T(8,128)(2,1)} %bitcast.607), channel_id=1, source_target_pairs={{16,3},{17,2},{18,1},{19,0},{20,7},{21,6},{22,5},{23,4},{24,11},{2... | collective-permute-start | bytes 1572872 | tf_op jit(solution)/shard_map/ppermute | solution.py:322
  (203 other events, 1261.2 us)
Sparse Core Ops, SparseCore 0:
  23.2 38.6 all-gather.8
  72.6 35.1 all-gather.10
  127.3 45.8 all-gather.12
  221.5 33.3 all-gather.14
  407.1 22.7 reduce-scatter.30
  432.9 24.7 reduce-scatter.28
  461.2 31.0 reduce-scatter.26
  495.8 35.2 reduce-scatter.34
  534.3 35.6 reduce-scatter.38
  572.8 30.8 reduce-scatter.24
  606.7 35.1 reduce-scatter.36
  645.6 35.1 reduce-scatter.32

commit v2 on v1

v2 whole, which is shorter than its diff:
```python
import functools

import jax
import jax.numpy as jnp
from jax import lax
from jax.experimental import pallas as pl
from jax.experimental.pallas import tpu as pltpu
from jax.sharding import PartitionSpec as P

HEAD_DIM = 64
LAYERS = 2

epsilon = 1e-06
fill_value = -1e30
score_scale = HEAD_DIM ** (-0.5)
low_type = jnp.bfloat16
wide_type = jnp.float32
VMEM = pl.BlockSpec(memory_space=pltpu.VMEM)
SMEM = pl.BlockSpec(memory_space=pltpu.SMEM)
ANY = pl.BlockSpec(memory_space=pl.ANY)
vmem_bytes = 56 * 1024 * 1024


def dot(left, right):
    return lax.dot_general(
        left, right, (((1,), (0,)), ((), ())), preferred_element_type=wide_type
    )


def dot_right(left, right):
    return lax.dot_general(
        left, right, (((1,), (1,)), ((), ())), preferred_element_type=wide_type
    )


def dot_left(left, right):
    return lax.dot_general(
        left, right, (((0,), (0,)), ((), ())), preferred_element_type=wide_type
    )


def piece_copies(meta, refs, offset, tiles, target, sems):
    if len(refs) == 1:
        return [pltpu.make_async_copy(refs[0], target(None, None), sems.at[0])]
    copies = []
    core = meta[4]
    for place in range(3):
        for block in range(2):
            source = refs[place].at[block, pl.ds(offset, tiles)]
            copies.append((source, target(block, meta[place])))
    copies.append((refs[3].at[pl.ds(offset, tiles)], target(core, meta[3])))
    copies.append((refs[4].at[pl.ds(offset, tiles)], target(1 - core, meta[3])))
    return [
        pltpu.make_async_copy(source, place, sems.at[index])
        for index, (source, place) in enumerate(copies)
    ]


def in_copies(meta, refs, offset, weight, sems):
    def target(block, row_block):
        if block is None:
            return weight
        return weight.at[:, pl.ds(row_block * 256, 256), pl.ds(block * 256, 256)]

    return piece_copies(meta, refs, offset, 3, target, sems)


def proj_copies(meta, refs, offset, weight, sems):
    def target(block, row_block):
        if block is None:
            return weight
        return weight.at[pl.ds(block, 1), :, pl.ds(row_block * 256, 256)]

    return piece_copies(meta, refs, offset, 1, target, sems)


def up_copies(meta, refs, offset, weight, sems):
    def target(block, row_block):
        if block is None:
            return weight
        return weight.at[pl.ds(block * 4, 4), pl.ds(row_block * 256, 256), :]

    return piece_copies(meta, refs, offset, 4, target, sems)


def down_copies(meta, refs, offset, weight, sems):
    def target(block, row_block):
        if block is None:
            return weight
        return weight.at[pl.ds(block * 4, 4), :, pl.ds(row_block * 256, 256)]

    return piece_copies(meta, refs, offset, 4, target, sems)


def start_all(copies):
    for copy in copies:
        copy.start()


def wait_all(copies):
    for copy in copies:
        copy.wait()


def standardize(inputs):
    width = inputs.shape[1]
    centre = jnp.sum(inputs, axis=1, keepdims=True) / width
    centred = inputs - centre
    spread = jnp.sum(centred * centred, axis=1, keepdims=True) / width
    rscale = lax.rsqrt(spread + epsilon)
    return centred * rscale, rscale


def mask_rows(meta, rows, slots):
    parts = []
    for seq in range(rows // slots):
        place = lax.broadcasted_iota(jnp.int32, (slots, 1), 0)
        parts.append(jnp.where(place < meta[5 + seq], 1.0, 0.0).astype(wide_type))
    return parts[0] if len(parts) == 1 else jnp.concatenate(parts, axis=0)


def gelu_and_slope(u):
    size = jnp.abs(u) * 0.7071067811865476
    t = 1.0 / (1.0 + 0.3275911 * size)
    bell = jnp.exp(-size * size)
    tail = t * (
        0.254829592
        + t * (-0.284496736 + t * (1.421413741 + t * (-1.453152027 + t * 1.061405429)))
    )
    tail = 0.5 * tail * bell
    share = jnp.where(u >= 0.0, 1.0 - tail, tail)
    return u * share, share + u * bell * 0.3989422804014327


def place_blocks(meta, place, blocks, target):
    width = blocks[0].shape[1]
    for index, block in enumerate(blocks):
        at = pl.multiple_of(meta[place + index] * width, width)
        target[:, pl.ds(at, width)] = block[...]


def key_bias(meta, seq, slots):
    place = lax.broadcasted_iota(jnp.int32, (1, slots), 1)
    return place < meta[5 + seq]


def split_refs(refs, counts):
    out = []
    at = 0
    for count in counts:
        out.append(refs[at : at + count])
        at += count
    return out


def attend_kernel(first, slots, counts, offsets, meta, *refs):
    (base, sums, params, in_refs, proj_refs, outs, scratch) = split_refs(refs, counts)
    gains, shifts, query_shift, value_shift = params
    x_ref, normed_ref, query_ref, key_ref, value_ref, lse_ref, mixed_ref, wide_ref, low_ref = outs
    in_weight, proj_weight, in_sems, proj_sems = scratch
    in_moves = in_copies(meta, in_refs, offsets[0], in_weight, in_sems)
    proj_moves = proj_copies(meta, proj_refs, offsets[1], proj_weight, proj_sems)
    start_all(in_moves)
    start_all(proj_moves)
    rows = x_ref.shape[0]
    if first:
        place_blocks(meta, 5 + rows // slots, base, x_ref)
        current = x_ref[...]
    else:
        own, arrived, bias = sums
        current = base[0][...] + own[...] + arrived[...].astype(wide_type) + bias[...]
        current = current * mask_rows(meta, rows, slots)
        x_ref[...] = current
    standard, _ = standardize(current)
    normed = (standard * gains[...] + shifts[...]).astype(low_type)
    normed_ref[...] = normed
    wait_all(in_moves)
    query_ref[...] = (dot(normed, in_weight[0]) + query_shift[...]).astype(low_type)
    key_ref[...] = dot(normed, in_weight[1]).astype(low_type)
    value_ref[...] = (dot(normed, in_weight[2]) + value_shift[...]).astype(low_type)
    heads = query_ref.shape[1] // HEAD_DIM
    for seq in range(rows // slots):
        span = slice(seq * slots, (seq + 1) * slots)
        valid = key_bias(meta, seq, slots)
        for head in range(heads):
            lanes = slice(head * HEAD_DIM, (head + 1) * HEAD_DIM)
            scores = dot_right(query_ref[span, lanes], key_ref[span, lanes]) * score_scale
            scores = jnp.where(valid, scores, fill_value)
            maximum = jnp.max(scores, axis=1, keepdims=True)
            exponent = jnp.exp(scores - maximum)
            mass = jnp.sum(exponent, axis=1, keepdims=True)
            attention = (exponent * (1.0 / mass)).astype(low_type)
            mixed_ref[span, lanes] = dot(attention, value_ref[span, lanes]).astype(low_type)
            lse_ref[span, head : head + 1] = maximum + jnp.log(mass)
    wait_all(proj_moves)
    block = proj_weight.shape[1]
    total = dot(mixed_ref[:, :block], proj_weight[0])
    for index in range(1, proj_weight.shape[0]):
        total = total + dot(
            mixed_ref[:, index * block : (index + 1) * block], proj_weight[index]
        )
    wide_ref[...] = total
    low_ref[...] = total.astype(low_type)


def feed_kernel(counts, offsets, meta, *refs):
    (sums, params, up_refs, down_refs, outs, scratch) = split_refs(refs, counts)
    base, own, arrived, bias = sums
    gains, shifts, up_shift = params
    middle_ref, normed_ref, hidden_ref, slope_ref, wide_ref, low_ref = outs
    up_weight, down_weight, up_sems, down_sems = scratch
    up_moves = up_copies(meta, up_refs, offsets[0], up_weight, up_sems)
    down_moves = down_copies(meta, down_refs, offsets[1], down_weight, down_sems)
    start_all(up_moves)
    start_all(down_moves)
    middle = base[...] + own[...] + arrived[...].astype(wide_type) + bias[...]
    middle_ref[...] = middle
    standard, _ = standardize(middle)
    normed = (standard * gains[...] + shifts[...]).astype(low_type)
    normed_ref[...] = normed
    wait_all(up_moves)
    width = up_weight.shape[2]
    for index in range(up_weight.shape[0]):
        lanes = slice(index * width, (index + 1) * width)
        pre = dot(normed_ref[...], up_weight[index]) + up_shift[:, lanes]
        hidden, slope = gelu_and_slope(pre)
        hidden_ref[:, lanes] = hidden.astype(low_type)
        slope_ref[:, lanes] = slope.astype(low_type)
    wait_all(down_moves)
    rows = down_weight.shape[0] * down_weight.shape[1]
    total = dot(hidden_ref[...], down_weight[...].reshape(rows, down_weight.shape[2]))
    wide_ref[...] = total
    low_ref[...] = total.astype(low_type)


def norm_back(grad_rows, inputs, gains):
    standard, rscale = standardize(inputs)
    width = inputs.shape[1]
    scaled = grad_rows * gains
    first = jnp.sum(scaled, axis=1, keepdims=True) / width
    second = jnp.sum(scaled * standard, axis=1, keepdims=True) / width
    grad_input = rscale * (scaled - first - standard * second)
    return (
        grad_input,
        jnp.sum(grad_rows * standard, axis=0, keepdims=True),
        jnp.sum(grad_rows, axis=0, keepdims=True),
    )


def last_kernel(slots, meta, factor, base, own, arrived, bias, *refs):
    seeds, (current_ref, grad_ref) = refs[:-2], refs[-2:]
    rows = base.shape[0]
    mask = mask_rows(meta, rows, slots)
    place_blocks(meta, 5 + rows // slots, seeds, grad_ref)
    current = base[...] + own[...] + arrived[...].astype(wide_type) + bias[...]
    current = current * mask
    current_ref[...] = current
    grad_ref[...] = grad_ref[...] + factor[0] * current


def pull_kernel(inputs, gains, base, own, arrived, grad_ref, gain_ref, shift_ref):
    summed = own[...] + arrived[...].astype(wide_type)
    grad, gain, shift = norm_back(summed, inputs[...], gains[...])
    grad_ref[...] = base[...] + grad
    gain_ref[...] = gain
    shift_ref[...] = shift


def feed_back_kernel(slots, counts, offsets, meta, *refs):
    (sums, up_refs, down_refs, outs, scratch) = split_refs(refs, counts)
    grad, slope_ref = sums
    masked_ref, masked_low_ref, pre_ref, down_bias_ref, up_bias_ref, wide_ref, low_ref = outs
    up_weight, down_weight, up_sems, down_sems = scratch
    up_moves = up_copies(meta, up_refs, offsets[0], up_weight, up_sems)
    down_moves = down_copies(meta, down_refs, offsets[1], down_weight, down_sems)
    start_all(down_moves)
    start_all(up_moves)
    masked = grad[...] * mask_rows(meta, grad.shape[0], slots)
    masked_ref[...] = masked
    masked_low = masked.astype(low_type)
    masked_low_ref[...] = masked_low
    down_bias_ref[...] = jnp.sum(masked_low.astype(wide_type), axis=0, keepdims=True)
    wait_all(down_moves)
    width = up_weight.shape[2]
    for index in range(up_weight.shape[0]):
        lanes = slice(index * width, (index + 1) * width)
        hidden = dot_right(masked_low_ref[...], down_weight[index])
        pre = (hidden * slope_ref[:, lanes].astype(wide_type)).astype(low_type)
        pre_ref[:, lanes] = pre
        up_bias_ref[:, lanes] = jnp.sum(pre.astype(wide_type), axis=0, keepdims=True)
    wait_all(up_moves)
    total = dot_right(pre_ref[:, :width], up_weight[0])
    for index in range(1, up_weight.shape[0]):
        lanes = slice(index * width, (index + 1) * width)
        total = total + dot_right(pre_ref[:, lanes], up_weight[index])
    wide_ref[...] = total
    low_ref[...] = total.astype(low_type)


def attend_back_kernel(slots, counts, offsets, meta, *refs):
    (sums, params, saved, in_refs, proj_refs, outs, scratch) = split_refs(refs, counts)
    own, arrived, middle, masked = sums
    (gains,) = params
    query_ref, key_ref, value_ref, lse_ref = saved
    (
        grad_ref,
        low_grad_ref,
        gain_ref,
        shift_ref,
        proj_bias_ref,
        triple_ref,
        in_bias_ref,
        wide_ref,
        low_ref,
    ) = outs
    in_weight, proj_weight, mixed_grad, in_sems, proj_sems = scratch
    in_moves = in_copies(meta, in_refs, offsets[0], in_weight, in_sems)
    proj_moves = proj_copies(meta, proj_refs, offsets[1], proj_weight, proj_sems)
    start_all(proj_moves)
    start_all(in_moves)
    summed = own[...] + arrived[...].astype(wide_type)
    grad, gain, shift = norm_back(summed, middle[...], gains[...])
    grad = masked[...] + grad
    grad_ref[...] = grad
    gain_ref[...] = gain
    shift_ref[...] = shift
    grad_low = grad.astype(low_type)
    low_grad_ref[...] = grad_low
    proj_bias_ref[...] = jnp.sum(grad_low.astype(wide_type), axis=0, keepdims=True)
    wait_all(proj_moves)
    block = proj_weight.shape[1]
    for index in range(proj_weight.shape[0]):
        mixed_grad[:, index * block : (index + 1) * block] = dot_right(
            low_grad_ref[...], proj_weight[index]
        ).astype(low_type)
    heads = query_ref.shape[1] // HEAD_DIM
    rows = query_ref.shape[0]
    for seq in range(rows // slots):
        span = slice(seq * slots, (seq + 1) * slots)
        valid = key_bias(meta, seq, slots)
        for head in range(heads):
            lanes = slice(head * HEAD_DIM, (head + 1) * HEAD_DIM)
            queries = query_ref[span, lanes]
            keys = key_ref[span, lanes]
            outer = mixed_grad[span, lanes]
            scores = dot_right(queries, keys) * score_scale
            scores = jnp.where(valid, scores, fill_value)
            chance = jnp.exp(scores - lse_ref[span, head : head + 1])
            grad_chance = dot_right(outer, value_ref[span, lanes])
            inner = jnp.sum(grad_chance * chance, axis=1, keepdims=True)
            grad_scores = (chance * (grad_chance - inner)).astype(low_type)
            triple_ref[2, span, lanes] = dot_left(chance.astype(low_type), outer).astype(low_type)
            triple_ref[0, span, lanes] = (dot(grad_scores, keys) * score_scale).astype(low_type)
            triple_ref[1, span, lanes] = (dot_left(grad_scores, queries) * score_scale).astype(
                low_type
            )
    in_bias_ref[0:1, :] = jnp.sum(triple_ref[0].astype(wide_type), axis=0, keepdims=True)
    in_bias_ref[1:2, :] = jnp.sum(triple_ref[2].astype(wide_type), axis=0, keepdims=True)
    wait_all(in_moves)
    total = dot_right(triple_ref[0], in_weight[0])
    total = total + dot_right(triple_ref[1], in_weight[1])
    total = total + dot_right(triple_ref[2], in_weight[2])
    wide_ref[...] = total
    low_ref[...] = total.astype(low_type)


def feed_weight_kernel(meta, normed, pre, hidden, masked_low, *outs):
    def write(place, block, row_block):
        columns = pl.ds(pl.multiple_of(row_block * 256, 256), 256)
        for tile in range(4):
            lanes = pl.ds(pl.multiple_of(block * 1024 + tile * 256, 256), 256)
            place[tile] = dot_left(normed[:, columns], pre[:, lanes]).astype(low_type)
            place[4 + tile] = dot_left(hidden[:, lanes], masked_low[:, columns]).astype(low_type)

    write_pieces(meta, outs, write)


def attend_weight_kernel(meta, normed, triple, mixed, grad_low, *outs):
    def write(place, block, row_block):
        columns = pl.ds(pl.multiple_of(row_block * 256, 256), 256)
        lanes = pl.ds(pl.multiple_of(block * 256, 256), 256)
        for kind in range(3):
            place[kind] = dot_left(normed[:, columns], triple[kind, :, lanes]).astype(low_type)
        place[3] = dot_left(mixed[:, lanes], grad_low[:, columns]).astype(low_type)

    write_pieces(meta, outs, write)


def write_pieces(meta, outs, write):
    core = meta[4]
    for place in range(3):
        for block in range(2):
            write(outs[place].at[block], block, meta[place])
    write(outs[3], core, meta[3])
    write(outs[4], 1 - core, meta[3])


def flip_col(value):
    count = lax.axis_size("col")
    return lax.ppermute(value, "col", [(i, count - 1 - i) for i in range(count)])


def swap_core(value):
    count = lax.axis_size("dp")
    return lax.ppermute(value, "dp", [(i, count - 1 - i) for i in range(count)])


def group_shift(value, step):
    count = lax.axis_size("col")
    half = count // 2
    pairs = [(i, i // half * half + (i % half + step) % half) for i in range(count)]
    return lax.ppermute(value, "col", pairs)


def cross_row(value, first_step, second_step):
    rows = lax.axis_size("row")
    cols = lax.axis_size("col")
    pairs = []
    for core, step in ((0, first_step), (1, second_step)):
        for row in range(rows):
            for col in range(cols):
                source = (core * rows + row) * cols + col
                pairs.append((source, (core * rows + (row ^ step)) * cols + col))
    return lax.ppermute(value, ("dp", "row", "col"), pairs)


def group_total(wide, low):
    arrived = group_shift(low, 1)
    for step in range(2, lax.axis_size("col") // 2):
        wide = wide + group_shift(low, step).astype(wide_type)
    return wide, arrived


def butterfly_sum(value, axes):
    for axis in axes:
        count = lax.axis_size(axis)
        step = 1
        while step < count:
            value = value + lax.ppermute(value, axis, [(i, i ^ step) for i in range(count)])
            step *= 2
    return value


def after(value, *events):
    return lax.optimization_barrier((value,) + events)[0]


def order_blocks(pair):
    count = lax.axis_size("col")
    half = count // 2
    col_index = lax.axis_index("col")
    base = col_index // half * half
    wanted = lax.broadcasted_iota(jnp.int32, (count,) + pair.shape[1:], 0)
    whole = jnp.zeros((count,) + pair.shape[1:], pair.dtype)
    for step in range(half):
        piece = pair if step == 0 else group_shift(pair, step)
        source = base + (col_index - base + half - step) % half
        whole = jnp.where(wanted == source, piece[0][None], whole)
        whole = jnp.where(wanted == count - 1 - source, piece[1][None], whole)
    return whole


def add(left, right):
    return (left.astype(wide_type) + right.astype(wide_type)).astype(low_type)


def gather_near(own):
    return cross_row(own, 1, 2)


def gather_far(near, first_core):
    return cross_row(jnp.where(first_core, near[0], near[1]), 2, 1)


def gather_pieces(own, near, far):
    return (own, near, swap_core(near), far, swap_core(far))


def flip_tiles(shard, first_core):
    half = shard.shape[0] // 2
    got = flip_col(jnp.where(first_core, shard[:half], shard[half:]))
    return got, swap_core(got)


def join_tiles(shard, got, other, first_core):
    halves = jnp.where(first_core, jnp.stack([got, other]), jnp.stack([other, got]))
    return jnp.stack([shard, halves.reshape(shard.shape)])


def scatter_first(pieces):
    own, near, near_other, far, far_other = pieces
    return own, near, swap_core(near_other), add(far, swap_core(far_other))


def scatter_second(own, near, near_arrived, far, moved, first_core):
    moved = moved.astype(wide_type)
    total = near.astype(wide_type) + near_arrived.astype(wide_type)
    lower = total[0] + jnp.where(first_core, moved, 0.0)
    upper = total[1] + jnp.where(first_core, 0.0, moved)
    return own, jnp.stack([lower, upper]).astype(low_type)


def scatter_third(own, near, first_core):
    own = add(own, cross_row(near, 1, 2))
    half = own.shape[1] // 2
    lower, upper = own[:, :half], own[:, half:]
    arrived = swap_core(jnp.where(first_core, upper, lower))
    return add(jnp.where(first_core, lower, upper), arrived)


def scatter_fourth(part, first_core):
    part = add(part[0], flip_col(part[1]))
    other = swap_core(part)
    halves = jnp.where(first_core, jnp.stack([part, other]), jnp.stack([other, part]))
    return halves.reshape((-1,) + part.shape[1:]).astype(wide_type)


def body(
    states,
    teacher,
    cotangent,
    lengths,
    norm_gain,
    norm_bias,
    in_weight,
    in_bias,
    proj_weight,
    proj_bias,
    up_weight,
    up_bias,
    down_weight,
    down_bias,
):
    col_count = lax.axis_size("col")
    row_count = lax.axis_size("row")
    core_count = lax.axis_size("dp")
    half_group = col_count // 2
    col_index = lax.axis_index("col")
    row_index = lax.axis_index("row")
    core_index = lax.axis_index("dp")
    group_index = col_index // half_group
    first_core = core_index == 0
    token_rows, width = states.shape
    model_width = width * col_count
    seqs = lengths.shape[0] // 2
    rows = token_rows // 2
    slots = rows // seqs
    hidden_width = up_bias.shape[1]
    tiled = row_count == 4 and width == 256 and hidden_width == 1024 and model_width == 1024
    row_width = model_width // row_count
    heads_width = 2 * width
    feed_width = 2 * hidden_width
    in_thirds = jnp.transpose(in_weight, (0, 2, 1, 3))

    def own_half(value):
        return lax.dynamic_slice_in_dim(value, group_index * rows, rows, 0)

    def other_half(value):
        return lax.dynamic_slice_in_dim(value, (1 - group_index) * rows, rows, 0)

    def row_blocks(own, flipped, event):
        blocks = [own, flipped]
        for step in range(1, half_group):
            blocks = blocks + [group_shift(own, step), group_shift(after(flipped, event), step)]
        return blocks

    block_places = []
    for step in range(half_group):
        base = group_index * half_group
        source = base + (col_index - base + half_group - step) % half_group
        block_places = block_places + [source, col_count - 1 - source]

    def share_rows(value, kind=wide_type):
        own = lax.dynamic_slice_in_dim(value, col_index * width, width, 1)
        other = lax.dynamic_slice_in_dim(value, (col_count - 1 - col_index) * width, width, 1)
        received = flip_col(other.astype(kind)).astype(wide_type)
        lower = jnp.where(group_index == 0, own, received)
        upper = jnp.where(group_index == 0, received, own)
        return jnp.concatenate([lower, upper])

    own_lengths = lax.dynamic_slice_in_dim(lengths, group_index * seqs, seqs, 0)
    meta = jnp.concatenate(
        [
            jnp.stack(
                [
                    row_index,
                    row_index ^ (1 + core_index),
                    row_index ^ (2 - core_index),
                    row_index ^ 3,
                    core_index,
                ]
            ),
            own_lengths,
            jnp.stack(block_places),
        ]
    ).astype(jnp.int32)

    in_full, proj_full, up_full, down_full = ([None] * LAYERS for kind in range(4))
    feature_pack = jnp.concatenate(
        [norm_gain.reshape(-1, width), norm_bias.reshape(-1, width), proj_bias, down_bias]
    )
    hidden_pack = jnp.concatenate([in_bias.reshape(-1, width), up_bias.reshape(-1, width)])
    feature_rows = feature_pack.shape[0]
    small = jnp.concatenate([feature_pack, hidden_pack])
    small_flipped = flip_col(small)
    states_own, states_other = own_half(states), other_half(states)
    if tiled:

        def up_tiles(weight):
            return jnp.transpose(weight.reshape(256, 4, 256), (1, 0, 2))

        def down_tiles(weight):
            return weight.reshape(4, 256, 256)

        def attend_tiles(thirds, square):
            return jnp.concatenate([thirds, square[None]])

        count = 6
        shards, flips, owns, nears, fars = ([None] * count for kind in range(5))

        def flip(place, *events):
            layer = place // 3
            if place % 3 == 0:
                thirds, square = in_thirds[layer], proj_weight[layer]
                if events:
                    thirds, square = after(thirds, *events), after(square, *events)
                shards[place] = attend_tiles(thirds, square)
            elif place % 3 == 1:
                shards[place] = up_tiles(after(up_weight[layer], *events))
            else:
                shards[place] = down_tiles(after(down_weight[layer], *events))
            flips[place] = flip_tiles(shards[place], first_core)
            return flips[place][0]

        def near(place, *events):
            owns[place] = join_tiles(shards[place], *flips[place], first_core)
            nears[place] = gather_near(after(owns[place], *events))
            return nears[place]

        def far(place, *events):
            fars[place] = gather_far(after(nears[place], *events), first_core)
            return fars[place]

        def pieces(place):
            return gather_pieces(owns[place], nears[place], fars[place])

        slot = [flip(0)]
        states_flipped = flip_col(after(states_other, *slot))
        slot = [near(0), states_flipped]
        states_blocks = row_blocks(states_own, states_flipped, slot[0])
        slot = [far(0, *slot), flip(1, *slot), *states_blocks[2:]]
        slot = [near(1, *slot), flip(2, *slot)]
        states_blocks[0] = after(states_blocks[0], *slot)
        slot = [far(1, *slot), near(2, *slot), flip(3, *slot)]
        in_full[0], proj_full[0] = (pieces(0), 0), (pieces(0), 3)
    else:

        def both_blocks(shard):
            own = lax.all_gather(shard, "row", axis=0, tiled=False)
            return jnp.stack([own, flip_col(own)])

        for layer in range(LAYERS):
            whole = jnp.transpose(both_blocks(in_thirds[layer]), (2, 1, 3, 0, 4))
            in_full[layer] = ((whole.reshape(3, model_width, heads_width),), 0)
            whole = jnp.transpose(both_blocks(proj_weight[layer]), (0, 2, 1, 3))
            proj_full[layer] = ((whole.reshape(2, width, model_width),), 0)
            whole = both_blocks(up_weight[layer]).reshape(2, model_width, -1, 256)
            whole = jnp.transpose(whole, (0, 2, 1, 3))
            up_full[layer] = ((whole.reshape(-1, model_width, 256),), 0)
            whole = jnp.transpose(both_blocks(down_weight[layer]), (0, 2, 1, 3))
            down_full[layer] = ((whole.reshape(-1, 256, model_width),), 0)
        states_blocks = row_blocks(states_own, flip_col(states_other), states)

    small_pair = jnp.stack([small, small_flipped])
    feature_all = order_blocks(small_pair[:, :feature_rows])
    feature_all = jnp.transpose(feature_all, (1, 0, 2)).reshape(feature_rows, model_width)
    gains = feature_all[: 2 * LAYERS].reshape(LAYERS, 2, 1, model_width)
    shifts = feature_all[2 * LAYERS : 4 * LAYERS].reshape(LAYERS, 2, 1, model_width)
    proj_shift = feature_all[4 * LAYERS : 5 * LAYERS].reshape(LAYERS, 1, model_width)
    down_shift = feature_all[5 * LAYERS :].reshape(LAYERS, 1, model_width)
    hidden_pair = small_pair[:, feature_rows:]
    in_shift = hidden_pair[:, : 2 * LAYERS].reshape(2, LAYERS, 2, width)
    in_shift = jnp.transpose(in_shift, (1, 2, 0, 3)).reshape(LAYERS, 2, 1, heads_width)
    up_shift = hidden_pair[:, 2 * LAYERS :].reshape(2, LAYERS, hidden_width)
    up_shift = jnp.transpose(up_shift, (1, 0, 2)).reshape(LAYERS, 1, feed_width)


    def shape(*dims, kind=wide_type):
        return jax.ShapeDtypeStruct(dims, kind)

    def call(kernel, cost, operands, specs, outs, scratch=()):
        return pl.pallas_call(
            kernel,
            out_shape=outs,
            in_specs=specs,
            out_specs=[VMEM] * len(outs),
            scratch_shapes=list(scratch),
            compiler_params=pltpu.CompilerParams(vmem_limit_bytes=vmem_bytes),
            cost_estimate=pl.CostEstimate(
                flops=int(cost * 1.15e9), bytes_accessed=1024 * 1024, transcendentals=0
            ),
        )(*operands)

    wide_rows = shape(rows, model_width)
    low_rows = shape(rows, model_width, kind=low_type)
    low_heads = shape(rows, heads_width, kind=low_type)
    heads = heads_width // HEAD_DIM
    feed_tiles = feed_width // 256
    attend_scratch = [
        pltpu.VMEM((3, model_width, heads_width), low_type),
        pltpu.VMEM((2, width, model_width), low_type),
    ]
    feed_scratch = [
        pltpu.VMEM((feed_tiles, model_width, 256), low_type),
        pltpu.VMEM((feed_tiles, 256, model_width), low_type),
    ]
    sems = [pltpu.SemaphoreType.DMA((8,)), pltpu.SemaphoreType.DMA((8,))]

    def attend(layer, base, sums):
        first = len(sums) == 0
        params = [gains[layer, 0], shifts[layer, 0], in_shift[layer, 0], in_shift[layer, 1]]
        in_refs, in_offset = in_full[layer]
        proj_refs, proj_offset = proj_full[layer]
        counts = (len(base), len(sums), 4, len(in_refs), len(proj_refs), 9, 4)
        operands = [meta, *base, *sums, *params, *in_refs, *proj_refs]
        specs = [SMEM] + [VMEM] * (4 + len(base) + len(sums)) + [ANY] * (len(in_refs) + len(proj_refs))
        kernel = functools.partial(attend_kernel, first, slots, counts, (in_offset, proj_offset))
        outs = [
            wide_rows,
            low_rows,
            low_heads,
            low_heads,
            low_heads,
            shape(rows, heads),
            low_heads,
            wide_rows,
            low_rows,
        ]
        return call(kernel, 10.5, operands, specs, outs, attend_scratch + sems)

    def feed(layer, base, sums):
        params = [gains[layer, 1], shifts[layer, 1], up_shift[layer]]
        up_refs, up_offset = up_full[layer]
        down_refs, down_offset = down_full[layer]
        counts = (4, 3, len(up_refs), len(down_refs), 6, 4)
        operands = [meta, base, *sums, *params, *up_refs, *down_refs]
        specs = [SMEM] + [VMEM] * 7 + [ANY] * (len(up_refs) + len(down_refs))
        kernel = functools.partial(feed_kernel, counts, (up_offset, down_offset))
        low_feed = shape(rows, feed_width, kind=low_type)
        outs = [wide_rows, low_rows, low_feed, low_feed, wide_rows, low_rows]
        return call(kernel, 12.0, operands, specs, outs, feed_scratch + sems)

    def feed_back(layer, grad, slope):
        up_refs, up_offset = up_full[layer]
        down_refs, down_offset = down_full[layer]
        counts = (2, len(up_refs), len(down_refs), 7, 4)
        operands = [meta, grad, slope, *up_refs, *down_refs]
        specs = [SMEM] + [VMEM] * 2 + [ANY] * (len(up_refs) + len(down_refs))
        kernel = functools.partial(feed_back_kernel, slots, counts, (up_offset, down_offset))
        outs = [
            wide_rows,
            low_rows,
            shape(rows, feed_width, kind=low_type),
            shape(1, model_width),
            shape(1, feed_width),
            wide_rows,
            low_rows,
        ]
        return call(kernel, 10.0, operands, specs, outs, feed_scratch + sems)

    def attend_back(layer, sums, middle, masked, saved):
        in_refs, in_offset = in_full[layer]
        proj_refs, proj_offset = proj_full[layer]
        counts = (4, 1, 4, len(in_refs), len(proj_refs), 9, 5)
        operands = [meta, *sums, middle, masked, gains[layer, 1], *saved, *in_refs, *proj_refs]
        specs = [SMEM] + [VMEM] * 9 + [ANY] * (len(in_refs) + len(proj_refs))
        kernel = functools.partial(attend_back_kernel, slots, counts, (in_offset, proj_offset))
        outs = [
            wide_rows,
            low_rows,
            shape(1, model_width),
            shape(1, model_width),
            shape(1, model_width),
            shape(3, rows, heads_width, kind=low_type),
            shape(2, heads_width),
            wide_rows,
            low_rows,
        ]
        scratch = attend_scratch + [pltpu.VMEM((rows, heads_width), low_type)] + sems
        return call(kernel, 12.0, operands, specs, outs, scratch)

    def weight_tiles(kernel, tiles, cost, *operands):
        outs = [shape(2, tiles, 256, 256, kind=low_type)] * 3
        outs = outs + [shape(tiles, 256, 256, kind=low_type)] * 2
        specs = [SMEM] + [VMEM] * len(operands)
        return call(kernel, cost, (meta,) + operands, specs, outs)

    positions = jnp.arange(slots, dtype=jnp.int32)
    all_mask = (positions[None, :] < lengths[:, None]).reshape(token_rows, 1).astype(wide_type)
    teacher_wide = teacher.astype(wide_type)

    saved = []
    base, sums = states_blocks, ()
    for layer in range(LAYERS):
        if layer > 0:
            sums = (*sums, down_shift[layer - 1])
        current, normed_one, queries, keys, values, lse, mixed, wide, low = attend(
            layer, base, sums
        )
        event = wide
        if layer == 0 and tiled:
            slot = [event, *slot]
            slot = [far(2, *slot), near(3, *slot), flip(4, *slot)]
            up_full[0], down_full[0] = (pieces(1), 0), (pieces(2), 0)
        wide, arrived = group_total(wide, low)
        if layer == 0:
            token_total = butterfly_sum(after(jnp.sum(lengths), event), ("dp", "row"))
            token_total = token_total.astype(wide_type)
            factor = 2.0 * token_rows * core_count * row_count / token_total
            seed_share = cotangent - factor * all_mask * teacher_wide
            seed_own, seed_other = own_half(seed_share), other_half(seed_share)
            if tiled:
                arrived = after(arrived, *slot)
                slot = [far(3, *slot), near(4, *slot), flip(5, *slot)]
            else:
                seed_flipped = flip_col(seed_other)
        else:
            if tiled:
                slot = [event, *slot]
                slot = [far(5, *slot), seed_flipped]
                up_full[1], down_full[1] = (pieces(4), 0), (pieces(5), 0)
                arrived = after(arrived, seed_flipped)
            seed_blocks = row_blocks(after(seed_own, arrived), seed_flipped, arrived)
        middle, normed_two, hidden, slope, wide, low = feed(
            layer, current, (wide, arrived, proj_shift[layer])
        )
        event = wide
        if layer == 1:
            low = after(low, *seed_blocks)
        wide, arrived = group_total(wide, low)
        if layer == 0 and tiled:
            slot = [event, *slot]
            seed_flipped = flip_col(after(seed_other, *slot))
            slot = [far(4, *slot), near(5, *slot)]
            in_full[1], proj_full[1] = (pieces(3), 0), (pieces(3), 3)
        base, sums = [middle], (wide, arrived)
        saved.append(
            (current, normed_one, queries, keys, values, lse, mixed, middle, normed_two, hidden, slope)
        )
    final, grad = call(
        functools.partial(last_kernel, slots),
        4.3,
        (meta, factor.reshape(1), *base, *sums, down_shift[LAYERS - 1], *seed_blocks),
        [SMEM, SMEM] + [VMEM] * (4 + len(seed_blocks)),
        [wide_rows, wide_rows],
    )
    output_share = share_rows(final)
    residue = (output_share - teacher_wide) * all_mask
    squared = jnp.sum(residue * residue)

    feature_grads = {}
    hidden_grads = {}
    in_grads, proj_grads, up_grads, down_grads = ([None] * LAYERS for kind in range(4))

    def keep_feed(layer, tiles):
        up_grads[layer] = jnp.transpose(tiles[:4], (1, 0, 2)).reshape(256, 1024)
        down_grads[layer] = tiles[4:].reshape(1024, 256)

    def keep_attend(layer, tiles):
        in_grads[layer] = tiles[:3]
        proj_grads[layer] = tiles[3]

    def before_swap(low):
        for item in under_way:
            if item[0] == 1:
                item[0] = 2
                item[1] = item[1] + (cross_row(item[1][3], 2, 1),)
                low = after(low, item[1][4])
        return low

    def beside_swap(arrived, pieces, keep):
        value = scatter_first(pieces)
        events = [*pieces, *value]
        for item in under_way:
            if item[0] == 2:
                item[1] = scatter_second(*item[1], first_core)
                events.append(item[1][1])
            elif item[0] == 3:
                item[1] = scatter_third(*item[1], first_core)
                events.append(item[1])
            elif item[0] == 4:
                item[1] = scatter_fourth(item[1], first_core)
                events.append(item[1])
                item[2](item[1])
            item[0] += 1
        under_way.append([1, value, keep])
        return after(arrived, *events)

    under_way = []
    for layer in reversed(range(LAYERS)):
        current, normed_one, queries, keys, values, lse, mixed, middle, normed_two, hidden, slope = (
            saved[layer]
        )
        masked, masked_low, pre, down_bias_part, up_bias_part, wide, low = feed_back(
            layer, grad, slope
        )
        if tiled:
            low = before_swap(low)
        wide, arrived = group_total(wide, low)
        if tiled:
            if layer == LAYERS - 1:
                arrived = after(arrived, output_share)
            pieces = weight_tiles(
                feed_weight_kernel, 8, 9.0, normed_two, pre, hidden, masked_low
            )
            arrived = beside_swap(arrived, pieces, functools.partial(keep_feed, layer))
        (
            grad,
            grad_low,
            gain_two,
            shift_two,
            proj_bias_part,
            triple,
            in_bias_part,
            wide,
            low,
        ) = attend_back(layer, (wide, arrived), middle, masked, (queries, keys, values, lse))
        if tiled:
            low = before_swap(low)
        wide, arrived = group_total(wide, low)
        if tiled:
            pieces = weight_tiles(
                attend_weight_kernel, 4, 5.5, normed_one, triple, mixed, grad_low
            )
            arrived = beside_swap(arrived, pieces, functools.partial(keep_attend, layer))
        else:

            def product(spec, left, right):
                return jnp.einsum(spec, left, right, preferred_element_type=wide_type)

            def own_block(blocks):
                part = lax.psum_scatter(
                    blocks.astype(low_type), "row", scatter_dimension=1, tiled=False
                )
                mine = add(part[0], flip_col(part[1]))
                return mine.astype(wide_type) + swap_core(mine).astype(wide_type)

            def by_row(value):
                return value.reshape(rows, row_count, row_width)

            def by_block(value):
                return value.reshape(value.shape[:-1] + (2, -1))

            in_grads[layer] = own_block(
                product("trd,ptbe->brpde", by_row(normed_one), by_block(triple))
            )
            proj_grads[layer] = own_block(
                product("tbe,trd->bred", by_block(mixed), by_row(grad_low))
            )
            up_grads[layer] = own_block(product("trd,tbe->brde", by_row(normed_two), by_block(pre)))
            down_grads[layer] = own_block(
                product("tbe,trd->bred", by_block(hidden), by_row(masked_low))
            )
        grad, gain_one, shift_one = call(
            pull_kernel,
            4.3,
            (current, gains[layer, 0], grad, wide, arrived),
            [VMEM] * 5,
            [wide_rows, shape(1, model_width), shape(1, model_width)],
        )
        feature_grads[layer] = (
            gain_one,
            gain_two,
            shift_one,
            shift_two,
            proj_bias_part,
            down_bias_part,
        )
        hidden_grads[layer] = jnp.concatenate(
            [
                jnp.transpose(in_bias_part.reshape(2, 2, width), (1, 0, 2)),
                up_bias_part.reshape(2, -1, width),
            ],
            axis=1,
        )

    for step, value, saver in under_way:
        if step <= 1:
            value = value + (cross_row(value[3], 2, 1),)
        if step <= 2:
            value = scatter_second(*value, first_core)
        if step <= 3:
            value = scatter_third(*value, first_core)
        if step <= 4:
            saver(scatter_fourth(value, first_core))
    input_share = share_rows(grad, low_type)

    feature_parts = jnp.concatenate(
        [part for layer in range(LAYERS) for part in feature_grads[layer]]
    )
    feature_parts = feature_parts.reshape(-1, col_count, width)
    own_parts = lax.dynamic_index_in_dim(feature_parts, col_index, 1, False)
    other_parts = lax.dynamic_index_in_dim(feature_parts, col_count - 1 - col_index, 1, False)
    hidden_parts = jnp.concatenate([hidden_grads[layer] for layer in range(LAYERS)], axis=1)
    extra = jnp.zeros((1, width), wide_type).at[0, 0].set(squared)
    packed = jnp.concatenate(
        [jnp.stack([own_parts, other_parts]), hidden_parts, jnp.stack([extra, extra])], axis=1
    )
    packed = butterfly_sum(packed, ("dp", "row"))
    vectors = packed[0] + flip_col(packed[1])
    squared_total = butterfly_sum(packed[0, -1, 0], ("col",))
    loss_value = squared_total / (token_total * model_width)
    per_layer = len(feature_grads[0])
    features = vectors[: LAYERS * per_layer].reshape(LAYERS, per_layer, width)
    hiddens = vectors[LAYERS * per_layer : -1].reshape(LAYERS, -1, width)
    return (
        loss_value,
        output_share,
        input_share,
        features[:, 0:2],
        features[:, 2:4],
        jnp.transpose(jnp.stack(in_grads), (0, 2, 1, 3)),
        hiddens[:, 0:2],
        jnp.stack(proj_grads),
        features[:, 4],
        jnp.stack(up_grads),
        hiddens[:, 2:].reshape(LAYERS, hidden_width),
        jnp.stack(down_grads),
        features[:, 5],
    )


def solution(mesh):
    in_specs = (
        P(("dp", "row"), "col"),
        P(("dp", "row"), "col"),
        P(("dp", "row"), "col"),
        P(("dp", "row")),
        P(None, None, "col"),
        P(None, None, "col"),
        P(None, "row", None, "col"),
        P(None, None, "col"),
        P(None, "col", "row"),
        P(None, "col"),
        P(None, "row", "col"),
        P(None, "col"),
        P(None, "col", "row"),
        P(None, "col"),
    )
    out_specs = (
        P(),
        P(("dp", "row"), "col"),
        P(("dp", "row"), "col"),
        P(None, None, "col"),
        P(None, None, "col"),
        P(None, "row", None, "col"),
        P(None, None, "col"),
        P(None, "col", "row"),
        P(None, "col"),
        P(None, "row", "col"),
        P(None, "col"),
        P(None, "col", "row"),
        P(None, "col"),
    )
    return jax.shard_map(body, mesh=mesh, in_specs=in_specs, out_specs=out_specs, check_vma=False)
```

time: 720 us -> 566 us (0.79)
  the two profiles are of different devices: /device:TPU:1 before, /device:TPU:9 now
where the time goes in v2:
time: 566 us; the launch traced here: 556 us
  waiting for transfers between devices  204 us (36%)
  Pallas kernels  131 us (23%)
  starting transfers between devices  109 us (19%)
  other arithmetic  65.7 us (12%)
  local copies, waits for them, and re-layouts  37.3 us (7%)
  between operations  9.57 us (2%)
    pallas_call x15, Pallas kernels, call(): pl.pallas_call(kernel, out_shape=outs, in_specs=specs, out_specs=[VMEM] *...  131 us
    ppermute x16, waiting for transfers between devices, flip_col(): lax.ppermute(value, 'col', [(i, count - 1 - i) for i in range(count)])  123 us
    ppermute x13, waiting for transfers between devices, group_shift(): return lax.ppermute(value, 'col', pairs)  41.2 us
    ppermute x34, starting transfers between devices, swap_core(): return lax.ppermute(value, 'dp', [(i, count - 1 - i) for i in range(count)])  39.7 us
    ppermute x8, waiting for transfers between devices, butterfly_sum(): lax.ppermute(value, axis, [(i, i ^ step) for i in range(count)])  23 us
    ppermute x13, starting transfers between devices, group_shift(): return lax.ppermute(value, 'col', pairs)  19.9 us
    ppermute x20, starting transfers between devices, cross_row(): return lax.ppermute(value, ('dp', 'row', 'col'), pairs)  18.5 us
    convert_element_type x16, other arithmetic, add(): return (left.astype(wide_type) + right.astype(wide_type)).astype(low_type)  16.3 us
  transfers between devices with their start and end apart: 91, of which 33 were waited for; matrix products, arithmetic and copies ran while one was open for 15% of the time, Pallas kernels for 19%

profile of v2, /device:TPU:9, one launch (start us, length us, event | category | flops | bytes accessed | tf_op | source)
XLA Modules:
  0.0 555.6 jit_solution(6333968906835124072)
XLA Ops:
  8.5 8.6 %collective-permute-done = bf16[2,256,256]{2,1,0:T(8,128)(2,1)S(1)} collective-permute-done((bf16[2,256,256]{2,1,0:T(8,128)(2,1)S(1)}, bf16[2,256,256]{2,1,0:T(8,128)(2,1)S(1)}, u32[]{:S(2)}, u32[]{:S(2)}) %collective-permute-start) | collective-permute-done | bytes 262176 | tf_op jit(solution)/shard_map/ppermute | solution.py:400
  28.9 18.7 %collective-permute-done.3.refs_1_ = f32[320,256]{1,0:T(8,128)S(1)} collective-permute-done((f32[320,256]{1,0:T(8,128)}, f32[320,256]{1,0:T(8,128)S(1)}, u32[]{:S(2)}, u32[]{:S(2)}) %collective-permute-start.3) | collective-permute-done | bytes 327712 | tf_op jit(solution)/shard_map/ppermute | solution.py:400
  54.7 3.3 collective-permute-done.4
  63.4 6.5 %collective-permute-done.8.refs_3_ = f32[320,256]{1,0:T(8,128)S(1)} collective-permute-done((f32[320,256]{1,0:T(8,128)}, f32[320,256]{1,0:T(8,128)S(1)}, u32[]{:S(2)}, u32[]{:S(2)}) %collective-permute-start.8) | collective-permute-done | bytes 327712 | tf_op jit(solution)/shard_map/ppermute | solution.py:412
  71.9 2.5 collective-permute-start.13
  74.4 9.0 %collective-permute-done.10 = bf16[2,256,256]{2,1,0:T(8,128)(2,1)S(1)} collective-permute-done((bf16[2,256,256]{2,1,0:T(8,128)(2,1)S(1)}, bf16[2,256,256]{2,1,0:T(8,128)(2,1)S(1)}, u32[]{:S(2)}, u32[]{:S(2)}) %collective-permute-start.10) | collective-permute-done | bytes 262176 | tf_op jit(solution)/shard_map/ppermute | solution.py:400
  92.4 10.5 %shard_map.237 = (f32[320,1024]{1,0:T(8,128)}, bf16[320,1024]{1,0:T(8,128)(2,1)}, bf16[320,512]{1,0:T(8,128)(2,1)}, bf16[320,512]{1,0:T(8,128)(2,1)}, bf16[320,5...) custom-call(s32[10]{0:T(128)} %concatenate.26.meta, ...), custom_call_target="tpu_custom_call" | custom-call | flops 12074999808 | bytes 1048576 | tf_op jit(solution)/shard_map/pallas_call | solution.py:692
  113.3 7.5 %collective-permute-done.23 = bf16[2,256,256]{2,1,0:T(8,128)(2,1)S(1)} collective-permute-done((bf16[2,256,256]{2,1,0:T(8,128)(2,1)}, bf16[2,256,256]{2,1,0:T(8,128)(2,1)S(1)}, u32[]{:S(2)}, u32[]{:S(2)}) %collective-permute-start.23) | collective-permute-done | bytes 262176 | tf_op jit(solution)/shard_map/ppermute | solution.py:400
  131.6 2.3 collective-permute-start.26
  138.7 2.9 collective-permute-start.25
  148.1 6.7 %collective-permute-done.38 = bf16[2,256,256]{2,1,0:T(8,128)(2,1)S(1)} collective-permute-done((bf16[2,256,256]{2,1,0:T(8,128)(2,1)S(1)}, bf16[2,256,256]{2,1,0:T(8,128)(2,1)S(1)}, u32[]{:S(2)}, u32[]{:S(2)}) %collective-permute-start.38) | collective-permute-done | bytes 262176 | tf_op jit(solution)/shard_map/ppermute | solution.py:400
  156.1 12.1 %shard_map.238 = (f32[320,1024]{1,0:T(8,128)}, bf16[320,1024]{1,0:T(8,128)(2,1)}, bf16[320,2048]{1,0:T(8,128)(2,1)}, bf16[320,2048]{1,0:T(8,128)(2,1)}, f32[320,1024]{1,0:T(8,128)}, /*index=5*/bf16[320,1024]{1,0:T(8,128)(2,1)}) custom-call(s32[10]{0:T(128)} %concatenate.26.meta, f32[320,1024]{1,0:T(8,128)} %get-tuple-element.157.refs_0_.inputs, ...), custom_call_target="tpu_custom_call" | custom-call | flops 13799999488 | bytes 1048576 | tf_op jit(solution)/shard_map/pallas_call | solution.py:692
  172.9 12.0 %collective-permute-done.28.refs_2_ = bf16[320,1024]{1,0:T(8,128)(2,1)} collective-permute-done((bf16[320,1024]{1,0:T(8,128)(2,1)}, bf16[320,1024]{1,0:T(8,128)(2,1)}, u32[]{:S(2)}, u32[]{:S(2)}) %collective-permute-start.28) | collective-permute-done | bytes 655392 | tf_op jit(solution)/shard_map/ppermute | solution.py:412
  186.5 11.1 %shard_map.239 = (f32[320,1024]{1,0:T(8,128)}, bf16[320,1024]{1,0:T(8,128)(2,1)}, bf16[320,512]{1,0:T(8,128)(2,1)}, bf16[320,512]{1,0:T(8,128)(2,1)}, bf16[320,5...) custom-call(s32[10]{0:T(128)} %concatenate.26.meta, ...), custom_call_target="tpu_custom_call" | custom-call | flops 12074999808 | bytes 1048576 | tf_op jit(solution)/shard_map/pallas_call | solution.py:692
  201.4 14.5 %collective-permute-done.39.refs_1_ = f32[320,256]{1,0:T(8,128)} collective-permute-done((f32[320,256]{1,0:T(8,128)S(1)}, f32[320,256]{1,0:T(8,128)}, u32[]{:S(2)}, u32[]{:S(2)}) %collective-permute-start.39) | collective-permute-done | bytes 327712 | tf_op jit(solution)/shard_map/ppermute | solution.py:400
  217.7 5.1 collective-permute-done.35.refs_2_
  226.7 11.9 %shard_map.240 = (f32[320,1024]{1,0:T(8,128)}, bf16[320,1024]{1,0:T(8,128)(2,1)}, bf16[320,2048]{1,0:T(8,128)(2,1)}, bf16[320,2048]{1,0:T(8,128)(2,1)}, f32[320,1024]{1,0:T(8,128)}, /*index=5*/bf16[320,1024]{1,0:T(8,128)(2,1)}) custom-call(s32[10]{0:T(128)} %concatenate.26.meta, f32[320,1024]{1,0:T(8,128)} %get-tuple-element.172.refs_0_.inputs, ...), custom_call_target="tpu_custom_call" | custom-call | flops 13799999488 | bytes 1048576 | tf_op jit(solution)/shard_map/pallas_call | solution.py:692
  241.3 12.9 %collective-permute-done.50.arrived = bf16[320,1024]{1,0:T(8,128)(2,1)S(1)} collective-permute-done((bf16[320,1024]{1,0:T(8,128)(2,1)}, bf16[320,1024]{1,0:T(8,128)(2,1)S(1)}, u32[]{:S(2)}, u32[]{:S(2)}) %collective-permute-start.50) | collective-permute-done | bytes 655392 | tf_op jit(solution)/shard_map/ppermute | solution.py:412
  255.1 4.4 shard_map.241
  259.5 9.8 %shard_map.242 = (f32[320,1024]{1,0:T(8,128)}, bf16[320,1024]{1,0:T(8,128)(2,1)}, bf16[320,2048]{1,0:T(8,128)(2,1)}, f32[1,1024]{1,0:T(1,128)}, f32[1,2048]{1,0:...) custom-call(s32[10]{0:T(128)} %concatenate.26.meta, f32[320,1024]{1,0:T(8,128)} %get-tuple-element.189.refs_0_, ...), custom_call_target="tpu_custom_call" | custom-call | flops 11500000256 | bytes 1048576 | tf_op jit(solution)/shard_map/pallas_call | solution.py:692
  269.2 8.9 %shard_map.243 = (bf16[2,8,256,256]{3,2,1,0:T(8,128)(2,1)}, bf16[2,8,256,256]{3,2,1,0:T(8,128)(2,1)}, bf16[2,8,256,256]{3,2,1,0:T(8,128)(2,1)}, bf16[8,256,256]{2,1,0:T(8,128)(2,1)}, bf16[8,256,256]{2,1,0:T(8,128)(2,1)}) custom-call(s32[10]{0:T(128)} %concatenate.26.meta, bf16[320,1024]{1,0:T(8,128)(2,1)} %get-tuple-element.195.normed, ...), custom_call_target="tpu_custom_call" | custom-call | flops 10350000128 | bytes 1048576 | tf_op jit(solution)/shard_map/pallas_call | solution.py:692
  278.2 2.8 collective-permute-start.53
  282.8 2.4 collective-permute-start.51
  287.2 11.7 %collective-permute-done.52 = f32[320,256]{1,0:T(8,128)} collective-permute-done((f32[320,256]{1,0:T(8,128)}, f32[320,256]{1,0:T(8,128)}, u32[]{:S(2)}, u32[]{:S(2)}) %collective-permute-start.52) | collective-permute-done | bytes 327712 | tf_op jit(solution)/shard_map/ppermute | solution.py:400
  302.9 4.1 collective-permute-done.51.refs_1_
  310.2 11.7 %shard_map.244 = (f32[320,1024]{1,0:T(8,128)}, bf16[320,1024]{1,0:T(8,128)(2,1)}, f32[1,1024]{1,0:T(1,128)}, f32[1,1024]{1,0:T(1,128)}, f32[1,1024]{1,0:T(1,128)...) custom-call(s32[10]{0:T(128)} %concatenate.26.meta, ...), custom_call_target="tpu_custom_call" | custom-call | flops 13799999488 | bytes 1048576 | tf_op jit(solution)/shard_map/pallas_call | solution.py:692
  323.9 5.6 shard_map.245
  329.4 2.5 collective-permute-start.57
  338.6 4.5 shard_map.246
  343.1 7.5 %collective-permute-done.59 = bf16[4,256,256]{2,1,0:T(8,128)(2,1)S(1)} collective-permute-done((bf16[4,256,256]{2,1,0:T(8,128)(2,1)S(1)}, bf16[4,256,256]{2,1,0:T(8,128)(2,1)S(1)}, u32[]{:S(2)}, u32[]{:S(2)}) %collective-permute-start.59) | collective-permute-done | bytes 524320 | tf_op jit(solution)/shard_map/ppermute | solution.py:424
  352.6 9.8 %shard_map.247 = (f32[320,1024]{1,0:T(8,128)}, bf16[320,1024]{1,0:T(8,128)(2,1)}, bf16[320,2048]{1,0:T(8,128)(2,1)}, f32[1,1024]{1,0:T(1,128)}, f32[1,2048]{1,0:...) custom-call(s32[10]{0:T(128)} %concatenate.26.meta, f32[320,1024]{1,0:T(8,128)} %get-tuple-element.224.refs_0_, ...), custom_call_target="tpu_custom_call" | custom-call | flops 11500000256 | bytes 1048576 | tf_op jit(solution)/shard_map/pallas_call | solution.py:692
  362.4 8.9 %shard_map.248 = (bf16[2,8,256,256]{3,2,1,0:T(8,128)(2,1)}, bf16[2,8,256,256]{3,2,1,0:T(8,128)(2,1)}, bf16[2,8,256,256]{3,2,1,0:T(8,128)(2,1)}, bf16[8,256,256]{2,1,0:T(8,128)(2,1)}, bf16[8,256,256]{2,1,0:T(8,128)(2,1)}) custom-call(s32[10]{0:T(128)} %concatenate.26.meta, bf16[320,1024]{1,0:T(8,128)(2,1)} %get-tuple-element.229.normed, ...), custom_call_target="tpu_custom_call" | custom-call | flops 10350000128 | bytes 1048576 | tf_op jit(solution)/shard_map/pallas_call | solution.py:692
  384.2 5.0 collective-permute-done.83
  393.0 11.9 %shard_map.249 = (f32[320,1024]{1,0:T(8,128)}, bf16[320,1024]{1,0:T(8,128)(2,1)}, f32[1,1024]{1,0:T(1,128)}, f32[1,1024]{1,0:T(1,128)}, f32[1,1024]{1,0:T(1,128)...) custom-call(s32[10]{0:T(128)} %concatenate.26.meta, ...), custom_call_target="tpu_custom_call" | custom-call | flops 13799999488 | bytes 1048576 | tf_op jit(solution)/shard_map/pallas_call | solution.py:692
  404.9 5.3 shard_map.250
  412.3 8.6 %collective-permute-start.66 = (bf16[320,1024]{1,0:T(8,128)(2,1)}, bf16[320,1024]{1,0:T(8,128)(2,1)}, u32[]{:S(2)}, u32[]{:S(2)}) collective-permute-start(bf16[320,1024]{1,0:T(8,128)(2,1)} %get-tuple-element.247), channel_id=1, source_target_pairs={{0,1},{1,0},{2,3},{3,2},{4,5},{5,4},{6,7},{7,6},{8,9},{9,8},{10,11... | collective-permute-start | bytes 1966088 | tf_op jit(solution)/shard_map/ppermute | solution.py:412
  422.1 2.7 fusion.17
  424.9 2.8 pad_maximum_fusion.1
  430.3 5.2 collective-permute-done.89
  437.7 4.4 shard_map.251
  449.2 2.7 collective-permute-done.72
  454.7 15.9 %collective-permute-done.73 = f32[2,25,256]{2,0,1:T(2,128)} collective-permute-done((f32[2,25,256]{2,0,1:T(2,128)S(1)}, f32[2,25,256]{2,0,1:T(2,128)}, u32[]{:S(2)}, u32[]{:S(2)}) %collective-permute-start.73) | collective-permute-done | bytes 51232 | tf_op jit(solution)/shard_map/ppermute | solution.py:439
  471.9 6.5 %collective-permute-start.74 = (f32[]{:T(128)}, f32[]{:T(128)}, u32[]{:S(2)}, u32[]{:S(2)}) collective-permute-start(f32[]{:T(128)} %bitcast.96), channel_id=1, source_target_pairs={{0,1},{1,0},{2,3},{3,2},{4,5},{5,4},{6,7},{7,6},{8,9},{9,8},{10,11... | collective-permute-start | bytes 20 | tf_op jit(solution)/shard_map/ppermute | solution.py:439
  481.0 2.5 collective-permute-start.75
  488.8 7.6 %collective-permute-start.80 = (bf16[2,2,256,256]{3,2,1,0:T(8,128)(2,1)S(1)}, bf16[2,2,256,256]{3,2,1,0:T(8,128)(2,1)S(1)}, u32[]{:S(2)}, u32[]{:S(2)}) collective-permute-start(bf16[2,2,256,256]{3,2,1,0:T(8,128)(2,1)S(1)} %broadcast_select_fusion.2), channel_id=1, source_target_pairs={{0,16},{16,0},{1,17},{17,1},{2,18},{18,2},{3,19},{19,3},{4,20},{20... | collective-permute-start | bytes 1572872 | tf_op jit(solution)/shard_map/ppermute | solution.py:405
  504.4 10.5 %collective-permute-done.81 = bf16[2,256,256]{2,1,0:T(8,128)(2,1)S(1)} collective-permute-done((bf16[2,256,256]{2,1,0:T(8,128)(2,1)}, bf16[2,256,256]{2,1,0:T(8,128)(2,1)S(1)}, u32[]{:S(2)}, u32[]{:S(2)}) %collective-permute-start.81) | collective-permute-done | bytes 262176 | tf_op jit(solution)/shard_map/ppermute | solution.py:400
  520.3 22.4 %collective-permute-done.87 = bf16[4,256,256]{2,1,0:T(8,128)(2,1)S(1)} collective-permute-done((bf16[4,256,256]{2,1,0:T(8,128)(2,1)S(1)}, bf16[4,256,256]{2,1,0:T(8,128)(2,1)S(1)}, u32[]{:S(2)}, u32[]{:S(2)}) %collective-permute-start.87) | collective-permute-done | bytes 524320 | tf_op jit(solution)/shard_map/ppermute | solution.py:400
  551.4 2.7 pad_maximum_fusion.3
  (461 shorter events, 176.9 us)
Async XLA Ops:
  6.1 57.3 %collective-permute-start.7 = (f32[320,256]{1,0:T(8,128)S(1)}, f32[320,256]{1,0:T(8,128)}, u32[]{:S(2)}, u32[]{:S(2)}) collective-permute-start(f32[320,256]{1,0:T(8,128)S(1)} %get-tuple-element.156.refs_0_), channel_id=1, source_target_pairs={{0,1},{1,0},{2,3},{3,2},{4,5},{5,4},{6,7},{7,6},{8,9},{9,8},{10,11... | collective-permute-start | bytes 983048 | tf_op jit(solution)/shard_map/ppermute | solution.py:412
  8.4 19.9 %collective-permute-start.11 = (f32[24,256]{1,0:T(8,128)S(1)}, f32[24,256]{1,0:T(8,128)S(1)}, u32[]{:S(2)}, u32[]{:S(2)}) collective-permute-start(f32[24,256]{1,0:T(8,128)S(1)} %concatenate.28), channel_id=1, source_target_pairs={{0,3},{1,2},{2,1},{3,0},{4,7},{5,6},{6,5},{7,4},{8,11},{9,10},{10,... | collective-permute-start | bytes 73736 | tf_op jit(solution)/shard_map/ppermute | solution.py:400
  20.9 26.7 %collective-permute-start.2 = (bf16[2,4,256,256]{3,2,1,0:T(8,128)(2,1)}, bf16[2,4,256,256]{3,2,1,0:T(8,128)(2,1)}, u32[]{:S(2)}, u32[]{:S(2)}) collective-permute-start(bf16[2,4,256,256]{3,2,1,0:T(8,128)(2,1)} %pad_maximum_fusion.4.refs_8_.refs_13_.refs_9_.refs_14_), channel_id=1, source_target_pairs={{0,4},{1,5},{2,6},{3,7},{4,0},{5,1},{6,2},{7,3},{8,12},{9,13},{10,... | collective-permute-start | bytes 3145736 | tf_op jit(solution)/shard_map/ppermute | solution.py:424
  27.0 20.7 %collective-permute-start.3 = (f32[320,256]{1,0:T(8,128)}, f32[320,256]{1,0:T(8,128)S(1)}, u32[]{:S(2)}, u32[]{:S(2)}) collective-permute-start(f32[320,256]{1,0:T(8,128)} %get-tuple-element.150), channel_id=1, source_target_pairs={{0,3},{1,2},{2,1},{3,0},{4,7},{5,6},{6,5},{7,4},{8,11},{9,10},{10,... | collective-permute-start | bytes 983048 | tf_op jit(solution)/shard_map/ppermute | solution.py:400
  53.3 16.6 %collective-permute-start.6 = (bf16[4,256,256]{2,1,0:T(8,128)(2,1)S(1)}, bf16[4,256,256]{2,1,0:T(8,128)(2,1)S(1)}, u32[]{:S(2)}, u32[]{:S(2)}) collective-permute-start(bf16[4,256,256]{2,1,0:T(8,128)(2,1)S(1)} %select_bitcast_fusion.5), channel_id=1, source_target_pairs={{0,8},{1,9},{2,10},{3,11},{4,12},{5,13},{6,14},{7,15},{8,0},{9,1},... | collective-permute-start | bytes 1572872 | tf_op jit(solution)/shard_map/ppermute | solution.py:424
  69.9 16.2 %collective-permute-start.9 = (bf16[2,4,256,256]{3,2,1,0:T(8,128)(2,1)}, bf16[2,4,256,256]{3,2,1,0:T(8,128)(2,1)}, u32[]{:S(2)}, u32[]{:S(2)}) collective-permute-start(bf16[2,4,256,256]{3,2,1,0:T(8,128)(2,1)} %pad_maximum_fusion.5.refs_7_.refs_2_), channel_id=1, source_target_pairs={{0,4},{1,5},{2,6},{3,7},{4,0},{5,1},{6,2},{7,3},{8,12},{9,13},{10,... | collective-permute-start | bytes 3145736 | tf_op jit(solution)/shard_map/ppermute | solution.py:424
  71.9 19.7 %collective-permute-start.13 = (bf16[2,4,256,256]{3,2,1,0:T(8,128)(2,1)}, bf16[2,4,256,256]{3,2,1,0:T(8,128)(2,1)}, u32[]{:S(2)}, u32[]{:S(2)}) collective-permute-start(bf16[2,4,256,256]{3,2,1,0:T(8,128)(2,1)} %collective-permute-done.2.refs_9_.refs_14_.refs_10_.refs_15_), channel_id=1, source_target_pairs={{0,16},{16,0},{1,17},{17,1},{2,18},{18,2},{3,19},{19,3},{4,20},{20... | collective-permute-start | bytes 3145736 | tf_op jit(solution)/shard_map/ppermute | solution.py:405
  86.1 19.6 %collective-permute-start.17 = (bf16[2,4,256,256]{3,2,1,0:T(8,128)(2,1)S(1)}, bf16[2,4,256,256]{3,2,1,0:T(8,128)(2,1)S(1)}, u32[]{:S(2)}, u32[]{:S(2)}) collective-permute-start(bf16[2,4,256,256]{3,2,1,0:T(8,128)(2,1)S(1)} %pad_maximum_fusion.6.refs_12_.refs_7_), channel_id=1, source_target_pairs={{0,4},{1,5},{2,6},{3,7},{4,0},{5,1},{6,2},{7,3},{8,12},{9,13},{10,... | collective-permute-start | bytes 3145736 | tf_op jit(solution)/shard_map/ppermute | solution.py:424
  88.7 15.7 %collective-permute-start.18 = (bf16[4,256,256]{2,1,0:T(8,128)(2,1)S(1)}, bf16[4,256,256]{2,1,0:T(8,128)(2,1)S(1)}, u32[]{:S(2)}, u32[]{:S(2)}) collective-permute-start(bf16[4,256,256]{2,1,0:T(8,128)(2,1)S(1)} %select_bitcast_fusion.4), channel_id=1, source_target_pairs={{0,8},{1,9},{2,10},{3,11},{4,12},{5,13},{6,14},{7,15},{8,0},{9,1},... | collective-permute-start | bytes 1572872 | tf_op jit(solution)/shard_map/ppermute | solution.py:424
  111.4 30.2 %collective-permute-start.22 = (bf16[2,4,256,256]{3,2,1,0:T(8,128)(2,1)}, bf16[2,4,256,256]{3,2,1,0:T(8,128)(2,1)}, u32[]{:S(2)}, u32[]{:S(2)}) collective-permute-start(bf16[2,4,256,256]{3,2,1,0:T(8,128)(2,1)} %pad_maximum_fusion.7.refs_8_.refs_13_.refs_9_.refs_14_), channel_id=1, source_target_pairs={{0,4},{1,5},{2,6},{3,7},{4,0},{5,1},{6,2},{7,3},{8,12},{9,13},{10,... | collective-permute-start | bytes 3145736 | tf_op jit(solution)/shard_map/ppermute | solution.py:424
  121.2 20.5 %collective-permute-start.15 = (bf16[320,1024]{1,0:T(8,128)(2,1)}, bf16[320,1024]{1,0:T(8,128)(2,1)}, u32[]{:S(2)}, u32[]{:S(2)}) collective-permute-start(bf16[320,1024]{1,0:T(8,128)(2,1)} %get-tuple-element.159), channel_id=1, source_target_pairs={{0,1},{1,0},{2,3},{3,2},{4,5},{5,4},{6,7},{7,6},{8,9},{9,8},{10,11... | collective-permute-start | bytes 1966088 | tf_op jit(solution)/shard_map/ppermute | solution.py:412
  121.5 25.1 %collective-permute-start.24 = (bf16[2,4,256,256]{3,2,1,0:T(8,128)(2,1)}, bf16[2,4,256,256]{3,2,1,0:T(8,128)(2,1)}, u32[]{:S(2)}, u32[]{:S(2)}) collective-permute-start(bf16[2,4,256,256]{3,2,1,0:T(8,128)(2,1)} %collective-permute-done.9.refs_8_.refs_3_), channel_id=1, source_target_pairs={{0,16},{16,0},{1,17},{17,1},{2,18},{18,2},{3,19},{19,3},{4,20},{20... | collective-permute-start | bytes 3145736 | tf_op jit(solution)/shard_map/ppermute | solution.py:405
  131.6 24.5 %collective-permute-start.26 = (bf16[2,4,256,256]{3,2,1,0:T(8,128)(2,1)S(1)}, bf16[2,4,256,256]{3,2,1,0:T(8,128)(2,1)}, u32[]{:S(2)}, u32[]{:S(2)}) collective-permute-start(bf16[2,4,256,256]{3,2,1,0:T(8,128)(2,1)S(1)} %copy-done.16), channel_id=1, source_target_pairs={{0,16},{16,0},{1,17},{17,1},{2,18},{18,2},{3,19},{19,3},{4,20},{20... | collective-permute-start | bytes 3145736 | tf_op jit(solution)/shard_map/ppermute | solution.py:405
  145.2 23.1 %collective-permute-start.30 = (bf16[4,256,256]{2,1,0:T(8,128)(2,1)S(1)}, bf16[4,256,256]{2,1,0:T(8,128)(2,1)}, u32[]{:S(2)}, u32[]{:S(2)}) collective-permute-start(bf16[4,256,256]{2,1,0:T(8,128)(2,1)S(1)} %select_bitcast_fusion.2), channel_id=1, source_target_pairs={{0,8},{1,9},{2,10},{3,11},{4,12},{5,13},{6,14},{7,15},{8,0},{9,1},... | collective-permute-start | bytes 1572872 | tf_op jit(solution)/shard_map/ppermute | solution.py:424
  146.5 22.2 %collective-permute-start.37 = (bf16[2,4,256,256]{3,2,1,0:T(8,128)(2,1)}, bf16[2,4,256,256]{3,2,1,0:T(8,128)(2,1)}, u32[]{:S(2)}, u32[]{:S(2)}) collective-permute-start(bf16[2,4,256,256]{3,2,1,0:T(8,128)(2,1)} %pad_maximum_fusion.8.refs_7_.refs_2_), channel_id=1, source_target_pairs={{0,4},{1,5},{2,6},{3,7},{4,0},{5,1},{6,2},{7,3},{8,12},{9,13},{10,... | collective-permute-start | bytes 3145736 | tf_op jit(solution)/shard_map/ppermute | solution.py:424
  146.8 38.9 %collective-permute-start.29 = (bf16[2,4,256,256]{3,2,1,0:T(8,128)(2,1)}, bf16[2,4,256,256]{3,2,1,0:T(8,128)(2,1)}, u32[]{:S(2)}, u32[]{:S(2)}) collective-permute-start(bf16[2,4,256,256]{3,2,1,0:T(8,128)(2,1)} %collective-permute-done.22.refs_9_.refs_14_.refs_10_.refs_15_), channel_id=1, source_target_pairs={{0,16},{16,0},{1,17},{17,1},{2,18},{18,2},{3,19},{19,3},{4,20},{20... | collective-permute-start | bytes 3145736 | tf_op jit(solution)/shard_map/ppermute | solution.py:405
  168.2 16.7 %collective-permute-start.28 = (bf16[320,1024]{1,0:T(8,128)(2,1)}, bf16[320,1024]{1,0:T(8,128)(2,1)}, u32[]{:S(2)}, u32[]{:S(2)}) collective-permute-start(bf16[320,1024]{1,0:T(8,128)(2,1)} %get-tuple-element.170), channel_id=1, source_target_pairs={{0,1},{1,0},{2,3},{3,2},{4,5},{5,4},{6,7},{7,6},{8,9},{9,8},{10,11... | collective-permute-start | bytes 1966088 | tf_op jit(solution)/shard_map/ppermute | solution.py:412
  168.3 17.4 %collective-permute-start.31 = (bf16[4,256,256]{2,1,0:T(8,128)(2,1)}, bf16[4,256,256]{2,1,0:T(8,128)(2,1)S(1)}, u32[]{:S(2)}, u32[]{:S(2)}) collective-permute-start(bf16[4,256,256]{2,1,0:T(8,128)(2,1)} %collective-permute-done.30.refs_11_.refs_16_.refs_12_.refs_17_), channel_id=1, source_target_pairs={{0,16},{16,0},{1,17},{17,1},{2,18},{18,2},{3,19},{19,3},{4,20},{20... | collective-permute-start | bytes 1572872 | tf_op jit(solution)/shard_map/ppermute | solution.py:405
  170.3 27.3 %collective-permute-start.41 = (bf16[4,256,256]{2,1,0:T(8,128)(2,1)S(1)}, bf16[4,256,256]{2,1,0:T(8,128)(2,1)S(1)}, u32[]{:S(2)}, u32[]{:S(2)}) collective-permute-start(bf16[4,256,256]{2,1,0:T(8,128)(2,1)S(1)} %select_bitcast_fusion.1), channel_id=1, source_target_pairs={{0,8},{1,9},{2,10},{3,11},{4,12},{5,13},{6,14},{7,15},{8,0},{9,1},... | collective-permute-start | bytes 1572872 | tf_op jit(solution)/shard_map/ppermute | solution.py:424
  171.6 26.1 %collective-permute-start.44 = (bf16[2,4,256,256]{3,2,1,0:T(8,128)(2,1)S(1)}, bf16[2,4,256,256]{3,2,1,0:T(8,128)(2,1)S(1)}, u32[]{:S(2)}, u32[]{:S(2)}) collective-permute-start(bf16[2,4,256,256]{3,2,1,0:T(8,128)(2,1)S(1)} %pad_maximum_fusion.9.refs_12_.refs_7_), channel_id=1, source_target_pairs={{0,4},{1,5},{2,6},{3,7},{4,0},{5,1},{6,2},{7,3},{8,12},{9,13},{10,... | collective-permute-start | bytes 3145736 | tf_op jit(solution)/shard_map/ppermute | solution.py:424
  184.9 40.1 %collective-permute-start.40 = (bf16[2,4,256,256]{3,2,1,0:T(8,128)(2,1)}, bf16[2,4,256,256]{3,2,1,0:T(8,128)(2,1)S(1)}, u32[]{:S(2)}, u32[]{:S(2)}) collective-permute-start(bf16[2,4,256,256]{3,2,1,0:T(8,128)(2,1)} %collective-permute-done.37.refs_8_.refs_3_), channel_id=1, source_target_pairs={{0,16},{16,0},{1,17},{17,1},{2,18},{18,2},{3,19},{19,3},{4,20},{20... | collective-permute-start | bytes 3145736 | tf_op jit(solution)/shard_map/ppermute | solution.py:405
  197.8 19.2 %collective-permute-start.46 = (bf16[4,256,256]{2,1,0:T(8,128)(2,1)S(1)}, bf16[4,256,256]{2,1,0:T(8,128)(2,1)S(1)}, u32[]{:S(2)}, u32[]{:S(2)}) collective-permute-start(bf16[4,256,256]{2,1,0:T(8,128)(2,1)S(1)} %select_bitcast_fusion), channel_id=1, source_target_pairs={{0,8},{1,9},{2,10},{3,11},{4,12},{5,13},{6,14},{7,15},{8,0},{9,1},... | collective-permute-start | bytes 1572872 | tf_op jit(solution)/shard_map/ppermute | solution.py:424
  199.1 26.1 %collective-permute-start.45 = (bf16[2,4,256,256]{3,2,1,0:T(8,128)(2,1)S(1)}, bf16[2,4,256,256]{3,2,1,0:T(8,128)(2,1)S(1)}, u32[]{:S(2)}, u32[]{:S(2)}) collective-permute-start(bf16[2,4,256,256]{3,2,1,0:T(8,128)(2,1)S(1)} %collective-permute-done.44.refs_13_.refs_8_), channel_id=1, source_target_pairs={{0,16},{16,0},{1,17},{17,1},{2,18},{18,2},{3,19},{19,3},{4,20},{20... | collective-permute-start | bytes 3145736 | tf_op jit(solution)/shard_map/ppermute | solution.py:405
  199.6 16.3 %collective-permute-start.39 = (f32[320,256]{1,0:T(8,128)S(1)}, f32[320,256]{1,0:T(8,128)}, u32[]{:S(2)}, u32[]{:S(2)}) collective-permute-start(f32[320,256]{1,0:T(8,128)S(1)} %get-tuple-element.178), channel_id=1, source_target_pairs={{0,3},{1,2},{2,1},{3,0},{4,7},{5,6},{6,5},{7,4},{8,11},{9,10},{10,... | collective-permute-start | bytes 983048 | tf_op jit(solution)/shard_map/ppermute | solution.py:400
  200.5 22.3 %collective-permute-start.35 = (bf16[320,1024]{1,0:T(8,128)(2,1)S(1)}, bf16[320,1024]{1,0:T(8,128)(2,1)S(1)}, u32[]{:S(2)}, u32[]{:S(2)}) collective-permute-start(bf16[320,1024]{1,0:T(8,128)(2,1)S(1)} %copy-done.54), channel_id=1, source_target_pairs={{0,1},{1,0},{2,3},{3,2},{4,5},{5,4},{6,7},{7,6},{8,9},{9,8},{10,11... | collective-permute-start | bytes 1966088 | tf_op jit(solution)/shard_map/ppermute | solution.py:412
  222.8 15.8 %collective-permute-start.48 = (f32[320,256]{1,0:T(8,128)S(1)}, f32[320,256]{1,0:T(8,128)S(1)}, u32[]{:S(2)}, u32[]{:S(2)}) collective-permute-start(f32[320,256]{1,0:T(8,128)S(1)} %get-tuple-element.186.refs_0_), channel_id=1, source_target_pairs={{0,1},{1,0},{2,3},{3,2},{4,5},{5,4},{6,7},{7,6},{8,9},{9,8},{10,11... | collective-permute-start | bytes 983048 | tf_op jit(solution)/shard_map/ppermute | solution.py:412
  239.2 15.0 %collective-permute-start.50 = (bf16[320,1024]{1,0:T(8,128)(2,1)}, bf16[320,1024]{1,0:T(8,128)(2,1)S(1)}, u32[]{:S(2)}, u32[]{:S(2)}) collective-permute-start(bf16[320,1024]{1,0:T(8,128)(2,1)} %get-tuple-element.188), channel_id=1, source_target_pairs={{0,1},{1,0},{2,3},{3,2},{4,5},{5,4},{6,7},{7,6},{8,9},{9,8},{10,11... | collective-permute-start | bytes 1966088 | tf_op jit(solution)/shard_map/ppermute | solution.py:412
  278.2 32.1 %collective-permute-start.53 = (bf16[2,8,256,256]{3,2,1,0:T(8,128)(2,1)}, bf16[2,8,256,256]{3,2,1,0:T(8,128)(2,1)S(1)}, u32[]{:S(2)}, u32[]{:S(2)}) collective-permute-start(bf16[2,8,256,256]{3,2,1,0:T(8,128)(2,1)} %get-tuple-element.201), channel_id=1, source_target_pairs={{0,16},{16,0},{1,17},{17,1},{2,18},{18,2},{3,19},{19,3},{4,20},{20... | collective-permute-start | bytes 6291464 | tf_op jit(solution)/shard_map/ppermute | solution.py:405
  280.9 26.1 %collective-permute-start.54 = (bf16[8,256,256]{2,1,0:T(8,128)(2,1)}, bf16[8,256,256]{2,1,0:T(8,128)(2,1)}, u32[]{:S(2)}, u32[]{:S(2)}) collective-permute-start(bf16[8,256,256]{2,1,0:T(8,128)(2,1)} %get-tuple-element.203), channel_id=1, source_target_pairs={{0,16},{16,0},{1,17},{17,1},{2,18},{18,2},{3,19},{19,3},{4,20},{20... | collective-permute-start | bytes 3145736 | tf_op jit(solution)/shard_map/ppermute | solution.py:405
  282.7 16.2 %collective-permute-start.52 = (f32[320,256]{1,0:T(8,128)}, f32[320,256]{1,0:T(8,128)}, u32[]{:S(2)}, u32[]{:S(2)}) collective-permute-start(f32[320,256]{1,0:T(8,128)} %constant_dynamic-slice_fusion), channel_id=1, source_target_pairs={{0,3},{1,2},{2,1},{3,0},{4,7},{5,6},{6,5},{7,4},{8,11},{9,10},{10,... | collective-permute-start | bytes 983048 | tf_op jit(solution)/shard_map/ppermute | solution.py:400
  282.8 24.2 %collective-permute-start.51 = (bf16[320,1024]{1,0:T(8,128)(2,1)}, bf16[320,1024]{1,0:T(8,128)(2,1)}, u32[]{:S(2)}, u32[]{:S(2)}) collective-permute-start(bf16[320,1024]{1,0:T(8,128)(2,1)} %get-tuple-element.192), channel_id=1, source_target_pairs={{0,1},{1,0},{2,3},{3,2},{4,5},{5,4},{6,7},{7,6},{8,9},{9,8},{10,11... | collective-permute-start | bytes 1966088 | tf_op jit(solution)/shard_map/ppermute | solution.py:412
  322.7 15.9 %collective-permute-start.56 = (bf16[320,1024]{1,0:T(8,128)(2,1)}, bf16[320,1024]{1,0:T(8,128)(2,1)}, u32[]{:S(2)}, u32[]{:S(2)}) collective-permute-start(bf16[320,1024]{1,0:T(8,128)(2,1)} %get-tuple-element.213), channel_id=1, source_target_pairs={{0,1},{1,0},{2,3},{3,2},{4,5},{5,4},{6,7},{7,6},{8,9},{9,8},{10,11... | collective-permute-start | bytes 1966088 | tf_op jit(solution)/shard_map/ppermute | solution.py:412
  334.4 45.3 %collective-permute-start.63 = (bf16[2,8,256,256]{3,2,1,0:T(8,128)(2,1)}, bf16[2,8,256,256]{3,2,1,0:T(8,128)(2,1)S(1)}, u32[]{:S(2)}, u32[]{:S(2)}) collective-permute-start(bf16[2,8,256,256]{3,2,1,0:T(8,128)(2,1)} %pad_maximum_fusion), channel_id=1, source_target_pairs={{0,4},{1,5},{2,6},{3,7},{4,0},{5,1},{6,2},{7,3},{8,12},{9,13},{10,... | collective-permute-start | bytes 6291464 | tf_op jit(solution)/shard_map/ppermute | solution.py:424
  351.9 24.9 %collective-permute-start.69 = (bf16[2,4,256,256]{3,2,1,0:T(8,128)(2,1)}, bf16[2,4,256,256]{3,2,1,0:T(8,128)(2,1)}, u32[]{:S(2)}, u32[]{:S(2)}) collective-permute-start(bf16[2,4,256,256]{3,2,1,0:T(8,128)(2,1)} %pad_maximum_fusion.10), channel_id=1, source_target_pairs={{0,4},{1,5},{2,6},{3,7},{4,0},{5,1},{6,2},{7,3},{8,12},{9,13},{10,... | collective-permute-start | bytes 3145736 | tf_op jit(solution)/shard_map/ppermute | solution.py:424
  371.4 19.1 %collective-permute-start.61 = (bf16[2,8,256,256]{3,2,1,0:T(8,128)(2,1)}, bf16[2,8,256,256]{3,2,1,0:T(8,128)(2,1)}, u32[]{:S(2)}, u32[]{:S(2)}) collective-permute-start(bf16[2,8,256,256]{3,2,1,0:T(8,128)(2,1)} %get-tuple-element.235), channel_id=1, source_target_pairs={{0,16},{16,0},{1,17},{17,1},{2,18},{18,2},{3,19},{19,3},{4,20},{20... | collective-permute-start | bytes 6291464 | tf_op jit(solution)/shard_map/ppermute | solution.py:405
  374.0 19.0 %collective-permute-start.60 = (bf16[320,1024]{1,0:T(8,128)(2,1)}, bf16[320,1024]{1,0:T(8,128)(2,1)}, u32[]{:S(2)}, u32[]{:S(2)}) collective-permute-start(bf16[320,1024]{1,0:T(8,128)(2,1)} %get-tuple-element.228), channel_id=1, source_target_pairs={{0,1},{1,0},{2,3},{3,2},{4,5},{5,4},{6,7},{7,6},{8,9},{9,8},{10,11... | collective-permute-start | bytes 1966088 | tf_op jit(solution)/shard_map/ppermute | solution.py:412
  384.1 28.2 %collective-permute-start.65 = (bf16[8,256,256]{2,1,0:T(8,128)(2,1)S(1)}, bf16[8,256,256]{2,1,0:T(8,128)(2,1)}, u32[]{:S(2)}, u32[]{:S(2)}) collective-permute-start(bf16[8,256,256]{2,1,0:T(8,128)(2,1)S(1)} %add_convert_fusion.6), channel_id=1, source_target_pairs={{0,8},{1,9},{2,10},{3,11},{4,12},{5,13},{6,14},{7,15},{8,0},{9,1},... | collective-permute-start | bytes 3145736 | tf_op jit(solution)/shard_map/ppermute | solution.py:424
  389.3 20.9 %collective-permute-start.84 = (bf16[2,256,256]{2,1,0:T(8,128)(2,1)S(1)}, bf16[2,256,256]{2,1,0:T(8,128)(2,1)S(1)}, u32[]{:S(2)}, u32[]{:S(2)}) collective-permute-start(bf16[2,256,256]{2,1,0:T(8,128)(2,1)S(1)} %fusion.34), channel_id=1, source_target_pairs={{0,16},{16,0},{1,17},{17,1},{2,18},{18,2},{3,19},{19,3},{4,20},{20... | collective-permute-start | bytes 786440 | tf_op jit(solution)/shard_map/ppermute | solution.py:405
  410.2 17.7 %collective-permute-start.68 = (bf16[4,256,256]{2,1,0:T(8,128)(2,1)}, bf16[4,256,256]{2,1,0:T(8,128)(2,1)}, u32[]{:S(2)}, u32[]{:S(2)}) collective-permute-start(bf16[4,256,256]{2,1,0:T(8,128)(2,1)} %get-tuple-element.256), channel_id=1, source_target_pairs={{0,16},{16,0},{1,17},{17,1},{2,18},{18,2},{3,19},{19,3},{4,20},{20... | collective-permute-start | bytes 1572872 | tf_op jit(solution)/shard_map/ppermute | solution.py:405
  412.3 25.3 %collective-permute-start.66 = (bf16[320,1024]{1,0:T(8,128)(2,1)}, bf16[320,1024]{1,0:T(8,128)(2,1)}, u32[]{:S(2)}, u32[]{:S(2)}) collective-permute-start(bf16[320,1024]{1,0:T(8,128)(2,1)} %get-tuple-element.247), channel_id=1, source_target_pairs={{0,1},{1,0},{2,3},{3,2},{4,5},{5,4},{6,7},{7,6},{8,9},{9,8},{10,11... | collective-permute-start | bytes 1966088 | tf_op jit(solution)/shard_map/ppermute | solution.py:412
  420.9 16.7 %collective-permute-start.67 = (bf16[2,4,256,256]{3,2,1,0:T(8,128)(2,1)}, bf16[2,4,256,256]{3,2,1,0:T(8,128)(2,1)}, u32[]{:S(2)}, u32[]{:S(2)}) collective-permute-start(bf16[2,4,256,256]{3,2,1,0:T(8,128)(2,1)} %get-tuple-element.254), channel_id=1, source_target_pairs={{0,16},{16,0},{1,17},{17,1},{2,18},{18,2},{3,19},{19,3},{4,20},{20... | collective-permute-start | bytes 3145736 | tf_op jit(solution)/shard_map/ppermute | solution.py:405
  427.7 68.8 %collective-permute-start.85 = (bf16[2,8,256,256]{3,2,1,0:T(8,128)(2,1)}, bf16[2,8,256,256]{3,2,1,0:T(8,128)(2,1)}, u32[]{:S(2)}, u32[]{:S(2)}) collective-permute-start(bf16[2,8,256,256]{3,2,1,0:T(8,128)(2,1)} %pad_maximum_fusion.1), channel_id=1, source_target_pairs={{0,4},{1,5},{2,6},{3,7},{4,0},{5,1},{6,2},{7,3},{8,12},{9,13},{10,... | collective-permute-start | bytes 6291464 | tf_op jit(solution)/shard_map/ppermute | solution.py:424
  429.1 17.1 %collective-permute-start.78 = (bf16[4,256,256]{2,1,0:T(8,128)(2,1)S(1)}, bf16[4,256,256]{2,1,0:T(8,128)(2,1)S(1)}, u32[]{:S(2)}, u32[]{:S(2)}) collective-permute-start(bf16[4,256,256]{2,1,0:T(8,128)(2,1)S(1)} %add_convert_fusion.10), channel_id=1, source_target_pairs={{0,8},{1,9},{2,10},{3,11},{4,12},{5,13},{6,14},{7,15},{8,0},{9,1},... | collective-permute-start | bytes 1572872 | tf_op jit(solution)/shard_map/ppermute | solution.py:424
  444.2 40.9 %collective-permute-start.76 = (bf16[320,256]{1,0:T(8,128)(2,1)S(1)}, bf16[320,256]{1,0:T(8,128)(2,1)S(1)}, u32[]{:S(2)}, u32[]{:S(2)}) collective-permute-start(bf16[320,256]{1,0:T(8,128)(2,1)S(1)} %dynamic-slice_convert_fusion), channel_id=1, source_target_pairs={{0,3},{1,2},{2,1},{3,0},{4,7},{5,6},{6,5},{7,4},{8,11},{9,10},{10,... | collective-permute-start | bytes 491528 | tf_op jit(solution)/shard_map/ppermute | solution.py:400
  447.6 39.6 %collective-permute-start.79 = (bf16[2,4,256,256]{3,2,1,0:T(8,128)(2,1)}, bf16[2,4,256,256]{3,2,1,0:T(8,128)(2,1)}, u32[]{:S(2)}, u32[]{:S(2)}) collective-permute-start(bf16[2,4,256,256]{3,2,1,0:T(8,128)(2,1)} %pad_maximum_fusion.11), channel_id=1, source_target_pairs={{0,4},{1,5},{2,6},{3,7},{4,0},{5,1},{6,2},{7,3},{8,12},{9,13},{10,... | collective-permute-start | bytes 3145736 | tf_op jit(solution)/shard_map/ppermute | solution.py:424
  451.9 18.7 %collective-permute-start.73 = (f32[2,25,256]{2,0,1:T(2,128)S(1)}, f32[2,25,256]{2,0,1:T(2,128)}, u32[]{:S(2)}, u32[]{:S(2)}) collective-permute-start(f32[2,25,256]{2,0,1:T(2,128)S(1)} %add.206), channel_id=1, source_target_pairs={{0,8},{4,12},{8,0},{12,4},{1,9},{5,13},{9,1},{13,5},{2,10},{6,14},... | collective-permute-start | bytes 153608 | tf_op jit(solution)/shard_map/ppermute | solution.py:439
  499.7 17.5 %collective-permute-start.86 = (bf16[2,4,256,256]{3,2,1,0:T(8,128)(2,1)}, bf16[2,4,256,256]{3,2,1,0:T(8,128)(2,1)}, u32[]{:S(2)}, u32[]{:S(2)}) collective-permute-start(bf16[2,4,256,256]{3,2,1,0:T(8,128)(2,1)} %broadcast_select_fusion), channel_id=1, source_target_pairs={{0,16},{16,0},{1,17},{17,1},{2,18},{18,2},{3,19},{19,3},{4,20},{20... | collective-permute-start | bytes 3145736 | tf_op jit(solution)/shard_map/ppermute | solution.py:405
  518.9 23.8 %collective-permute-start.87 = (bf16[4,256,256]{2,1,0:T(8,128)(2,1)S(1)}, bf16[4,256,256]{2,1,0:T(8,128)(2,1)S(1)}, u32[]{:S(2)}, u32[]{:S(2)}) collective-permute-start(bf16[4,256,256]{2,1,0:T(8,128)(2,1)S(1)} %slice_bitcast_fusion.14), channel_id=1, source_target_pairs={{0,3},{1,2},{2,1},{3,0},{4,7},{5,6},{6,5},{7,4},{8,11},{9,10},{10,... | collective-permute-start | bytes 1572872 | tf_op jit(solution)/shard_map/ppermute | solution.py:400
  (115 other events, 1003.5 us)

commit v3 on v2

--- a/solution.py
+++ b/solution.py
@@ -395,6 +395,36 @@
     write(outs[4], 1 - core, meta[3])
 
 
+def near_add_kernel(meta, near, arrived, moved, out):
+    for block in range(2):
+        extra = jnp.where(meta[4] == block, moved[...].astype(wide_type), 0.0)
+        total = near[block].astype(wide_type) + arrived[block].astype(wide_type) + extra
+        out[block] = total.astype(low_type)
+
+
+def finish_feed_kernel(meta, *refs):
+    halves, (up, down) = refs[:-2], refs[-2:]
+    first = meta[4] == 0
+    for layer in range(len(halves) // 2):
+        part, other = halves[2 * layer], halves[2 * layer + 1]
+        for tile in range(4):
+            mine, its = part[tile].astype(wide_type), other[tile].astype(wide_type)
+            up[layer, :, tile * 256 : (tile + 1) * 256] = jnp.where(first, mine, its)
+            down[layer, tile * 256 : (tile + 1) * 256, :] = jnp.where(first, its, mine)
+
+
+def finish_attend_kernel(meta, *refs):
+    halves, (thirds, square) = refs[:-2], refs[-2:]
+    first = meta[4] == 0
+    for layer in range(len(halves) // 2):
+        part, other = halves[2 * layer], halves[2 * layer + 1]
+        mine, its = part[...].astype(wide_type), other[...].astype(wide_type)
+        thirds[layer, 0] = jnp.where(first, mine[0], its[0])
+        thirds[layer, 1] = jnp.where(first, mine[1], its[1])
+        thirds[layer, 2] = jnp.where(first, its[0], mine[0])
+        square[layer] = jnp.where(first, its[1], mine[1])
+
+
 def flip_col(value):
     count = lax.axis_size("col")
     return lax.ppermute(value, "col", [(i, count - 1 - i) for i in range(count)])
@@ -492,27 +522,12 @@
     return own, near, swap_core(near_other), add(far, swap_core(far_other))
 
 
-def scatter_second(own, near, near_arrived, far, moved, first_core):
-    moved = moved.astype(wide_type)
-    total = near.astype(wide_type) + near_arrived.astype(wide_type)
-    lower = total[0] + jnp.where(first_core, moved, 0.0)
-    upper = total[1] + jnp.where(first_core, 0.0, moved)
-    return own, jnp.stack([lower, upper]).astype(low_type)
-
-
-def scatter_third(own, near, first_core):
-    own = add(own, cross_row(near, 1, 2))
+def scatter_third(own, arrived, first_core):
+    own = add(own, arrived)
     half = own.shape[1] // 2
     lower, upper = own[:, :half], own[:, half:]
     arrived = swap_core(jnp.where(first_core, upper, lower))
     return add(jnp.where(first_core, lower, upper), arrived)
-
-
-def scatter_fourth(part, first_core):
-    part = add(part[0], flip_col(part[1]))
-    other = swap_core(part)
-    halves = jnp.where(first_core, jnp.stack([part, other]), jnp.stack([other, part]))
-    return halves.reshape((-1,) + part.shape[1:]).astype(wide_type)
 
 
 def body(
@@ -558,25 +573,21 @@
     def other_half(value):
         return lax.dynamic_slice_in_dim(value, (1 - group_index) * rows, rows, 0)
 
-    def row_blocks(own, flipped, event):
-        blocks = [own, flipped]
-        for step in range(1, half_group):
-            blocks = blocks + [group_shift(own, step), group_shift(after(flipped, event), step)]
-        return blocks
-
     block_places = []
     for step in range(half_group):
         base = group_index * half_group
         source = base + (col_index - base + half_group - step) % half_group
         block_places = block_places + [source, col_count - 1 - source]
 
-    def share_rows(value, kind=wide_type):
+    def join_rows(value, received):
         own = lax.dynamic_slice_in_dim(value, col_index * width, width, 1)
-        other = lax.dynamic_slice_in_dim(value, (col_count - 1 - col_index) * width, width, 1)
-        received = flip_col(other.astype(kind)).astype(wide_type)
         lower = jnp.where(group_index == 0, own, received)
         upper = jnp.where(group_index == 0, received, own)
         return jnp.concatenate([lower, upper])
+
+    def share_rows(value, kind):
+        other = lax.dynamic_slice_in_dim(value, (col_count - 1 - col_index) * width, width, 1)
+        return join_rows(value, flip_col(other.astype(kind)).astype(wide_type))
 
     own_lengths = lax.dynamic_slice_in_dim(lengths, group_index * seqs, seqs, 0)
     meta = jnp.concatenate(
@@ -602,56 +613,94 @@
     hidden_pack = jnp.concatenate([in_bias.reshape(-1, width), up_bias.reshape(-1, width)])
     feature_rows = feature_pack.shape[0]
     small = jnp.concatenate([feature_pack, hidden_pack])
-    small_flipped = flip_col(small)
     states_own, states_other = own_half(states), other_half(states)
+    gate = []
+
+    def gated(value):
+        return after(value, *gate) if gate else value
+
+    def all_shifts(value):
+        return [group_shift(value, step) for step in range(1, half_group)]
+
+    def all_blocks(own, own_shifts, flipped, flipped_shifts):
+        blocks = [own, flipped]
+        for pair in zip(own_shifts, flipped_shifts):
+            blocks = blocks + list(pair)
+        return blocks
+
+    total_steps = [
+        (axis, 2**bit)
+        for axis in ("dp", "row")
+        for bit in range(lax.axis_size(axis).bit_length() - 1)
+    ]
+    token_total = jnp.sum(lengths)
+
+    def count_step(value, axis, step):
+        size = lax.axis_size(axis)
+        return value + lax.ppermute(value, axis, [(i, i ^ step) for i in range(size)])
+
     if tiled:
+        count = 6
+        shards, flips, owns, nears, near_others, fars, far_others = (
+            [None] * count for kind in range(7)
+        )
 
         def up_tiles(weight):
             return jnp.transpose(weight.reshape(256, 4, 256), (1, 0, 2))
 
-        def down_tiles(weight):
-            return weight.reshape(4, 256, 256)
-
-        def attend_tiles(thirds, square):
-            return jnp.concatenate([thirds, square[None]])
-
-        count = 6
-        shards, flips, owns, nears, fars = ([None] * count for kind in range(5))
-
-        def flip(place, *events):
+        def flip(place):
             layer = place // 3
             if place % 3 == 0:
-                thirds, square = in_thirds[layer], proj_weight[layer]
-                if events:
-                    thirds, square = after(thirds, *events), after(square, *events)
-                shards[place] = attend_tiles(thirds, square)
+                square = gated(proj_weight[layer])[None]
+                shards[place] = jnp.concatenate([gated(in_thirds[layer]), square])
             elif place % 3 == 1:
-                shards[place] = up_tiles(after(up_weight[layer], *events))
+                shards[place] = up_tiles(gated(up_weight[layer]))
             else:
-                shards[place] = down_tiles(after(down_weight[layer], *events))
+                shards[place] = gated(down_weight[layer]).reshape(4, 256, 256)
             flips[place] = flip_tiles(shards[place], first_core)
             return flips[place][0]
 
-        def near(place, *events):
+        def near(place):
             owns[place] = join_tiles(shards[place], *flips[place], first_core)
-            nears[place] = gather_near(after(owns[place], *events))
+            nears[place] = cross_row(gated(owns[place]), 1, 2)
             return nears[place]
 
-        def far(place, *events):
-            fars[place] = gather_far(after(nears[place], *events), first_core)
+        def near_swap(place):
+            near_others[place] = swap_core(gated(nears[place]))
+            return near_others[place]
+
+        def far(place):
+            value = gated(nears[place])
+            fars[place] = cross_row(jnp.where(first_core, value[0], value[1]), 2, 1)
             return fars[place]
 
+        def far_swap(place):
+            far_others[place] = swap_core(gated(fars[place]))
+            return far_others[place]
+
         def pieces(place):
-            return gather_pieces(owns[place], nears[place], fars[place])
-
-        slot = [flip(0)]
-        states_flipped = flip_col(after(states_other, *slot))
-        slot = [near(0), states_flipped]
-        states_blocks = row_blocks(states_own, states_flipped, slot[0])
-        slot = [far(0, *slot), flip(1, *slot), *states_blocks[2:]]
-        slot = [near(1, *slot), flip(2, *slot)]
-        states_blocks[0] = after(states_blocks[0], *slot)
-        slot = [far(1, *slot), near(2, *slot), flip(3, *slot)]
+            return (
+                owns[place],
+                nears[place],
+                near_others[place],
+                fars[place],
+                far_others[place],
+            )
+
+        gate = [flip(0)]
+        states_flipped = flip_col(gated(states_other))
+        shifts_own = all_shifts(gated(states_own))
+        small_flipped = flip_col(gated(small))
+        gate = [near(0), states_flipped, small_flipped, *shifts_own]
+        small_pair = jnp.stack([small, gated(small_flipped)])
+        feature_all = order_blocks(small_pair[:, :feature_rows])
+        shifts_flipped = all_shifts(gated(states_flipped))
+        token_total = count_step(gated(token_total), *total_steps[0])
+        gate = [far(0), flip(1), near_swap(0), token_total, feature_all, *shifts_flipped]
+        states_blocks = all_blocks(states_own, shifts_own, states_flipped, shifts_flipped)
+        token_total = count_step(gated(token_total), *total_steps[1])
+        first_slot = [near(1), flip(2), token_total]
+        far_swap(0)
         in_full[0], proj_full[0] = (pieces(0), 0), (pieces(0), 3)
     else:
 
@@ -669,10 +718,16 @@
             up_full[layer] = ((whole.reshape(-1, model_width, 256),), 0)
             whole = jnp.transpose(both_blocks(down_weight[layer]), (0, 2, 1, 3))
             down_full[layer] = ((whole.reshape(-1, 256, model_width),), 0)
-        states_blocks = row_blocks(states_own, flip_col(states_other), states)
-
-    small_pair = jnp.stack([small, small_flipped])
-    feature_all = order_blocks(small_pair[:, :feature_rows])
+        states_flipped = flip_col(states_other)
+        small_flipped = flip_col(small)
+        states_blocks = all_blocks(
+            states_own, all_shifts(states_own), states_flipped, all_shifts(states_flipped)
+        )
+        for step in total_steps:
+            token_total = count_step(token_total, *step)
+        small_pair = jnp.stack([small, small_flipped])
+        feature_all = order_blocks(small_pair[:, :feature_rows])
+
     feature_all = jnp.transpose(feature_all, (1, 0, 2)).reshape(feature_rows, model_width)
     gains = feature_all[: 2 * LAYERS].reshape(LAYERS, 2, 1, model_width)
     shifts = feature_all[2 * LAYERS : 4 * LAYERS].reshape(LAYERS, 2, 1, model_width)
@@ -697,7 +752,7 @@
             scratch_shapes=list(scratch),
             compiler_params=pltpu.CompilerParams(vmem_limit_bytes=vmem_bytes),
             cost_estimate=pl.CostEstimate(
-                flops=int(cost * 1.15e9), bytes_accessed=1024 * 1024, transcendentals=0
+                flops=int(cost * 9.2e9), bytes_accessed=1024 * 1024, transcendentals=0
             ),
         )(*operands)
 
@@ -799,6 +854,27 @@
     all_mask = (positions[None, :] < lengths[:, None]).reshape(token_rows, 1).astype(wide_type)
     teacher_wide = teacher.astype(wide_type)
 
+    def near_add(near, arrived, moved):
+        tiles = moved.shape[0]
+        both = pl.BlockSpec((2, 4, 256, 256), lambda index: (0, index, 0, 0))
+        single = pl.BlockSpec((4, 256, 256), lambda index: (index, 0, 0))
+        return pl.pallas_call(
+            near_add_kernel,
+            grid=(tiles // 4,),
+            out_shape=shape(2, tiles, 256, 256, kind=low_type),
+            in_specs=[SMEM, both, both, single],
+            out_specs=both,
+            cost_estimate=pl.CostEstimate(
+                flops=int(tiles * 2.4e9), bytes_accessed=1024 * 1024, transcendentals=0
+            ),
+        )(meta, near, arrived, moved)
+
+    def finish(kernel, cost, outs, parts):
+        halves = []
+        for part in parts:
+            halves = halves + [part, swap_core(part)]
+        return call(kernel, cost, (meta, *halves), [SMEM] + [VMEM] * len(halves), outs)
+
     saved = []
     base, sums = states_blocks, ()
     for layer in range(LAYERS):
@@ -808,41 +884,51 @@
             layer, base, sums
         )
         event = wide
-        if layer == 0 and tiled:
-            slot = [event, *slot]
-            slot = [far(2, *slot), near(3, *slot), flip(4, *slot)]
-            up_full[0], down_full[0] = (pieces(1), 0), (pieces(2), 0)
-        wide, arrived = group_total(wide, low)
         if layer == 0:
-            token_total = butterfly_sum(after(jnp.sum(lengths), event), ("dp", "row"))
+            if tiled:
+                gate = [wide, *first_slot]
+                token_total = count_step(gated(token_total), *total_steps[2])
+                second_slot = [far(1), near(2), flip(3), near_swap(1), token_total]
+            wide, arrived = group_total(wide, low)
             token_total = token_total.astype(wide_type)
             factor = 2.0 * token_rows * core_count * row_count / token_total
             seed_share = cotangent - factor * all_mask * teacher_wide
             seed_own, seed_other = own_half(seed_share), other_half(seed_share)
             if tiled:
-                arrived = after(arrived, *slot)
-                slot = [far(3, *slot), near(4, *slot), flip(5, *slot)]
-            else:
-                seed_flipped = flip_col(seed_other)
+                gate = [*second_slot, arrived]
+                second_slot = [far(2), near(3), flip(4), far_swap(1), near_swap(2)]
+                gate = [fars[2]]
+                far_swap(2)
+                up_full[0], down_full[0] = (pieces(1), 0), (pieces(2), 0)
         else:
             if tiled:
-                slot = [event, *slot]
-                slot = [far(5, *slot), seed_flipped]
+                low = after(low, seed_flipped)
+                gate = [event, *second_slot, seed_flipped]
+                second_slot = [far(5), far_swap(4), near_swap(5)]
+                gate = [fars[5]]
+                far_swap(5)
                 up_full[1], down_full[1] = (pieces(4), 0), (pieces(5), 0)
-                arrived = after(arrived, seed_flipped)
-            seed_blocks = row_blocks(after(seed_own, arrived), seed_flipped, arrived)
+            wide, arrived = group_total(wide, low)
+            gate = [arrived]
+            shifts_own, shifts_flipped = all_shifts(gated(seed_own)), all_shifts(gated(seed_flipped))
+            seed_blocks = all_blocks(seed_own, shifts_own, seed_flipped, shifts_flipped)
         middle, normed_two, hidden, slope, wide, low = feed(
             layer, current, (wide, arrived, proj_shift[layer])
         )
-        event = wide
         if layer == 1:
             low = after(low, *seed_blocks)
+        event = wide
         wide, arrived = group_total(wide, low)
-        if layer == 0 and tiled:
-            slot = [event, *slot]
-            seed_flipped = flip_col(after(seed_other, *slot))
-            slot = [far(4, *slot), near(5, *slot)]
-            in_full[1], proj_full[1] = (pieces(3), 0), (pieces(3), 3)
+        if layer == 0:
+            gate = [event, *second_slot] if tiled else []
+            if tiled:
+                second_slot = [far(3), near(4), flip(5), near_swap(3)]
+                gate = [fars[3]]
+                far_swap(3)
+                in_full[1], proj_full[1] = (pieces(3), 0), (pieces(3), 3)
+                gate = [arrived, *second_slot]
+                second_slot = [near(5), far(4), near_swap(4)]
+            seed_flipped = flip_col(gated(seed_other))
         base, sums = [middle], (wide, arrived)
         saved.append(
             (current, normed_one, queries, keys, values, lse, mixed, middle, normed_two, hidden, slope)
@@ -854,49 +940,16 @@
         [SMEM, SMEM] + [VMEM] * (4 + len(seed_blocks)),
         [wide_rows, wide_rows],
     )
-    output_share = share_rows(final)
-    residue = (output_share - teacher_wide) * all_mask
-    squared = jnp.sum(residue * residue)
+    output_other = lax.dynamic_slice_in_dim(
+        final, (col_count - 1 - col_index) * width, width, 1
+    )
+    output_halves = [flip_col(output_other[: rows // 2])]
 
     feature_grads = {}
     hidden_grads = {}
     in_grads, proj_grads, up_grads, down_grads = ([None] * LAYERS for kind in range(4))
 
-    def keep_feed(layer, tiles):
-        up_grads[layer] = jnp.transpose(tiles[:4], (1, 0, 2)).reshape(256, 1024)
-        down_grads[layer] = tiles[4:].reshape(1024, 256)
-
-    def keep_attend(layer, tiles):
-        in_grads[layer] = tiles[:3]
-        proj_grads[layer] = tiles[3]
-
-    def before_swap(low):
-        for item in under_way:
-            if item[0] == 1:
-                item[0] = 2
-                item[1] = item[1] + (cross_row(item[1][3], 2, 1),)
-                low = after(low, item[1][4])
-        return low
-
-    def beside_swap(arrived, pieces, keep):
-        value = scatter_first(pieces)
-        events = [*pieces, *value]
-        for item in under_way:
-            if item[0] == 2:
-                item[1] = scatter_second(*item[1], first_core)
-                events.append(item[1][1])
-            elif item[0] == 3:
-                item[1] = scatter_third(*item[1], first_core)
-                events.append(item[1])
-            elif item[0] == 4:
-                item[1] = scatter_fourth(item[1], first_core)
-                events.append(item[1])
-                item[2](item[1])
-            item[0] += 1
-        under_way.append([1, value, keep])
-        return after(arrived, *events)
-
-    under_way = []
+    way = []
     for layer in reversed(range(LAYERS)):
         current, normed_one, queries, keys, values, lse, mixed, middle, normed_two, hidden, slope = (
             saved[layer]
@@ -905,15 +958,26 @@
             layer, grad, slope
         )
         if tiled:
-            low = before_swap(low)
-        wide, arrived = group_total(wide, low)
+            if layer == LAYERS - 1:
+                gate = [low, output_halves[0]]
+            else:
+                gate = [low, far_moved, near_moved]
+        wide, arrived = group_total(wide, gated(low))
         if tiled:
-            if layer == LAYERS - 1:
-                arrived = after(arrived, output_share)
-            pieces = weight_tiles(
-                feed_weight_kernel, 8, 9.0, normed_two, pre, hidden, masked_low
+            tiles = weight_tiles(
+                feed_weight_kernel, 8, 9.0, normed_two, gated(pre), hidden, masked_low
             )
-            arrived = beside_swap(arrived, pieces, functools.partial(keep_feed, layer))
+            way.append(scatter_first(tiles))
+            gate = [arrived, *tiles, *way[-1]]
+            if layer < LAYERS - 1:
+                own, near_part, near_arrived, far_part = way[-2]
+                near_sent = near_add(near_part, near_arrived, far_moved)
+                part = scatter_third(way[-3][0], near_moved, first_core)
+                gate = gate + [near_sent, part]
+                near_moved = cross_row(near_sent, 1, 2)
+                flip_moved = flip_col(after(part[1], *gate))
+            arrived = gated(arrived)
+            far_moved = cross_row(gated(way[-1][3]), 2, 1)
         (
             grad,
             grad_low,
@@ -925,14 +989,29 @@
             wide,
             low,
         ) = attend_back(layer, (wide, arrived), middle, masked, (queries, keys, values, lse))
+        if layer == LAYERS - 1:
+            output_halves.append(flip_col(gated(output_other[rows // 2 :])))
         if tiled:
-            low = before_swap(low)
-        wide, arrived = group_total(wide, low)
+            gate = [low, far_moved] + (output_halves[1:] if layer == LAYERS - 1 else [])
+        wide, arrived = group_total(wide, gated(low))
         if tiled:
-            pieces = weight_tiles(
-                attend_weight_kernel, 4, 5.5, normed_one, triple, mixed, grad_low
+            own, near_part, near_arrived, far_part = way[-1]
+            near_sent = near_add(near_part, near_arrived, far_moved)
+            if layer < LAYERS - 1:
+                gate = [*gate, near_sent]
+            tiles = weight_tiles(
+                attend_weight_kernel, 4, 5.5, normed_one, gated(triple), mixed, grad_low
             )
-            arrived = beside_swap(arrived, pieces, functools.partial(keep_attend, layer))
+            way.append(scatter_first(tiles))
+            gate = [arrived, *tiles, *way[-1], near_sent]
+            if layer < LAYERS - 1:
+                feed_parts = [add(part[0], flip_moved)]
+                part = scatter_third(way[-3][0], near_moved, first_core)
+                gate = gate + [part, *feed_parts]
+                flip_moved = flip_col(after(part[1], *gate))
+            near_moved = cross_row(near_sent, 1, 2)
+            arrived = gated(arrived)
+            far_moved = cross_row(gated(way[-1][3]), 2, 1)
         else:
 
             def product(spec, left, right):
@@ -984,21 +1063,42 @@
             axis=1,
         )
 
-    for step, value, saver in under_way:
-        if step <= 1:
-            value = value + (cross_row(value[3], 2, 1),)
-        if step <= 2:
-            value = scatter_second(*value, first_core)
-        if step <= 3:
-            value = scatter_third(*value, first_core)
-        if step <= 4:
-            saver(scatter_fourth(value, first_core))
-    input_share = share_rows(grad, low_type)
+    if tiled:
+        gate = [grad, far_moved]
+        input_share = share_rows(gated(grad), low_type)
+        own, near_part, near_arrived, far_part = way[-1]
+        near_sent = near_add(near_part, near_arrived, far_moved)
+        attend_parts = [add(part[0], flip_moved)]
+        part = scatter_third(way[-2][0], near_moved, first_core)
+        last_moved = cross_row(after(near_sent, part), 1, 2)
+        feed_parts.append(add(part[0], flip_col(part[1])))
+        part = scatter_third(way[-1][0], last_moved, first_core)
+        gate = [part]
+        attend_parts.append(add(part[0], flip_col(part[1])))
+        up_grad, down_grad = finish(
+            finish_feed_kernel,
+            3.0,
+            [shape(LAYERS, 256, 1024), shape(LAYERS, 1024, 256)],
+            feed_parts[::-1],
+        )
+        in_grad, proj_grad = finish(
+            finish_attend_kernel,
+            2.0,
+            [shape(LAYERS, 3, 256, 256), shape(LAYERS, 256, 256)],
+            attend_parts[::-1],
+        )
+    else:
+        input_share = share_rows(grad, low_type)
+        up_grad, down_grad = jnp.stack(up_grads), jnp.stack(down_grads)
+        in_grad, proj_grad = jnp.stack(in_grads), jnp.stack(proj_grads)
+    output_share = join_rows(gated(final), gated(jnp.concatenate(output_halves)))
+    residue = (output_share - teacher_wide) * all_mask
+    squared = jnp.sum(residue * residue)
 
     feature_parts = jnp.concatenate(
         [part for layer in range(LAYERS) for part in feature_grads[layer]]
     )
-    feature_parts = feature_parts.reshape(-1, col_count, width)
+    feature_parts = gated(feature_parts).reshape(-1, col_count, width)
     own_parts = lax.dynamic_index_in_dim(feature_parts, col_index, 1, False)
     other_parts = lax.dynamic_index_in_dim(feature_parts, col_count - 1 - col_index, 1, False)
     hidden_parts = jnp.concatenate([hidden_grads[layer] for layer in range(LAYERS)], axis=1)
@@ -1019,13 +1119,13 @@
         input_share,
         features[:, 0:2],
         features[:, 2:4],
-        jnp.transpose(jnp.stack(in_grads), (0, 2, 1, 3)),
+        jnp.transpose(in_grad, (0, 2, 1, 3)),
         hiddens[:, 0:2],
-        jnp.stack(proj_grads),
+        proj_grad,
         features[:, 4],
-        jnp.stack(up_grads),
+        up_grad,
         hiddens[:, 2:].reshape(LAYERS, hidden_width),
-        jnp.stack(down_grads),
+        down_grad,
         features[:, 5],
     )
 

time: 566 us -> 529 us (0.935)
  the two profiles are of different devices: /device:TPU:9 before, /device:TPU:1 now
where the time goes in v3:
time: 529 us; the launch traced here: 520 us
  Pallas kernels  153 us (29%)
  waiting for transfers between devices  149 us (28%)
  starting transfers between devices  133 us (25%)
  other arithmetic  39.6 us (7%)
  local copies, waits for them, and re-layouts  35.5 us (7%)
  between operations  9.14 us (2%)
    pallas_call x17, Pallas kernels, call(): pl.pallas_call(kernel, out_shape=outs, in_specs=specs, out_specs=[VMEM] *...  138 us
    ppermute x13, waiting for transfers between devices, group_shift(): return lax.ppermute(value, 'col', pairs)  60.2 us
    ppermute x34, starting transfers between devices, swap_core(): return lax.ppermute(value, 'dp', [(i, count - 1 - i) for i in range(count)])  40.9 us
    ppermute x20, waiting for transfers between devices, cross_row(): return lax.ppermute(value, ('dp', 'row', 'col'), pairs)  39.3 us
    ppermute x17, waiting for transfers between devices, flip_col(): lax.ppermute(value, 'col', [(i, count - 1 - i) for i in range(count)])  36.8 us
    ppermute x17, starting transfers between devices, flip_col(): lax.ppermute(value, 'col', [(i, count - 1 - i) for i in range(count)])  29 us
    ppermute x20, starting transfers between devices, cross_row(): return lax.ppermute(value, ('dp', 'row', 'col'), pairs)  19.7 us
    ppermute x13, starting transfers between devices, group_shift(): return lax.ppermute(value, 'col', pairs)  17.2 us
  transfers between devices with their start and end apart: 92, of which 33 were waited for; matrix products, arithmetic and copies ran while one was open for 11% of the time, Pallas kernels for 26%

profile of v3, /device:TPU:1, one launch (start us, length us, event | category | flops | bytes accessed | tf_op | source)
XLA Modules:
  0.0 519.6 jit_solution(12589044586058178337)
XLA Ops:
  3.8 4.2 collective-permute-start
  8.0 6.1 %collective-permute-done = bf16[2,256,256]{2,1,0:T(8,128)(2,1)S(1)} collective-permute-done((bf16[2,256,256]{2,1,0:T(8,128)(2,1)S(1)}, bf16[2,256,256]{2,1,0:T(8,128)(2,1)S(1)}, u32[]{:S(2)}, u32[]{:S(2)}) %collective-permute-start) | collective-permute-done | bytes 262176 | tf_op jit(solution)/shard_map/ppermute | solution.py:430
  22.2 3.3 collective-permute-start.1
  25.4 3.0 collective-permute-start.2
  32.2 7.9 %collective-permute-done.5 = f32[24,256]{1,0:T(8,128)S(1)} collective-permute-done((f32[24,256]{1,0:T(8,128)S(1)}, f32[24,256]{1,0:T(8,128)S(1)}, u32[]{:S(2)}, u32[]{:S(2)}) %collective-permute-start.5) | collective-permute-done | bytes 24608 | tf_op jit(solution)/shard_map/ppermute | solution.py:430
  51.1 4.0 collective-permute-done.10
  57.3 5.7 %collective-permute-done.6.refs_3_ = f32[320,256]{1,0:T(8,128)} collective-permute-done((f32[320,256]{1,0:T(8,128)}, f32[320,256]{1,0:T(8,128)}, u32[]{:S(2)}, u32[]{:S(2)}) %collective-permute-start.6) | collective-permute-done | bytes 327712 | tf_op jit(solution)/shard_map/ppermute | solution.py:442
  66.5 6.0 %collective-permute-done.16 = bf16[2,256,256]{2,1,0:T(8,128)(2,1)} collective-permute-done((bf16[2,256,256]{2,1,0:T(8,128)(2,1)S(1)}, bf16[2,256,256]{2,1,0:T(8,128)(2,1)}, u32[]{:S(2)}, u32[]{:S(2)}) %collective-permute-start.16) | collective-permute-done | bytes 262176 | tf_op jit(solution)/shard_map/ppermute | solution.py:430
  79.9 10.4 %shard_map.237 = (f32[320,1024]{1,0:T(8,128)}, bf16[320,1024]{1,0:T(8,128)(2,1)}, bf16[320,512]{1,0:T(8,128)(2,1)}, bf16[320,512]{1,0:T(8,128)(2,1)}, bf16[320,5...) custom-call(s32[10]{0:T(128)} %concatenate.29.meta, ...), custom_call_target="tpu_custom_call" | custom-call | flops 96599998464 | bytes 1048576 | tf_op jit(solution)/shard_map/pallas_call | solution.py:747
  92.3 3.4 collective-permute-start.13
  96.9 8.9 %collective-permute-start.23 = (s32[]{:T(128)}, s32[]{:T(128)}, u32[]{:S(2)}, u32[]{:S(2)}) collective-permute-start(s32[]{:T(128)} %add.146), channel_id=1, source_target_pairs={{0,8},{4,12},{8,0},{12,4},{1,9},{5,13},{9,1},{13,5},{2,10},{6,14},... | collective-permute-start | bytes 20 | tf_op jit(solution)/shard_map/ppermute | solution.py:640
  110.0 7.7 %collective-permute-done.22 = bf16[2,256,256]{2,1,0:T(8,128)(2,1)} collective-permute-done((bf16[2,256,256]{2,1,0:T(8,128)(2,1)S(1)}, bf16[2,256,256]{2,1,0:T(8,128)(2,1)}, u32[]{:S(2)}, u32[]{:S(2)}) %collective-permute-start.22) | collective-permute-done | bytes 262176 | tf_op jit(solution)/shard_map/ppermute | solution.py:430
  135.3 12.1 %shard_map.238 = (f32[320,1024]{1,0:T(8,128)}, bf16[320,1024]{1,0:T(8,128)(2,1)}, bf16[320,2048]{1,0:T(8,128)(2,1)}, bf16[320,2048]{1,0:T(8,128)(2,1)}, f32[320,1024]{1,0:T(8,128)}, /*index=5*/bf16[320,1024]{1,0:T(8,128)(2,1)}) custom-call(s32[10]{0:T(128)} %concatenate.29.meta, f32[320,1024]{1,0:T(8,128)} %get-tuple-element.190.refs_0_.inputs, ...), custom_call_target="tpu_custom_call" | custom-call | flops 110399995904 | bytes 1048576 | tf_op jit(solution)/shard_map/pallas_call | solution.py:747
  155.1 4.9 collective-permute-start.28
  161.0 6.6 %collective-permute-done.33.refs_11_.refs_16_.refs_12_.refs_17_ = bf16[4,256,256]{2,1,0:T(8,128)(2,1)} collective-permute-done((bf16[4,256,256]{2,1,0:T(8,128)(2,1)S(1)}, bf16[4,256,256]{2,1,0:T(8,128)(2,1)}, u32[]{:S(2)}, u32[]{:S(2)}) %collective-permute-start.33) | collective-permute-done | bytes 524320 | tf_op jit(solution)/shard_map/ppermute | solution.py:454
  168.7 6.1 %collective-permute-done.28.refs_2_ = bf16[320,1024]{1,0:T(8,128)(2,1)S(1)} collective-permute-done((bf16[320,1024]{1,0:T(8,128)(2,1)}, bf16[320,1024]{1,0:T(8,128)(2,1)S(1)}, u32[]{:S(2)}, u32[]{:S(2)}) %collective-permute-start.28) | collective-permute-done | bytes 655392 | tf_op jit(solution)/shard_map/ppermute | solution.py:442
  178.7 11.1 %shard_map.239 = (f32[320,1024]{1,0:T(8,128)}, bf16[320,1024]{1,0:T(8,128)(2,1)}, bf16[320,512]{1,0:T(8,128)(2,1)}, bf16[320,512]{1,0:T(8,128)(2,1)}, bf16[320,5...) custom-call(s32[10]{0:T(128)} %concatenate.29.meta, ...), custom_call_target="tpu_custom_call" | custom-call | flops 96599998464 | bytes 1048576 | tf_op jit(solution)/shard_map/pallas_call | solution.py:747
  190.5 6.5 %collective-permute-done.43.refs_13_.refs_8_ = bf16[2,4,256,256]{3,2,1,0:T(8,128)(2,1)S(1)} collective-permute-done((bf16[2,4,256,256]{3,2,1,0:T(8,128)(2,1)S(1)}, bf16[2,4,256,256]{3,2,1,0:T(8,128)(2,1)S(1)}, u32[]{:S(2)}, u32[]{:S(2)}) %collective-permute-start.43) | collective-permute-done | bytes 1048608 | tf_op jit(solution)/shard_map/ppermute | solution.py:454
  199.1 6.4 %collective-permute-done.46.refs_15_.refs_10_ = bf16[4,256,256]{2,1,0:T(8,128)(2,1)S(1)} collective-permute-done((bf16[4,256,256]{2,1,0:T(8,128)(2,1)S(1)}, bf16[4,256,256]{2,1,0:T(8,128)(2,1)S(1)}, u32[]{:S(2)}, u32[]{:S(2)}) %collective-permute-start.46) | collective-permute-done | bytes 524320 | tf_op jit(solution)/shard_map/ppermute | solution.py:454
  207.1 6.6 %collective-permute-done.39.refs_2_ = bf16[320,1024]{1,0:T(8,128)(2,1)S(1)} collective-permute-done((bf16[320,1024]{1,0:T(8,128)(2,1)}, bf16[320,1024]{1,0:T(8,128)(2,1)S(1)}, u32[]{:S(2)}, u32[]{:S(2)}) %collective-permute-start.39) | collective-permute-done | bytes 655392 | tf_op jit(solution)/shard_map/ppermute | solution.py:442
  216.5 11.9 %shard_map.240 = (f32[320,1024]{1,0:T(8,128)}, bf16[320,1024]{1,0:T(8,128)(2,1)}, bf16[320,2048]{1,0:T(8,128)(2,1)}, bf16[320,2048]{1,0:T(8,128)(2,1)}, f32[320,1024]{1,0:T(8,128)}, /*index=5*/bf16[320,1024]{1,0:T(8,128)(2,1)}) custom-call(s32[10]{0:T(128)} %concatenate.29.meta, f32[320,1024]{1,0:T(8,128)} %get-tuple-element.211.refs_0_.inputs, ...), custom_call_target="tpu_custom_call" | custom-call | flops 110399995904 | bytes 1048576 | tf_op jit(solution)/shard_map/pallas_call | solution.py:747
  230.8 12.7 %collective-permute-done.50.arrived = bf16[320,1024]{1,0:T(8,128)(2,1)S(1)} collective-permute-done((bf16[320,1024]{1,0:T(8,128)(2,1)}, bf16[320,1024]{1,0:T(8,128)(2,1)S(1)}, u32[]{:S(2)}, u32[]{:S(2)}) %collective-permute-start.50) | collective-permute-done | bytes 655392 | tf_op jit(solution)/shard_map/ppermute | solution.py:442
  244.3 4.4 shard_map.241
  252.9 9.8 %shard_map.242 = (f32[320,1024]{1,0:T(8,128)}, bf16[320,1024]{1,0:T(8,128)(2,1)}, bf16[320,2048]{1,0:T(8,128)(2,1)}, f32[1,1024]{1,0:T(1,128)}, f32[1,2048]{1,0:...) custom-call(s32[10]{0:T(128)} %concatenate.29.meta, f32[320,1024]{1,0:T(8,128)} %get-tuple-element.229.refs_0_, ...), custom_call_target="tpu_custom_call" | custom-call | flops 92000002048 | bytes 1048576 | tf_op jit(solution)/shard_map/pallas_call | solution.py:747
  262.7 9.0 %shard_map.243 = (bf16[2,8,256,256]{3,2,1,0:T(8,128)(2,1)}, bf16[2,8,256,256]{3,2,1,0:T(8,128)(2,1)}, bf16[2,8,256,256]{3,2,1,0:T(8,128)(2,1)}, bf16[8,256,256]{2,1,0:T(8,128)(2,1)}, bf16[8,256,256]{2,1,0:T(8,128)(2,1)}) custom-call(s32[10]{0:T(128)} %concatenate.29.meta, bf16[320,1024]{1,0:T(8,128)(2,1)} %get-tuple-element.235.normed, ...), custom_call_target="tpu_custom_call" | custom-call | flops 82800001024 | bytes 1048576 | tf_op jit(solution)/shard_map/pallas_call | solution.py:747
  271.7 3.5 collective-permute-start.53
  275.3 5.4 %collective-permute-done.54 = bf16[8,256,256]{2,1,0:T(8,128)(2,1)S(1)} collective-permute-done((bf16[8,256,256]{2,1,0:T(8,128)(2,1)}, bf16[8,256,256]{2,1,0:T(8,128)(2,1)S(1)}, u32[]{:S(2)}, u32[]{:S(2)}) %collective-permute-start.54) | collective-permute-done | bytes 1048608 | tf_op jit(solution)/shard_map/ppermute | solution.py:435
  282.3 8.9 %collective-permute-done.52.refs_1_ = bf16[320,1024]{1,0:T(8,128)(2,1)S(1)} collective-permute-done((bf16[320,1024]{1,0:T(8,128)(2,1)S(1)}, bf16[320,1024]{1,0:T(8,128)(2,1)S(1)}, u32[]{:S(2)}, u32[]{:S(2)}) %collective-permute-start.52) | collective-permute-done | bytes 655392 | tf_op jit(solution)/shard_map/ppermute | solution.py:442
  293.0 11.7 %shard_map.244 = (f32[320,1024]{1,0:T(8,128)}, bf16[320,1024]{1,0:T(8,128)(2,1)}, f32[1,1024]{1,0:T(1,128)}, f32[1,1024]{1,0:T(1,128)}, f32[1,1024]{1,0:T(1,128)...) custom-call(s32[10]{0:T(128)} %concatenate.29.meta, ...), custom_call_target="tpu_custom_call" | custom-call | flops 110399995904 | bytes 1048576 | tf_op jit(solution)/shard_map/pallas_call | solution.py:747
  306.0 5.7 %shard_map.245 = (bf16[2,4,256,256]{3,2,1,0:T(8,128)(2,1)}, bf16[2,4,256,256]{3,2,1,0:T(8,128)(2,1)}, bf16[2,4,256,256]{3,2,1,0:T(8,128)(2,1)}, bf16[4,256,256]{2,1,0:T(8,128)(2,1)}, bf16[4,256,256]{2,1,0:T(8,128)(2,1)}) custom-call(s32[10]{0:T(128)} %concatenate.29.meta, bf16[320,1024]{1,0:T(8,128)(2,1)} %get-tuple-element.257.normed, ...), custom_call_target="tpu_custom_call" | custom-call | flops 50600001536 | bytes 1048576 | tf_op jit(solution)/shard_map/pallas_call | solution.py:747
  311.7 3.3 collective-permute-start.59
  315.1 4.3 shard_map.246
  322.1 4.3 shard_map.247
  326.4 9.8 %shard_map.248 = (f32[320,1024]{1,0:T(8,128)}, bf16[320,1024]{1,0:T(8,128)(2,1)}, bf16[320,2048]{1,0:T(8,128)(2,1)}, f32[1,1024]{1,0:T(1,128)}, f32[1,2048]{1,0:...) custom-call(s32[10]{0:T(128)} %concatenate.29.meta, f32[320,1024]{1,0:T(8,128)} %get-tuple-element.268.refs_0_, ...), custom_call_target="tpu_custom_call" | custom-call | flops 92000002048 | bytes 1048576 | tf_op jit(solution)/shard_map/pallas_call | solution.py:747
  337.0 3.2 shard_map.250
  341.5 9.3 %collective-permute-done.61 = bf16[2,8,256,256]{3,2,1,0:T(8,128)(2,1)S(1)} collective-permute-done((bf16[2,8,256,256]{3,2,1,0:T(8,128)(2,1)}, bf16[2,8,256,256]{3,2,1,0:T(8,128)(2,1)S(1)}, u32[]{:S(2)}, u32[]{:S(2)}) %collective-permute-start.61) | collective-permute-done | bytes 2097184 | tf_op jit(solution)/shard_map/ppermute | solution.py:454
  350.8 9.7 %shard_map.249 = (bf16[2,8,256,256]{3,2,1,0:T(8,128)(2,1)}, bf16[2,8,256,256]{3,2,1,0:T(8,128)(2,1)}, bf16[2,8,256,256]{3,2,1,0:T(8,128)(2,1)}, bf16[8,256,256]{2,1,0:T(8,128)(2,1)}, bf16[8,256,256]{2,1,0:T(8,128)(2,1)}) custom-call(s32[10]{0:T(128)} %concatenate.29.meta, bf16[320,1024]{1,0:T(8,128)(2,1)} %get-tuple-element.274.normed, ...), custom_call_target="tpu_custom_call" | custom-call | flops 82800001024 | bytes 1048576 | tf_op jit(solution)/shard_map/pallas_call | solution.py:747
  373.3 7.6 %collective-permute-done.62.refs_1_ = bf16[320,1024]{1,0:T(8,128)(2,1)S(1)} collective-permute-done((bf16[320,1024]{1,0:T(8,128)(2,1)}, bf16[320,1024]{1,0:T(8,128)(2,1)S(1)}, u32[]{:S(2)}, u32[]{:S(2)}) %collective-permute-start.62) | collective-permute-done | bytes 655392 | tf_op jit(solution)/shard_map/ppermute | solution.py:442
  384.0 11.9 %shard_map.251 = (f32[320,1024]{1,0:T(8,128)}, bf16[320,1024]{1,0:T(8,128)(2,1)}, f32[1,1024]{1,0:T(1,128)}, f32[1,1024]{1,0:T(1,128)}, f32[1,1024]{1,0:T(1,128)...) custom-call(s32[10]{0:T(128)} %concatenate.29.meta, ...), custom_call_target="tpu_custom_call" | custom-call | flops 110399995904 | bytes 1048576 | tf_op jit(solution)/shard_map/pallas_call | solution.py:747
  398.1 3.9 shard_map.252
  403.8 5.4 %shard_map.253 = (bf16[2,4,256,256]{3,2,1,0:T(8,128)(2,1)}, bf16[2,4,256,256]{3,2,1,0:T(8,128)(2,1)}, bf16[2,4,256,256]{3,2,1,0:T(8,128)(2,1)}, bf16[4,256,256]{2,1,0:T(8,128)(2,1)}, bf16[4,256,256]{2,1,0:T(8,128)(2,1)}) custom-call(s32[10]{0:T(128)} %concatenate.29.meta, bf16[320,1024]{1,0:T(8,128)(2,1)} %get-tuple-element.295.normed, ...), custom_call_target="tpu_custom_call" | custom-call | flops 50600001536 | bytes 1048576 | tf_op jit(solution)/shard_map/pallas_call | solution.py:747
  420.4 11.5 %collective-permute-done.67.arrived = bf16[320,1024]{1,0:T(8,128)(2,1)S(1)} collective-permute-done((bf16[320,1024]{1,0:T(8,128)(2,1)}, bf16[320,1024]{1,0:T(8,128)(2,1)S(1)}, u32[]{:S(2)}, u32[]{:S(2)}) %collective-permute-start.67) | collective-permute-done | bytes 655392 | tf_op jit(solution)/shard_map/ppermute | solution.py:442
  440.5 3.2 shard_map.255
  447.1 4.4 shard_map.254
  454.0 5.9 %collective-permute-done.76 = bf16[2,4,256,256]{3,2,1,0:T(8,128)(2,1)S(1)} collective-permute-done((bf16[2,4,256,256]{3,2,1,0:T(8,128)(2,1)}, bf16[2,4,256,256]{3,2,1,0:T(8,128)(2,1)S(1)}, u32[]{:S(2)}, u32[]{:S(2)}) %collective-permute-start.76) | collective-permute-done | bytes 1048608 | tf_op jit(solution)/shard_map/ppermute | solution.py:454
  479.3 3.9 shard_map.257
  487.3 12.9 %collective-permute-start.81 = (f32[]{:T(128)}, f32[]{:T(128)}, u32[]{:S(2)}, u32[]{:S(2)}) collective-permute-start(f32[]{:T(128)} %bitcast.86), channel_id=1, source_target_pairs={{0,1},{1,0},{2,3},{3,2},{4,5},{5,4},{6,7},{7,6},{8,9},{9,8},{10,11... | collective-permute-start | bytes 20 | tf_op jit(solution)/shard_map/ppermute | solution.py:469
  506.6 4.6 collective-permute-start.86
  (458 shorter events, 177.5 us)
Async XLA Ops:
  17.7 23.4 %collective-permute-start.4 = (bf16[2,4,256,256]{3,2,1,0:T(8,128)(2,1)}, bf16[2,4,256,256]{3,2,1,0:T(8,128)(2,1)}, u32[]{:S(2)}, u32[]{:S(2)}) collective-permute-start(bf16[2,4,256,256]{3,2,1,0:T(8,128)(2,1)} %pad_maximum_fusion.refs_8_.refs_13_.refs_9_.refs_14_), channel_id=1, source_target_pairs={{0,4},{1,5},{2,6},{3,7},{4,0},{5,1},{6,2},{7,3},{8,12},{9,13},{10,... | collective-permute-start | bytes 3145736 | tf_op jit(solution)/shard_map/ppermute | solution.py:454
  22.2 17.9 %collective-permute-start.1 = (f32[320,256]{1,0:T(8,128)}, f32[320,256]{1,0:T(8,128)S(1)}, u32[]{:S(2)}, u32[]{:S(2)}) collective-permute-start(f32[320,256]{1,0:T(8,128)} %get-tuple-element.180), channel_id=1, source_target_pairs={{0,3},{1,2},{2,1},{3,0},{4,7},{5,6},{6,5},{7,4},{8,11},{9,10},{10,... | collective-permute-start | bytes 983048 | tf_op jit(solution)/shard_map/ppermute | solution.py:430
  25.4 15.7 %collective-permute-start.2 = (f32[320,256]{1,0:T(8,128)}, f32[320,256]{1,0:T(8,128)}, u32[]{:S(2)}, u32[]{:S(2)}) collective-permute-start(f32[320,256]{1,0:T(8,128)} %get-tuple-element.181.refs_0_), channel_id=1, source_target_pairs={{0,1},{1,0},{2,3},{3,2},{4,5},{5,4},{6,7},{7,6},{8,9},{9,8},{10,11... | collective-permute-start | bytes 983048 | tf_op jit(solution)/shard_map/ppermute | solution.py:442
  42.5 20.6 %collective-permute-start.8 = (bf16[2,4,256,256]{3,2,1,0:T(8,128)(2,1)}, bf16[2,4,256,256]{3,2,1,0:T(8,128)(2,1)}, u32[]{:S(2)}, u32[]{:S(2)}) collective-permute-start(bf16[2,4,256,256]{3,2,1,0:T(8,128)(2,1)} %collective-permute-done.4.refs_9_.refs_14_.refs_10_.refs_15_), channel_id=1, source_target_pairs={{0,16},{16,0},{1,17},{17,1},{2,18},{18,2},{3,19},{19,3},{4,20},{20... | collective-permute-start | bytes 3145736 | tf_op jit(solution)/shard_map/ppermute | solution.py:435
  48.3 14.7 %collective-permute-start.6 = (f32[320,256]{1,0:T(8,128)}, f32[320,256]{1,0:T(8,128)}, u32[]{:S(2)}, u32[]{:S(2)}) collective-permute-start(f32[320,256]{1,0:T(8,128)} %copy-done.75), channel_id=1, source_target_pairs={{0,1},{1,0},{2,3},{3,2},{4,5},{5,4},{6,7},{7,6},{8,9},{9,8},{10,11... | collective-permute-start | bytes 983048 | tf_op jit(solution)/shard_map/ppermute | solution.py:442
  48.4 14.7 %collective-permute-start.9 = (bf16[4,256,256]{2,1,0:T(8,128)(2,1)S(1)}, bf16[4,256,256]{2,1,0:T(8,128)(2,1)}, u32[]{:S(2)}, u32[]{:S(2)}) collective-permute-start(bf16[4,256,256]{2,1,0:T(8,128)(2,1)S(1)} %select_bitcast_fusion.5), channel_id=1, source_target_pairs={{0,8},{1,9},{2,10},{3,11},{4,12},{5,13},{6,14},{7,15},{8,0},{9,1},... | collective-permute-start | bytes 1572872 | tf_op jit(solution)/shard_map/ppermute | solution.py:454
  55.1 18.8 %collective-permute-start.14 = (bf16[2,256,256]{2,1,0:T(8,128)(2,1)S(1)}, bf16[2,256,256]{2,1,0:T(8,128)(2,1)S(1)}, u32[]{:S(2)}, u32[]{:S(2)}) collective-permute-start(bf16[2,256,256]{2,1,0:T(8,128)(2,1)S(1)} %collective-permute-done.10), channel_id=1, source_target_pairs={{0,16},{16,0},{1,17},{17,1},{2,18},{18,2},{3,19},{19,3},{4,20},{20... | collective-permute-start | bytes 786440 | tf_op jit(solution)/shard_map/ppermute | solution.py:435
  64.5 15.4 %collective-permute-start.12 = (bf16[4,256,256]{2,1,0:T(8,128)(2,1)}, bf16[4,256,256]{2,1,0:T(8,128)(2,1)}, u32[]{:S(2)}, u32[]{:S(2)}) collective-permute-start(bf16[4,256,256]{2,1,0:T(8,128)(2,1)} %collective-permute-done.9.refs_11_.refs_16_.refs_12_.refs_17_), channel_id=1, source_target_pairs={{0,16},{16,0},{1,17},{17,1},{2,18},{18,2},{3,19},{19,3},{4,20},{20... | collective-permute-start | bytes 1572872 | tf_op jit(solution)/shard_map/ppermute | solution.py:435
  76.0 14.3 %collective-permute-start.15 = (bf16[2,4,256,256]{3,2,1,0:T(8,128)(2,1)S(1)}, bf16[2,4,256,256]{3,2,1,0:T(8,128)(2,1)}, u32[]{:S(2)}, u32[]{:S(2)}) collective-permute-start(bf16[2,4,256,256]{3,2,1,0:T(8,128)(2,1)S(1)} %pad_maximum_fusion.1.refs_7_.refs_2_), channel_id=1, source_target_pairs={{0,4},{1,5},{2,6},{3,7},{4,0},{5,1},{6,2},{7,3},{8,12},{9,13},{10,... | collective-permute-start | bytes 3145736 | tf_op jit(solution)/shard_map/ppermute | solution.py:454
  90.3 27.4 %collective-permute-start.18 = (bf16[2,4,256,256]{3,2,1,0:T(8,128)(2,1)}, bf16[2,4,256,256]{3,2,1,0:T(8,128)(2,1)}, u32[]{:S(2)}, u32[]{:S(2)}) collective-permute-start(bf16[2,4,256,256]{3,2,1,0:T(8,128)(2,1)} %collective-permute-done.15.refs_8_.refs_3_), channel_id=1, source_target_pairs={{0,16},{16,0},{1,17},{17,1},{2,18},{18,2},{3,19},{19,3},{4,20},{20... | collective-permute-start | bytes 3145736 | tf_op jit(solution)/shard_map/ppermute | solution.py:435
  91.8 26.0 %collective-permute-start.21 = (bf16[2,4,256,256]{3,2,1,0:T(8,128)(2,1)}, bf16[2,4,256,256]{3,2,1,0:T(8,128)(2,1)S(1)}, u32[]{:S(2)}, u32[]{:S(2)}) collective-permute-start(bf16[2,4,256,256]{3,2,1,0:T(8,128)(2,1)} %pad_maximum_fusion.2.refs_12_.refs_7_), channel_id=1, source_target_pairs={{0,4},{1,5},{2,6},{3,7},{4,0},{5,1},{6,2},{7,3},{8,12},{9,13},{10,... | collective-permute-start | bytes 3145736 | tf_op jit(solution)/shard_map/ppermute | solution.py:454
  92.3 25.4 %collective-permute-start.13 = (bf16[320,1024]{1,0:T(8,128)(2,1)}, bf16[320,1024]{1,0:T(8,128)(2,1)}, u32[]{:S(2)}, u32[]{:S(2)}) collective-permute-start(bf16[320,1024]{1,0:T(8,128)(2,1)} %get-tuple-element.192), channel_id=1, source_target_pairs={{0,1},{1,0},{2,3},{3,2},{4,5},{5,4},{6,7},{7,6},{8,9},{9,8},{10,11... | collective-permute-start | bytes 1966088 | tf_op jit(solution)/shard_map/ppermute | solution.py:442
  117.8 16.5 %collective-permute-start.25 = (bf16[2,4,256,256]{3,2,1,0:T(8,128)(2,1)S(1)}, bf16[2,4,256,256]{3,2,1,0:T(8,128)(2,1)}, u32[]{:S(2)}, u32[]{:S(2)}) collective-permute-start(bf16[2,4,256,256]{3,2,1,0:T(8,128)(2,1)S(1)} %collective-permute-done.21.refs_13_.refs_8_), channel_id=1, source_target_pairs={{0,16},{16,0},{1,17},{17,1},{2,18},{18,2},{3,19},{19,3},{4,20},{20... | collective-permute-start | bytes 3145736 | tf_op jit(solution)/shard_map/ppermute | solution.py:435
  131.6 15.9 %collective-permute-start.30 = (bf16[2,4,256,256]{3,2,1,0:T(8,128)(2,1)S(1)}, bf16[2,4,256,256]{3,2,1,0:T(8,128)(2,1)}, u32[]{:S(2)}, u32[]{:S(2)}) collective-permute-start(bf16[2,4,256,256]{3,2,1,0:T(8,128)(2,1)S(1)} %pad_maximum_fusion.3.refs_8_.refs_13_.refs_9_.refs_14_), channel_id=1, source_target_pairs={{0,4},{1,5},{2,6},{3,7},{4,0},{5,1},{6,2},{7,3},{8,12},{9,13},{10,... | collective-permute-start | bytes 3145736 | tf_op jit(solution)/shard_map/ppermute | solution.py:454
  150.6 24.2 %collective-permute-start.32 = (bf16[2,4,256,256]{3,2,1,0:T(8,128)(2,1)}, bf16[2,4,256,256]{3,2,1,0:T(8,128)(2,1)}, u32[]{:S(2)}, u32[]{:S(2)}) collective-permute-start(bf16[2,4,256,256]{3,2,1,0:T(8,128)(2,1)} %collective-permute-done.30.refs_9_.refs_14_.refs_10_.refs_15_), channel_id=1, source_target_pairs={{0,16},{16,0},{1,17},{17,1},{2,18},{18,2},{3,19},{19,3},{4,20},{20... | collective-permute-start | bytes 3145736 | tf_op jit(solution)/shard_map/ppermute | solution.py:435
  150.8 24.0 %collective-permute-start.36 = (bf16[2,4,256,256]{3,2,1,0:T(8,128)(2,1)}, bf16[2,4,256,256]{3,2,1,0:T(8,128)(2,1)S(1)}, u32[]{:S(2)}, u32[]{:S(2)}) collective-permute-start(bf16[2,4,256,256]{3,2,1,0:T(8,128)(2,1)} %pad_maximum_fusion.4.refs_7_.refs_2_), channel_id=1, source_target_pairs={{0,4},{1,5},{2,6},{3,7},{4,0},{5,1},{6,2},{7,3},{8,12},{9,13},{10,... | collective-permute-start | bytes 3145736 | tf_op jit(solution)/shard_map/ppermute | solution.py:454
  153.4 14.2 %collective-permute-start.33 = (bf16[4,256,256]{2,1,0:T(8,128)(2,1)S(1)}, bf16[4,256,256]{2,1,0:T(8,128)(2,1)}, u32[]{:S(2)}, u32[]{:S(2)}) collective-permute-start(bf16[4,256,256]{2,1,0:T(8,128)(2,1)S(1)} %select_bitcast_fusion.2), channel_id=1, source_target_pairs={{0,8},{1,9},{2,10},{3,11},{4,12},{5,13},{6,14},{7,15},{8,0},{9,1},... | collective-permute-start | bytes 1572872 | tf_op jit(solution)/shard_map/ppermute | solution.py:454
  155.1 19.7 %collective-permute-start.28 = (bf16[320,1024]{1,0:T(8,128)(2,1)}, bf16[320,1024]{1,0:T(8,128)(2,1)S(1)}, u32[]{:S(2)}, u32[]{:S(2)}) collective-permute-start(bf16[320,1024]{1,0:T(8,128)(2,1)} %get-tuple-element.206), channel_id=1, source_target_pairs={{0,1},{1,0},{2,3},{3,2},{4,5},{5,4},{6,7},{7,6},{8,9},{9,8},{10,11... | collective-permute-start | bytes 1966088 | tf_op jit(solution)/shard_map/ppermute | solution.py:442
  174.8 15.1 %collective-permute-start.38 = (f32[320,256]{1,0:T(8,128)S(1)}, f32[320,256]{1,0:T(8,128)S(1)}, u32[]{:S(2)}, u32[]{:S(2)}) collective-permute-start(f32[320,256]{1,0:T(8,128)S(1)} %get-tuple-element.216), channel_id=1, source_target_pairs={{0,3},{1,2},{2,1},{3,0},{4,7},{5,6},{6,5},{7,4},{8,11},{9,10},{10,... | collective-permute-start | bytes 983048 | tf_op jit(solution)/shard_map/ppermute | solution.py:430
  175.8 14.7 %collective-permute-start.40 = (bf16[2,4,256,256]{3,2,1,0:T(8,128)(2,1)S(1)}, bf16[2,4,256,256]{3,2,1,0:T(8,128)(2,1)S(1)}, u32[]{:S(2)}, u32[]{:S(2)}) collective-permute-start(bf16[2,4,256,256]{3,2,1,0:T(8,128)(2,1)S(1)} %collective-permute-done.36.refs_8_.refs_3_), channel_id=1, source_target_pairs={{0,16},{16,0},{1,17},{17,1},{2,18},{18,2},{3,19},{19,3},{4,20},{20... | collective-permute-start | bytes 3145736 | tf_op jit(solution)/shard_map/ppermute | solution.py:435
  177.8 19.2 %collective-permute-start.43 = (bf16[2,4,256,256]{3,2,1,0:T(8,128)(2,1)S(1)}, bf16[2,4,256,256]{3,2,1,0:T(8,128)(2,1)S(1)}, u32[]{:S(2)}, u32[]{:S(2)}) collective-permute-start(bf16[2,4,256,256]{3,2,1,0:T(8,128)(2,1)S(1)} %pad_maximum_fusion.5.refs_12_.refs_7_), channel_id=1, source_target_pairs={{0,4},{1,5},{2,6},{3,7},{4,0},{5,1},{6,2},{7,3},{8,12},{9,13},{10,... | collective-permute-start | bytes 3145736 | tf_op jit(solution)/shard_map/ppermute | solution.py:454
  197.7 17.5 %collective-permute-start.45 = (bf16[2,4,256,256]{3,2,1,0:T(8,128)(2,1)S(1)}, bf16[2,4,256,256]{3,2,1,0:T(8,128)(2,1)S(1)}, u32[]{:S(2)}, u32[]{:S(2)}) collective-permute-start(bf16[2,4,256,256]{3,2,1,0:T(8,128)(2,1)S(1)} %collective-permute-done.43.refs_13_.refs_8_), channel_id=1, source_target_pairs={{0,16},{16,0},{1,17},{17,1},{2,18},{18,2},{3,19},{19,3},{4,20},{20... | collective-permute-start | bytes 3145736 | tf_op jit(solution)/shard_map/ppermute | solution.py:435
  197.7 16.0 %collective-permute-start.39 = (bf16[320,1024]{1,0:T(8,128)(2,1)}, bf16[320,1024]{1,0:T(8,128)(2,1)S(1)}, u32[]{:S(2)}, u32[]{:S(2)}) collective-permute-start(bf16[320,1024]{1,0:T(8,128)(2,1)} %get-tuple-element.217), channel_id=1, source_target_pairs={{0,1},{1,0},{2,3},{3,2},{4,5},{5,4},{6,7},{7,6},{8,9},{9,8},{10,11... | collective-permute-start | bytes 1966088 | tf_op jit(solution)/shard_map/ppermute | solution.py:442
  198.4 16.8 %collective-permute-start.44 = (bf16[4,256,256]{2,1,0:T(8,128)(2,1)S(1)}, bf16[4,256,256]{2,1,0:T(8,128)(2,1)S(1)}, u32[]{:S(2)}, u32[]{:S(2)}) collective-permute-start(bf16[4,256,256]{2,1,0:T(8,128)(2,1)S(1)} %collective-permute-done.41.refs_10_.refs_5_), channel_id=1, source_target_pairs={{0,16},{16,0},{1,17},{17,1},{2,18},{18,2},{3,19},{19,3},{4,20},{20... | collective-permute-start | bytes 1572872 | tf_op jit(solution)/shard_map/ppermute | solution.py:435
  213.7 14.7 %collective-permute-start.48 = (f32[320,256]{1,0:T(8,128)S(1)}, f32[320,256]{1,0:T(8,128)S(1)}, u32[]{:S(2)}, u32[]{:S(2)}) collective-permute-start(f32[320,256]{1,0:T(8,128)S(1)} %get-tuple-element.226.refs_0_), channel_id=1, source_target_pairs={{0,1},{1,0},{2,3},{3,2},{4,5},{5,4},{6,7},{7,6},{8,9},{9,8},{10,11... | collective-permute-start | bytes 983048 | tf_op jit(solution)/shard_map/ppermute | solution.py:442
  214.5 14.1 %collective-permute-start.49 = (f32[320,256]{1,0:T(8,128)S(1)}, f32[320,256]{1,0:T(8,128)S(1)}, u32[]{:S(2)}, u32[]{:S(2)}) collective-permute-start(f32[320,256]{1,0:T(8,128)S(1)} %collective-permute-done.38.refs_1_), channel_id=1, source_target_pairs={{0,1},{1,0},{2,3},{3,2},{4,5},{5,4},{6,7},{7,6},{8,9},{9,8},{10,11... | collective-permute-start | bytes 983048 | tf_op jit(solution)/shard_map/ppermute | solution.py:442
  229.3 14.2 %collective-permute-start.50 = (bf16[320,1024]{1,0:T(8,128)(2,1)}, bf16[320,1024]{1,0:T(8,128)(2,1)S(1)}, u32[]{:S(2)}, u32[]{:S(2)}) collective-permute-start(bf16[320,1024]{1,0:T(8,128)(2,1)} %get-tuple-element.228), channel_id=1, source_target_pairs={{0,1},{1,0},{2,3},{3,2},{4,5},{5,4},{6,7},{7,6},{8,9},{9,8},{10,11... | collective-permute-start | bytes 1966088 | tf_op jit(solution)/shard_map/ppermute | solution.py:442
  271.7 19.5 %collective-permute-start.53 = (bf16[2,8,256,256]{3,2,1,0:T(8,128)(2,1)}, bf16[2,8,256,256]{3,2,1,0:T(8,128)(2,1)S(1)}, u32[]{:S(2)}, u32[]{:S(2)}) collective-permute-start(bf16[2,8,256,256]{3,2,1,0:T(8,128)(2,1)} %get-tuple-element.242), channel_id=1, source_target_pairs={{0,16},{16,0},{1,17},{17,1},{2,18},{18,2},{3,19},{19,3},{4,20},{20... | collective-permute-start | bytes 6291464 | tf_op jit(solution)/shard_map/ppermute | solution.py:435
  275.3 15.9 %collective-permute-start.52 = (bf16[320,1024]{1,0:T(8,128)(2,1)S(1)}, bf16[320,1024]{1,0:T(8,128)(2,1)S(1)}, u32[]{:S(2)}, u32[]{:S(2)}) collective-permute-start(bf16[320,1024]{1,0:T(8,128)(2,1)S(1)} %copy-done.61), channel_id=1, source_target_pairs={{0,1},{1,0},{2,3},{3,2},{4,5},{5,4},{6,7},{7,6},{8,9},{9,8},{10,11... | collective-permute-start | bytes 1966088 | tf_op jit(solution)/shard_map/ppermute | solution.py:442
  292.1 13.9 %collective-permute-start.55 = (bf16[8,256,256]{2,1,0:T(8,128)(2,1)S(1)}, bf16[8,256,256]{2,1,0:T(8,128)(2,1)S(1)}, u32[]{:S(2)}, u32[]{:S(2)}) collective-permute-start(bf16[8,256,256]{2,1,0:T(8,128)(2,1)S(1)} %add_convert_fusion.7), channel_id=1, source_target_pairs={{0,8},{1,9},{2,10},{3,11},{4,12},{5,13},{6,14},{7,15},{8,0},{9,1},... | collective-permute-start | bytes 3145736 | tf_op jit(solution)/shard_map/ppermute | solution.py:454
  306.0 15.4 %collective-permute-start.57 = (bf16[320,1024]{1,0:T(8,128)(2,1)}, bf16[320,1024]{1,0:T(8,128)(2,1)}, u32[]{:S(2)}, u32[]{:S(2)}) collective-permute-start(bf16[320,1024]{1,0:T(8,128)(2,1)} %get-tuple-element.256), channel_id=1, source_target_pairs={{0,1},{1,0},{2,3},{3,2},{4,5},{5,4},{6,7},{7,6},{8,9},{9,8},{10,11... | collective-permute-start | bytes 1966088 | tf_op jit(solution)/shard_map/ppermute | solution.py:442
  319.4 31.4 %collective-permute-start.61 = (bf16[2,8,256,256]{3,2,1,0:T(8,128)(2,1)}, bf16[2,8,256,256]{3,2,1,0:T(8,128)(2,1)S(1)}, u32[]{:S(2)}, u32[]{:S(2)}) collective-permute-start(bf16[2,8,256,256]{3,2,1,0:T(8,128)(2,1)} %shard_map.246), channel_id=1, source_target_pairs={{0,4},{1,5},{2,6},{3,7},{4,0},{5,1},{6,2},{7,3},{8,12},{9,13},{10,... | collective-permute-start | bytes 6291464 | tf_op jit(solution)/shard_map/ppermute | solution.py:454
  321.4 14.8 %collective-permute-start.60 = (bf16[4,256,256]{2,1,0:T(8,128)(2,1)S(1)}, bf16[4,256,256]{2,1,0:T(8,128)(2,1)S(1)}, u32[]{:S(2)}, u32[]{:S(2)}) collective-permute-start(bf16[4,256,256]{2,1,0:T(8,128)(2,1)S(1)} %add_convert_fusion.11), channel_id=1, source_target_pairs={{0,8},{1,9},{2,10},{3,11},{4,12},{5,13},{6,14},{7,15},{8,0},{9,1},... | collective-permute-start | bytes 1572872 | tf_op jit(solution)/shard_map/ppermute | solution.py:454
  340.2 26.7 %collective-permute-start.70 = (bf16[2,4,256,256]{3,2,1,0:T(8,128)(2,1)}, bf16[2,4,256,256]{3,2,1,0:T(8,128)(2,1)}, u32[]{:S(2)}, u32[]{:S(2)}) collective-permute-start(bf16[2,4,256,256]{3,2,1,0:T(8,128)(2,1)} %shard_map.250), channel_id=1, source_target_pairs={{0,4},{1,5},{2,6},{3,7},{4,0},{5,1},{6,2},{7,3},{8,12},{9,13},{10,... | collective-permute-start | bytes 3145736 | tf_op jit(solution)/shard_map/ppermute | solution.py:454
  360.5 20.3 %collective-permute-start.63 = (bf16[2,8,256,256]{3,2,1,0:T(8,128)(2,1)}, bf16[2,8,256,256]{3,2,1,0:T(8,128)(2,1)}, u32[]{:S(2)}, u32[]{:S(2)}) collective-permute-start(bf16[2,8,256,256]{3,2,1,0:T(8,128)(2,1)} %get-tuple-element.281), channel_id=1, source_target_pairs={{0,16},{16,0},{1,17},{17,1},{2,18},{18,2},{3,19},{19,3},{4,20},{20... | collective-permute-start | bytes 6291464 | tf_op jit(solution)/shard_map/ppermute | solution.py:435
  364.8 16.0 %collective-permute-start.62 = (bf16[320,1024]{1,0:T(8,128)(2,1)}, bf16[320,1024]{1,0:T(8,128)(2,1)S(1)}, u32[]{:S(2)}, u32[]{:S(2)}) collective-permute-start(bf16[320,1024]{1,0:T(8,128)(2,1)} %get-tuple-element.273), channel_id=1, source_target_pairs={{0,1},{1,0},{2,3},{3,2},{4,5},{5,4},{6,7},{7,6},{8,9},{9,8},{10,11... | collective-permute-start | bytes 1966088 | tf_op jit(solution)/shard_map/ppermute | solution.py:442
  370.3 45.4 %collective-permute-start.71 = (bf16[2,2,256,256]{3,2,1,0:T(8,128)(2,1)}, bf16[2,2,256,256]{3,2,1,0:T(8,128)(2,1)}, u32[]{:S(2)}, u32[]{:S(2)}) collective-permute-start(bf16[2,2,256,256]{3,2,1,0:T(8,128)(2,1)} %broadcast_select_fusion.3), channel_id=1, source_target_pairs={{0,16},{16,0},{1,17},{17,1},{2,18},{18,2},{3,19},{19,3},{4,20},{20... | collective-permute-start | bytes 1572872 | tf_op jit(solution)/shard_map/ppermute | solution.py:435
  380.8 36.5 %collective-permute-start.72 = (bf16[4,256,256]{2,1,0:T(8,128)(2,1)}, bf16[4,256,256]{2,1,0:T(8,128)(2,1)}, u32[]{:S(2)}, u32[]{:S(2)}) collective-permute-start(bf16[4,256,256]{2,1,0:T(8,128)(2,1)} %slice_bitcast_fusion.2), channel_id=1, source_target_pairs={{0,3},{1,2},{2,1},{3,0},{4,7},{5,6},{6,5},{7,4},{8,11},{9,10},{10,... | collective-permute-start | bytes 1572872 | tf_op jit(solution)/shard_map/ppermute | solution.py:430
  402.0 30.7 %collective-permute-start.74 = (bf16[2,8,256,256]{3,2,1,0:T(8,128)(2,1)}, bf16[2,8,256,256]{3,2,1,0:T(8,128)(2,1)}, u32[]{:S(2)}, u32[]{:S(2)}) collective-permute-start(bf16[2,8,256,256]{3,2,1,0:T(8,128)(2,1)} %shard_map.252), channel_id=1, source_target_pairs={{0,4},{1,5},{2,6},{3,7},{4,0},{5,1},{6,2},{7,3},{8,12},{9,13},{10,... | collective-permute-start | bytes 6291464 | tf_op jit(solution)/shard_map/ppermute | solution.py:454
  409.3 22.6 %collective-permute-start.68 = (bf16[2,4,256,256]{3,2,1,0:T(8,128)(2,1)}, bf16[2,4,256,256]{3,2,1,0:T(8,128)(2,1)}, u32[]{:S(2)}, u32[]{:S(2)}) collective-permute-start(bf16[2,4,256,256]{3,2,1,0:T(8,128)(2,1)} %get-tuple-element.302), channel_id=1, source_target_pairs={{0,16},{16,0},{1,17},{17,1},{2,18},{18,2},{3,19},{19,3},{4,20},{20... | collective-permute-start | bytes 3145736 | tf_op jit(solution)/shard_map/ppermute | solution.py:435
  415.2 16.6 %collective-permute-start.67 = (bf16[320,1024]{1,0:T(8,128)(2,1)}, bf16[320,1024]{1,0:T(8,128)(2,1)S(1)}, u32[]{:S(2)}, u32[]{:S(2)}) collective-permute-start(bf16[320,1024]{1,0:T(8,128)(2,1)} %get-tuple-element.294), channel_id=1, source_target_pairs={{0,1},{1,0},{2,3},{3,2},{4,5},{5,4},{6,7},{7,6},{8,9},{9,8},{10,11... | collective-permute-start | bytes 1966088 | tf_op jit(solution)/shard_map/ppermute | solution.py:442
  438.5 40.1 %collective-permute-start.91 = (bf16[4,256,256]{2,1,0:T(8,128)(2,1)}, bf16[4,256,256]{2,1,0:T(8,128)(2,1)}, u32[]{:S(2)}, u32[]{:S(2)}) collective-permute-start(bf16[4,256,256]{2,1,0:T(8,128)(2,1)} %fusion.1.refs_2_), channel_id=1, source_target_pairs={{0,16},{16,0},{1,17},{17,1},{2,18},{18,2},{3,19},{19,3},{4,20},{20... | collective-permute-start | bytes 1572872 | tf_op jit(solution)/shard_map/ppermute | solution.py:435
  438.5 24.0 %collective-permute-start.87 = (bf16[2,256,256]{2,1,0:T(8,128)(2,1)}, bf16[2,256,256]{2,1,0:T(8,128)(2,1)}, u32[]{:S(2)}, u32[]{:S(2)}) collective-permute-start(bf16[2,256,256]{2,1,0:T(8,128)(2,1)} %slice_bitcast_fusion.8), channel_id=1, source_target_pairs={{0,3},{1,2},{2,1},{3,0},{4,7},{5,6},{6,5},{7,4},{8,11},{9,10},{10,... | collective-permute-start | bytes 786440 | tf_op jit(solution)/shard_map/ppermute | solution.py:430
  445.3 14.5 %collective-permute-start.76 = (bf16[2,4,256,256]{3,2,1,0:T(8,128)(2,1)}, bf16[2,4,256,256]{3,2,1,0:T(8,128)(2,1)S(1)}, u32[]{:S(2)}, u32[]{:S(2)}) collective-permute-start(bf16[2,4,256,256]{3,2,1,0:T(8,128)(2,1)} %shard_map.255), channel_id=1, source_target_pairs={{0,4},{1,5},{2,6},{3,7},{4,0},{5,1},{6,2},{7,3},{8,12},{9,13},{10,... | collective-permute-start | bytes 3145736 | tf_op jit(solution)/shard_map/ppermute | solution.py:454
  453.1 14.5 %collective-permute-start.89 = (bf16[4,256,256]{2,1,0:T(8,128)(2,1)S(1)}, bf16[4,256,256]{2,1,0:T(8,128)(2,1)S(1)}, u32[]{:S(2)}, u32[]{:S(2)}) collective-permute-start(bf16[4,256,256]{2,1,0:T(8,128)(2,1)S(1)} %slice_bitcast_fusion), channel_id=1, source_target_pairs={{0,3},{1,2},{2,1},{3,0},{4,7},{5,6},{6,5},{7,4},{8,11},{9,10},{10,... | collective-permute-start | bytes 1572872 | tf_op jit(solution)/shard_map/ppermute | solution.py:430
  463.5 50.7 %collective-permute-start.88 = (bf16[2,256,256]{2,1,0:T(8,128)(2,1)S(1)}, bf16[2,256,256]{2,1,0:T(8,128)(2,1)S(1)}, u32[]{:S(2)}, u32[]{:S(2)}) collective-permute-start(bf16[2,256,256]{2,1,0:T(8,128)(2,1)S(1)} %fusion.8.refs_2_), channel_id=1, source_target_pairs={{0,16},{16,0},{1,17},{17,1},{2,18},{18,2},{3,19},{19,3},{4,20},{20... | collective-permute-start | bytes 786440 | tf_op jit(solution)/shard_map/ppermute | solution.py:435
  483.4 23.1 %collective-permute-start.84 = (f32[25,256]{1,0:T(8,128)S(1)}, f32[25,256]{1,0:T(8,128)S(1)}, u32[]{:S(2)}, u32[]{:S(2)}) collective-permute-start(f32[25,256]{1,0:T(8,128)S(1)} %bitcast.218), channel_id=1, source_target_pairs={{0,3},{1,2},{2,1},{3,0},{4,7},{5,6},{6,5},{7,4},{8,11},{9,10},{10,... | collective-permute-start | bytes 76808 | tf_op jit(solution)/shard_map/ppermute | solution.py:430
  484.4 22.1 %collective-permute-start.85 = (bf16[2,256,256]{2,1,0:T(8,128)(2,1)S(1)}, bf16[2,256,256]{2,1,0:T(8,128)(2,1)S(1)}, u32[]{:S(2)}, u32[]{:S(2)}) collective-permute-start(bf16[2,256,256]{2,1,0:T(8,128)(2,1)S(1)} %slice_bitcast_fusion.10), channel_id=1, source_target_pairs={{0,3},{1,2},{2,1},{3,0},{4,7},{5,6},{6,5},{7,4},{8,11},{9,10},{10,... | collective-permute-start | bytes 786440 | tf_op jit(solution)/shard_map/ppermute | solution.py:430
  (125 other events, 1045.4 us)

commit v4 on v3

--- a/solution.py
+++ b/solution.py
@@ -508,8 +508,7 @@
 
 def flip_tiles(shard, first_core):
     half = shard.shape[0] // 2
-    got = flip_col(jnp.where(first_core, shard[:half], shard[half:]))
-    return got, swap_core(got)
+    return flip_col(jnp.where(first_core, shard[:half], shard[half:]))
 
 
 def join_tiles(shard, got, other, first_core):
@@ -658,11 +657,12 @@
             else:
                 shards[place] = gated(down_weight[layer]).reshape(4, 256, 256)
             flips[place] = flip_tiles(shards[place], first_core)
-            return flips[place][0]
+            return flips[place]
 
         def near(place):
-            owns[place] = join_tiles(shards[place], *flips[place], first_core)
-            nears[place] = cross_row(gated(owns[place]), 1, 2)
+            got = gated(flips[place])
+            owns[place] = join_tiles(shards[place], got, swap_core(got), first_core)
+            nears[place] = cross_row(owns[place], 1, 2)
             return nears[place]
 
         def near_swap(place):
@@ -691,14 +691,15 @@
         states_flipped = flip_col(gated(states_other))
         shifts_own = all_shifts(gated(states_own))
         small_flipped = flip_col(gated(small))
-        gate = [near(0), states_flipped, small_flipped, *shifts_own]
+        token_total = count_step(gated(token_total), *total_steps[0])
+        gate = [near(0), states_flipped, small_flipped, token_total, *shifts_own]
         small_pair = jnp.stack([small, gated(small_flipped)])
         feature_all = order_blocks(small_pair[:, :feature_rows])
         shifts_flipped = all_shifts(gated(states_flipped))
-        token_total = count_step(gated(token_total), *total_steps[0])
+        token_total = count_step(gated(token_total), *total_steps[1])
         gate = [far(0), flip(1), near_swap(0), token_total, feature_all, *shifts_flipped]
         states_blocks = all_blocks(states_own, shifts_own, states_flipped, shifts_flipped)
-        token_total = count_step(gated(token_total), *total_steps[1])
+        token_total = count_step(gated(token_total), *total_steps[2])
         first_slot = [near(1), flip(2), token_total]
         far_swap(0)
         in_full[0], proj_full[0] = (pieces(0), 0), (pieces(0), 3)
@@ -887,8 +888,7 @@
         if layer == 0:
             if tiled:
                 gate = [wide, *first_slot]
-                token_total = count_step(gated(token_total), *total_steps[2])
-                second_slot = [far(1), near(2), flip(3), near_swap(1), token_total]
+                second_slot = [far(1), near(2), flip(3), near_swap(1)]
             wide, arrived = group_total(wide, low)
             token_total = token_total.astype(wide_type)
             factor = 2.0 * token_rows * core_count * row_count / token_total
@@ -961,7 +961,7 @@
             if layer == LAYERS - 1:
                 gate = [low, output_halves[0]]
             else:
-                gate = [low, far_moved, near_moved]
+                gate = [low, far_moved]
         wide, arrived = group_total(wide, gated(low))
         if tiled:
             tiles = weight_tiles(
@@ -999,11 +999,18 @@
             near_sent = near_add(near_part, near_arrived, far_moved)
             if layer < LAYERS - 1:
                 gate = [*gate, near_sent]
+            else:
+                received = gated(jnp.concatenate(output_halves))
             tiles = weight_tiles(
                 attend_weight_kernel, 4, 5.5, normed_one, gated(triple), mixed, grad_low
             )
             way.append(scatter_first(tiles))
             gate = [arrived, *tiles, *way[-1], near_sent]
+            if layer == LAYERS - 1:
+                output_share = join_rows(final, received)
+                residue = (output_share - teacher_wide) * all_mask
+                squared = jnp.sum(residue * residue)
+                gate = gate + [squared]
             if layer < LAYERS - 1:
                 feed_parts = [add(part[0], flip_moved)]
                 part = scatter_third(way[-3][0], near_moved, first_core)
@@ -1013,6 +1020,10 @@
             arrived = gated(arrived)
             far_moved = cross_row(gated(way[-1][3]), 2, 1)
         else:
+            if layer == LAYERS - 1:
+                output_share = join_rows(final, jnp.concatenate(output_halves))
+                residue = (output_share - teacher_wide) * all_mask
+                squared = jnp.sum(residue * residue)
 
             def product(spec, left, right):
                 return jnp.einsum(spec, left, right, preferred_element_type=wide_type)
@@ -1091,10 +1102,6 @@
         input_share = share_rows(grad, low_type)
         up_grad, down_grad = jnp.stack(up_grads), jnp.stack(down_grads)
         in_grad, proj_grad = jnp.stack(in_grads), jnp.stack(proj_grads)
-    output_share = join_rows(gated(final), gated(jnp.concatenate(output_halves)))
-    residue = (output_share - teacher_wide) * all_mask
-    squared = jnp.sum(residue * residue)
-
     feature_parts = jnp.concatenate(
         [part for layer in range(LAYERS) for part in feature_grads[layer]]
     )

time: 529 us -> 512 us (0.968)
  starting transfers between devices: 133 us -> 107 us
  waiting for transfers between devices: 149 us -> 164 us
    ppermute x13, waiting for transfers between devices: 60.2 us -> 72.5 us  [group_shift(): return lax.ppermute(value, 'col', pairs)]
    ppermute x13, starting transfers between devices: 17.2 us -> 7.26 us  [group_shift(): return lax.ppermute(value, 'col', pairs)]
    ppermute x20, waiting for transfers between devices: 39.3 us -> 48.7 us  [cross_row(): return lax.ppermute(value, ('dp', 'row', 'col'), pairs)]
    ppermute x20, starting transfers between devices: 19.7 us -> 12.4 us  [cross_row(): return lax.ppermute(value, ('dp', 'row', 'col'), pairs)]
    ppermute x17, waiting for transfers between devices: 36.8 us -> 29.5 us  [flip_col(): lax.ppermute(value, 'col', [(i, count - 1 - i) for i in range(count)])]
    ppermute x3, starting transfers between devices: 10.8 us -> 4.34 us  [count_step(): lax.ppermute(value, axis, [(i, i ^ step) for i in range(size)])]
    unnamed x178 -> x188, local copies, waits for them, and re-layouts: 15.1 us -> 15.8 us
  transfers between devices with their start and end apart: 92 -> 92, of which waited for: 33 -> 35; matrix products, arithmetic and copies ran while one was open for 11% -> 10% of each run, Pallas kernels for 26% -> 27%
where the time goes in v4:
time: 512 us; the launch traced here: 502 us
  waiting for transfers between devices  164 us (32%)
  Pallas kernels  152 us (30%)
  starting transfers between devices  107 us (21%)
  other arithmetic  35.5 us (7%)
  local copies, waits for them, and re-layouts  34.2 us (7%)
  between operations  9.35 us (2%)
    pallas_call x17, Pallas kernels, call(): pl.pallas_call(kernel, out_shape=outs, in_specs=specs, out_specs=[VMEM] *...  137 us
    ppermute x13, waiting for transfers between devices, group_shift(): return lax.ppermute(value, 'col', pairs)  72.5 us
    ppermute x20, waiting for transfers between devices, cross_row(): return lax.ppermute(value, ('dp', 'row', 'col'), pairs)  48.7 us
    ppermute x34, starting transfers between devices, swap_core(): return lax.ppermute(value, 'dp', [(i, count - 1 - i) for i in range(count)])  36.3 us
    ppermute x17, starting transfers between devices, flip_col(): lax.ppermute(value, 'col', [(i, count - 1 - i) for i in range(count)])  33.4 us
    ppermute x17, waiting for transfers between devices, flip_col(): lax.ppermute(value, 'col', [(i, count - 1 - i) for i in range(count)])  29.5 us
    unnamed x188, local copies, waits for them, and re-layouts  15.8 us
    convert_element_type x16, other arithmetic, add(): return (left.astype(wide_type) + right.astype(wide_type)).astype(low_type)  14.6 us
  transfers between devices with their start and end apart: 92, of which 35 were waited for; matrix products, arithmetic and copies ran while one was open for 10% of the time, Pallas kernels for 27%

profile of v4, /device:TPU:1, one launch (start us, length us, event | category | flops | bytes accessed | tf_op | source)
XLA Modules:
  0.0 501.6 jit_solution(7219914086012154557)
XLA Ops:
  3.8 4.2 collective-permute-start
  8.0 6.1 %collective-permute-done = bf16[2,256,256]{2,1,0:T(8,128)(2,1)S(1)} collective-permute-done((bf16[2,256,256]{2,1,0:T(8,128)(2,1)S(1)}, bf16[2,256,256]{2,1,0:T(8,128)(2,1)S(1)}, u32[]{:S(2)}, u32[]{:S(2)}) %collective-permute-start) | collective-permute-done | bytes 262176 | tf_op jit(solution)/shard_map/ppermute | solution.py:430
  22.2 3.3 collective-permute-start.1
  25.4 3.0 collective-permute-start.2
  36.1 4.0 collective-permute-done.5
  47.7 3.2 collective-permute-start.11
  52.5 4.5 collective-permute-done.11
  57.0 8.1 %collective-permute-done.7.refs_3_ = f32[320,256]{1,0:T(8,128)} collective-permute-done((f32[320,256]{1,0:T(8,128)}, f32[320,256]{1,0:T(8,128)}, u32[]{:S(2)}, u32[]{:S(2)}) %collective-permute-start.7) | collective-permute-done | bytes 327712 | tf_op jit(solution)/shard_map/ppermute | solution.py:442
  73.2 10.4 %shard_map.237 = (f32[320,1024]{1,0:T(8,128)}, bf16[320,1024]{1,0:T(8,128)(2,1)}, bf16[320,512]{1,0:T(8,128)(2,1)}, bf16[320,512]{1,0:T(8,128)(2,1)}, bf16[320,5...) custom-call(s32[10]{0:T(128)} %concatenate.29.meta, ...), custom_call_target="tpu_custom_call" | custom-call | flops 96599998464 | bytes 1048576 | tf_op jit(solution)/shard_map/pallas_call | solution.py:748
  95.9 13.4 %collective-permute-done.14.refs_2_ = bf16[320,1024]{1,0:T(8,128)(2,1)} collective-permute-done((bf16[320,1024]{1,0:T(8,128)(2,1)}, bf16[320,1024]{1,0:T(8,128)(2,1)}, u32[]{:S(2)}, u32[]{:S(2)}) %collective-permute-start.14) | collective-permute-done | bytes 655392 | tf_op jit(solution)/shard_map/ppermute | solution.py:442
  109.3 5.7 %collective-permute-done.23 = bf16[2,256,256]{2,1,0:T(8,128)(2,1)S(1)} collective-permute-done((bf16[2,256,256]{2,1,0:T(8,128)(2,1)S(1)}, bf16[2,256,256]{2,1,0:T(8,128)(2,1)S(1)}, u32[]{:S(2)}, u32[]{:S(2)}) %collective-permute-start.23) | collective-permute-done | bytes 262176 | tf_op jit(solution)/shard_map/ppermute | solution.py:430
  119.7 5.0 %collective-permute-done.26.refs_15_.refs_10_ = bf16[4,256,256]{2,1,0:T(8,128)(2,1)} collective-permute-done((bf16[4,256,256]{2,1,0:T(8,128)(2,1)S(1)}, bf16[4,256,256]{2,1,0:T(8,128)(2,1)}, u32[]{:S(2)}, u32[]{:S(2)}) %collective-permute-start.26) | collective-permute-done | bytes 524320 | tf_op jit(solution)/shard_map/ppermute | solution.py:454
  130.2 12.1 %shard_map.238 = (f32[320,1024]{1,0:T(8,128)}, bf16[320,1024]{1,0:T(8,128)(2,1)}, bf16[320,2048]{1,0:T(8,128)(2,1)}, bf16[320,2048]{1,0:T(8,128)(2,1)}, f32[320,1024]{1,0:T(8,128)}, /*index=5*/bf16[320,1024]{1,0:T(8,128)(2,1)}) custom-call(s32[10]{0:T(128)} %concatenate.29.meta, f32[320,1024]{1,0:T(8,128)} %get-tuple-element.190.refs_0_.inputs, ...), custom_call_target="tpu_custom_call" | custom-call | flops 110399995904 | bytes 1048576 | tf_op jit(solution)/shard_map/pallas_call | solution.py:748
  151.0 11.5 %collective-permute-done.33.refs_11_.refs_16_.refs_12_.refs_17_ = bf16[4,256,256]{2,1,0:T(8,128)(2,1)} collective-permute-done((bf16[4,256,256]{2,1,0:T(8,128)(2,1)S(1)}, bf16[4,256,256]{2,1,0:T(8,128)(2,1)}, u32[]{:S(2)}, u32[]{:S(2)}) %collective-permute-start.33) | collective-permute-done | bytes 524320 | tf_op jit(solution)/shard_map/ppermute | solution.py:454
  163.3 4.9 collective-permute-done.37
  174.4 11.1 %shard_map.239 = (f32[320,1024]{1,0:T(8,128)}, bf16[320,1024]{1,0:T(8,128)(2,1)}, bf16[320,512]{1,0:T(8,128)(2,1)}, bf16[320,512]{1,0:T(8,128)(2,1)}, bf16[320,5...) custom-call(s32[10]{0:T(128)} %concatenate.29.meta, ...), custom_call_target="tpu_custom_call" | custom-call | flops 96599998464 | bytes 1048576 | tf_op jit(solution)/shard_map/pallas_call | solution.py:748
  185.5 6.7 %collective-permute-done.43.refs_13_.refs_8_ = bf16[2,4,256,256]{3,2,1,0:T(8,128)(2,1)S(1)} collective-permute-done((bf16[2,4,256,256]{3,2,1,0:T(8,128)(2,1)S(1)}, bf16[2,4,256,256]{3,2,1,0:T(8,128)(2,1)S(1)}, u32[]{:S(2)}, u32[]{:S(2)}) %collective-permute-start.43) | collective-permute-done | bytes 1048608 | tf_op jit(solution)/shard_map/ppermute | solution.py:454
  193.4 7.3 %collective-permute-done.46.refs_15_.refs_10_ = bf16[4,256,256]{2,1,0:T(8,128)(2,1)S(1)} collective-permute-done((bf16[4,256,256]{2,1,0:T(8,128)(2,1)S(1)}, bf16[4,256,256]{2,1,0:T(8,128)(2,1)S(1)}, u32[]{:S(2)}, u32[]{:S(2)}) %collective-permute-start.46) | collective-permute-done | bytes 524320 | tf_op jit(solution)/shard_map/ppermute | solution.py:454
  202.3 7.6 %collective-permute-done.39.refs_2_ = bf16[320,1024]{1,0:T(8,128)(2,1)S(1)} collective-permute-done((bf16[320,1024]{1,0:T(8,128)(2,1)}, bf16[320,1024]{1,0:T(8,128)(2,1)S(1)}, u32[]{:S(2)}, u32[]{:S(2)}) %collective-permute-start.39) | collective-permute-done | bytes 655392 | tf_op jit(solution)/shard_map/ppermute | solution.py:442
  212.8 11.9 %shard_map.240 = (f32[320,1024]{1,0:T(8,128)}, bf16[320,1024]{1,0:T(8,128)(2,1)}, bf16[320,2048]{1,0:T(8,128)(2,1)}, bf16[320,2048]{1,0:T(8,128)(2,1)}, f32[320,1024]{1,0:T(8,128)}, /*index=5*/bf16[320,1024]{1,0:T(8,128)(2,1)}) custom-call(s32[10]{0:T(128)} %concatenate.29.meta, f32[320,1024]{1,0:T(8,128)} %get-tuple-element.210.refs_0_.inputs, ...), custom_call_target="tpu_custom_call" | custom-call | flops 110399995904 | bytes 1048576 | tf_op jit(solution)/shard_map/pallas_call | solution.py:748
  226.5 13.7 %collective-permute-done.50.arrived = bf16[320,1024]{1,0:T(8,128)(2,1)S(1)} collective-permute-done((bf16[320,1024]{1,0:T(8,128)(2,1)}, bf16[320,1024]{1,0:T(8,128)(2,1)S(1)}, u32[]{:S(2)}, u32[]{:S(2)}) %collective-permute-start.50) | collective-permute-done | bytes 655392 | tf_op jit(solution)/shard_map/ppermute | solution.py:442
  241.1 4.4 shard_map.241
  248.2 9.8 %shard_map.242 = (f32[320,1024]{1,0:T(8,128)}, bf16[320,1024]{1,0:T(8,128)(2,1)}, bf16[320,2048]{1,0:T(8,128)(2,1)}, f32[1,1024]{1,0:T(1,128)}, f32[1,2048]{1,0:...) custom-call(s32[10]{0:T(128)} %concatenate.29.meta, f32[320,1024]{1,0:T(8,128)} %get-tuple-element.228.refs_0_, ...), custom_call_target="tpu_custom_call" | custom-call | flops 92000002048 | bytes 1048576 | tf_op jit(solution)/shard_map/pallas_call | solution.py:748
  258.0 9.0 %shard_map.243 = (bf16[2,8,256,256]{3,2,1,0:T(8,128)(2,1)}, bf16[2,8,256,256]{3,2,1,0:T(8,128)(2,1)}, bf16[2,8,256,256]{3,2,1,0:T(8,128)(2,1)}, bf16[8,256,256]{2,1,0:T(8,128)(2,1)}, bf16[8,256,256]{2,1,0:T(8,128)(2,1)}) custom-call(s32[10]{0:T(128)} %concatenate.29.meta, bf16[320,1024]{1,0:T(8,128)(2,1)} %get-tuple-element.234.normed, ...), custom_call_target="tpu_custom_call" | custom-call | flops 82800001024 | bytes 1048576 | tf_op jit(solution)/shard_map/pallas_call | solution.py:748
  267.0 3.0 collective-permute-start.53
  270.9 4.7 collective-permute-done.54
  277.0 9.3 %collective-permute-done.52.refs_1_ = bf16[320,1024]{1,0:T(8,128)(2,1)} collective-permute-done((bf16[320,1024]{1,0:T(8,128)(2,1)}, bf16[320,1024]{1,0:T(8,128)(2,1)}, u32[]{:S(2)}, u32[]{:S(2)}) %collective-permute-start.52) | collective-permute-done | bytes 655392 | tf_op jit(solution)/shard_map/ppermute | solution.py:442
  288.5 11.7 %shard_map.244 = (f32[320,1024]{1,0:T(8,128)}, bf16[320,1024]{1,0:T(8,128)(2,1)}, f32[1,1024]{1,0:T(1,128)}, f32[1,1024]{1,0:T(1,128)}, f32[1,1024]{1,0:T(1,128)...) custom-call(s32[10]{0:T(128)} %concatenate.29.meta, ...), custom_call_target="tpu_custom_call" | custom-call | flops 110399995904 | bytes 1048576 | tf_op jit(solution)/shard_map/pallas_call | solution.py:748
  302.4 5.7 %shard_map.245 = (bf16[2,4,256,256]{3,2,1,0:T(8,128)(2,1)}, bf16[2,4,256,256]{3,2,1,0:T(8,128)(2,1)}, bf16[2,4,256,256]{3,2,1,0:T(8,128)(2,1)}, bf16[4,256,256]{2,1,0:T(8,128)(2,1)}, bf16[4,256,256]{2,1,0:T(8,128)(2,1)}) custom-call(s32[10]{0:T(128)} %concatenate.29.meta, bf16[320,1024]{1,0:T(8,128)(2,1)} %get-tuple-element.256.normed, ...), custom_call_target="tpu_custom_call" | custom-call | flops 50600001536 | bytes 1048576 | tf_op jit(solution)/shard_map/pallas_call | solution.py:748
  310.6 4.3 shard_map.246
  319.5 4.3 shard_map.247
  323.8 9.8 %shard_map.248 = (f32[320,1024]{1,0:T(8,128)}, bf16[320,1024]{1,0:T(8,128)(2,1)}, bf16[320,2048]{1,0:T(8,128)(2,1)}, f32[1,1024]{1,0:T(1,128)}, f32[1,2048]{1,0:...) custom-call(s32[10]{0:T(128)} %concatenate.29.meta, f32[320,1024]{1,0:T(8,128)} %get-tuple-element.268.refs_0_, ...), custom_call_target="tpu_custom_call" | custom-call | flops 92000002048 | bytes 1048576 | tf_op jit(solution)/shard_map/pallas_call | solution.py:748
  334.5 3.1 shard_map.250
  338.2 9.1 %shard_map.249 = (bf16[2,8,256,256]{3,2,1,0:T(8,128)(2,1)}, bf16[2,8,256,256]{3,2,1,0:T(8,128)(2,1)}, bf16[2,8,256,256]{3,2,1,0:T(8,128)(2,1)}, bf16[8,256,256]{2,1,0:T(8,128)(2,1)}, bf16[8,256,256]{2,1,0:T(8,128)(2,1)}) custom-call(s32[10]{0:T(128)} %concatenate.29.meta, bf16[320,1024]{1,0:T(8,128)(2,1)} %get-tuple-element.274.normed, ...), custom_call_target="tpu_custom_call" | custom-call | flops 82800001024 | bytes 1048576 | tf_op jit(solution)/shard_map/pallas_call | solution.py:748
  353.4 3.9 collective-permute-done.70
  362.3 5.5 %collective-permute-done.61.refs_1_ = bf16[320,1024]{1,0:T(8,128)(2,1)S(1)} collective-permute-done((bf16[320,1024]{1,0:T(8,128)(2,1)S(1)}, bf16[320,1024]{1,0:T(8,128)(2,1)S(1)}, u32[]{:S(2)}, u32[]{:S(2)}) %collective-permute-start.61) | collective-permute-done | bytes 655392 | tf_op jit(solution)/shard_map/ppermute | solution.py:442
  370.9 11.7 %shard_map.251 = (f32[320,1024]{1,0:T(8,128)}, bf16[320,1024]{1,0:T(8,128)(2,1)}, f32[1,1024]{1,0:T(1,128)}, f32[1,1024]{1,0:T(1,128)}, f32[1,1024]{1,0:T(1,128)...) custom-call(s32[10]{0:T(128)} %concatenate.29.meta, ...), custom_call_target="tpu_custom_call" | custom-call | flops 110399995904 | bytes 1048576 | tf_op jit(solution)/shard_map/pallas_call | solution.py:748
  384.7 3.9 shard_map.252
  389.0 5.4 %shard_map.253 = (bf16[2,4,256,256]{3,2,1,0:T(8,128)(2,1)}, bf16[2,4,256,256]{3,2,1,0:T(8,128)(2,1)}, bf16[2,4,256,256]{3,2,1,0:T(8,128)(2,1)}, bf16[4,256,256]{2,1,0:T(8,128)(2,1)}, bf16[4,256,256]{2,1,0:T(8,128)(2,1)}) custom-call(s32[10]{0:T(128)} %concatenate.29.meta, bf16[320,1024]{1,0:T(8,128)(2,1)} %get-tuple-element.295.normed, ...), custom_call_target="tpu_custom_call" | custom-call | flops 50600001536 | bytes 1048576 | tf_op jit(solution)/shard_map/pallas_call | solution.py:748
  394.5 3.5 collective-permute-start.68
  406.6 11.8 %collective-permute-done.67.arrived = bf16[320,1024]{1,0:T(8,128)(2,1)S(1)} collective-permute-done((bf16[320,1024]{1,0:T(8,128)(2,1)S(1)}, bf16[320,1024]{1,0:T(8,128)(2,1)S(1)}, u32[]{:S(2)}, u32[]{:S(2)}) %collective-permute-start.67) | collective-permute-done | bytes 655392 | tf_op jit(solution)/shard_map/ppermute | solution.py:442
  427.1 3.1 shard_map.255
  432.5 4.4 shard_map.254
  439.7 6.3 %collective-permute-done.76 = bf16[2,4,256,256]{3,2,1,0:T(8,128)(2,1)S(1)} collective-permute-done((bf16[2,4,256,256]{3,2,1,0:T(8,128)(2,1)}, bf16[2,4,256,256]{3,2,1,0:T(8,128)(2,1)S(1)}, u32[]{:S(2)}, u32[]{:S(2)}) %collective-permute-start.76) | collective-permute-done | bytes 1048608 | tf_op jit(solution)/shard_map/ppermute | solution.py:454
  455.0 4.3 collective-permute-done.83
  464.8 3.9 shard_map.257
  472.8 9.2 %collective-permute-start.81 = (f32[]{:T(128)}, f32[]{:T(128)}, u32[]{:S(2)}, u32[]{:S(2)}) collective-permute-start(f32[]{:T(128)} %bitcast.86), channel_id=1, source_target_pairs={{0,1},{1,0},{2,3},{3,2},{4,5},{5,4},{6,7},{7,6},{8,9},{9,8},{10,11... | collective-permute-start | bytes 20 | tf_op jit(solution)/shard_map/ppermute | solution.py:469
  488.5 5.4 %collective-permute-start.86 = (bf16[2,256,256]{2,1,0:T(8,128)(2,1)S(1)}, bf16[2,256,256]{2,1,0:T(8,128)(2,1)S(1)}, u32[]{:S(2)}, u32[]{:S(2)}) collective-permute-start(bf16[2,256,256]{2,1,0:T(8,128)(2,1)S(1)} %fusion.9.refs_0_), channel_id=1, source_target_pairs={{0,16},{16,0},{1,17},{17,1},{2,18},{18,2},{3,19},{19,3},{4,20},{20... | collective-permute-start | bytes 786440 | tf_op jit(solution)/shard_map/ppermute | solution.py:435
  (468 shorter events, 164.0 us)
Async XLA Ops:
  17.7 23.4 %collective-permute-start.4 = (bf16[2,4,256,256]{3,2,1,0:T(8,128)(2,1)}, bf16[2,4,256,256]{3,2,1,0:T(8,128)(2,1)}, u32[]{:S(2)}, u32[]{:S(2)}) collective-permute-start(bf16[2,4,256,256]{3,2,1,0:T(8,128)(2,1)} %pad_maximum_fusion.refs_8_.refs_13_.refs_9_.refs_14_), channel_id=1, source_target_pairs={{0,4},{1,5},{2,6},{3,7},{4,0},{5,1},{6,2},{7,3},{8,12},{9,13},{10,... | collective-permute-start | bytes 3145736 | tf_op jit(solution)/shard_map/ppermute | solution.py:454
  22.2 17.9 %collective-permute-start.1 = (f32[320,256]{1,0:T(8,128)}, f32[320,256]{1,0:T(8,128)S(1)}, u32[]{:S(2)}, u32[]{:S(2)}) collective-permute-start(f32[320,256]{1,0:T(8,128)} %get-tuple-element.179), channel_id=1, source_target_pairs={{0,3},{1,2},{2,1},{3,0},{4,7},{5,6},{6,5},{7,4},{8,11},{9,10},{10,... | collective-permute-start | bytes 983048 | tf_op jit(solution)/shard_map/ppermute | solution.py:430
  25.4 15.7 %collective-permute-start.2 = (f32[320,256]{1,0:T(8,128)}, f32[320,256]{1,0:T(8,128)}, u32[]{:S(2)}, u32[]{:S(2)}) collective-permute-start(f32[320,256]{1,0:T(8,128)} %get-tuple-element.180.refs_0_), channel_id=1, source_target_pairs={{0,1},{1,0},{2,3},{3,2},{4,5},{5,4},{6,7},{7,6},{8,9},{9,8},{10,11... | collective-permute-start | bytes 983048 | tf_op jit(solution)/shard_map/ppermute | solution.py:442
  42.5 22.6 %collective-permute-start.9 = (bf16[2,4,256,256]{3,2,1,0:T(8,128)(2,1)}, bf16[2,4,256,256]{3,2,1,0:T(8,128)(2,1)}, u32[]{:S(2)}, u32[]{:S(2)}) collective-permute-start(bf16[2,4,256,256]{3,2,1,0:T(8,128)(2,1)} %collective-permute-done.4.refs_9_.refs_14_.refs_10_.refs_15_), channel_id=1, source_target_pairs={{0,16},{16,0},{1,17},{17,1},{2,18},{18,2},{3,19},{19,3},{4,20},{20... | collective-permute-start | bytes 3145736 | tf_op jit(solution)/shard_map/ppermute | solution.py:435
  50.9 14.2 %collective-permute-start.7 = (f32[320,256]{1,0:T(8,128)}, f32[320,256]{1,0:T(8,128)}, u32[]{:S(2)}, u32[]{:S(2)}) collective-permute-start(f32[320,256]{1,0:T(8,128)} %copy-done.81), channel_id=1, source_target_pairs={{0,1},{1,0},{2,3},{3,2},{4,5},{5,4},{6,7},{7,6},{8,9},{9,8},{10,11... | collective-permute-start | bytes 983048 | tf_op jit(solution)/shard_map/ppermute | solution.py:442
  50.9 14.2 %collective-permute-start.10 = (bf16[4,256,256]{2,1,0:T(8,128)(2,1)S(1)}, bf16[4,256,256]{2,1,0:T(8,128)(2,1)}, u32[]{:S(2)}, u32[]{:S(2)}) collective-permute-start(bf16[4,256,256]{2,1,0:T(8,128)(2,1)S(1)} %select_bitcast_fusion.5), channel_id=1, source_target_pairs={{0,8},{1,9},{2,10},{3,11},{4,12},{5,13},{6,14},{7,15},{8,0},{9,1},... | collective-permute-start | bytes 1572872 | tf_op jit(solution)/shard_map/ppermute | solution.py:454
  67.4 16.3 %collective-permute-start.17 = (bf16[2,256,256]{2,1,0:T(8,128)(2,1)S(1)}, bf16[2,256,256]{2,1,0:T(8,128)(2,1)S(1)}, u32[]{:S(2)}, u32[]{:S(2)}) collective-permute-start(bf16[2,256,256]{2,1,0:T(8,128)(2,1)S(1)} %bitcast.214), channel_id=1, source_target_pairs={{0,3},{1,2},{2,1},{3,0},{4,7},{5,6},{6,5},{7,4},{8,11},{9,10},{10,... | collective-permute-start | bytes 786440 | tf_op jit(solution)/shard_map/ppermute | solution.py:430
  71.9 14.1 %collective-permute-start.16 = (bf16[2,4,256,256]{3,2,1,0:T(8,128)(2,1)S(1)}, bf16[2,4,256,256]{3,2,1,0:T(8,128)(2,1)}, u32[]{:S(2)}, u32[]{:S(2)}) collective-permute-start(bf16[2,4,256,256]{3,2,1,0:T(8,128)(2,1)S(1)} %pad_maximum_fusion.1.refs_7_.refs_2_), channel_id=1, source_target_pairs={{0,4},{1,5},{2,6},{3,7},{4,0},{5,1},{6,2},{7,3},{8,12},{9,13},{10,... | collective-permute-start | bytes 3145736 | tf_op jit(solution)/shard_map/ppermute | solution.py:454
  88.4 26.6 %collective-permute-start.19 = (bf16[2,4,256,256]{3,2,1,0:T(8,128)(2,1)}, bf16[2,4,256,256]{3,2,1,0:T(8,128)(2,1)}, u32[]{:S(2)}, u32[]{:S(2)}) collective-permute-start(bf16[2,4,256,256]{3,2,1,0:T(8,128)(2,1)} %collective-permute-done.16.refs_8_.refs_3_), channel_id=1, source_target_pairs={{0,16},{16,0},{1,17},{17,1},{2,18},{18,2},{3,19},{19,3},{4,20},{20... | collective-permute-start | bytes 3145736 | tf_op jit(solution)/shard_map/ppermute | solution.py:435
  91.1 23.9 %collective-permute-start.22 = (bf16[2,4,256,256]{3,2,1,0:T(8,128)(2,1)}, bf16[2,4,256,256]{3,2,1,0:T(8,128)(2,1)}, u32[]{:S(2)}, u32[]{:S(2)}) collective-permute-start(bf16[2,4,256,256]{3,2,1,0:T(8,128)(2,1)} %pad_maximum_fusion.2.refs_12_.refs_7_), channel_id=1, source_target_pairs={{0,4},{1,5},{2,6},{3,7},{4,0},{5,1},{6,2},{7,3},{8,12},{9,13},{10,... | collective-permute-start | bytes 3145736 | tf_op jit(solution)/shard_map/ppermute | solution.py:454
  92.3 16.9 %collective-permute-start.14 = (bf16[320,1024]{1,0:T(8,128)(2,1)}, bf16[320,1024]{1,0:T(8,128)(2,1)}, u32[]{:S(2)}, u32[]{:S(2)}) collective-permute-start(bf16[320,1024]{1,0:T(8,128)(2,1)} %get-tuple-element.192), channel_id=1, source_target_pairs={{0,1},{1,0},{2,3},{3,2},{4,5},{5,4},{6,7},{7,6},{8,9},{9,8},{10,11... | collective-permute-start | bytes 1966088 | tf_op jit(solution)/shard_map/ppermute | solution.py:442
  93.6 21.4 %collective-permute-start.20 = (bf16[4,256,256]{2,1,0:T(8,128)(2,1)S(1)}, bf16[4,256,256]{2,1,0:T(8,128)(2,1)}, u32[]{:S(2)}, u32[]{:S(2)}) collective-permute-start(bf16[4,256,256]{2,1,0:T(8,128)(2,1)S(1)} %select_bitcast_fusion.4), channel_id=1, source_target_pairs={{0,8},{1,9},{2,10},{3,11},{4,12},{5,13},{6,14},{7,15},{8,0},{9,1},... | collective-permute-start | bytes 1572872 | tf_op jit(solution)/shard_map/ppermute | solution.py:454
  93.9 21.1 %collective-permute-start.23 = (bf16[2,256,256]{2,1,0:T(8,128)(2,1)S(1)}, bf16[2,256,256]{2,1,0:T(8,128)(2,1)S(1)}, u32[]{:S(2)}, u32[]{:S(2)}) collective-permute-start(bf16[2,256,256]{2,1,0:T(8,128)(2,1)S(1)} %fusion.11), channel_id=1, source_target_pairs={{0,3},{1,2},{2,1},{3,0},{4,7},{5,6},{6,5},{7,4},{8,11},{9,10},{10,... | collective-permute-start | bytes 786440 | tf_op jit(solution)/shard_map/ppermute | solution.py:430
  126.4 15.8 %collective-permute-start.31 = (bf16[2,256,256]{2,1,0:T(8,128)(2,1)S(1)}, bf16[2,256,256]{2,1,0:T(8,128)(2,1)S(1)}, u32[]{:S(2)}, u32[]{:S(2)}) collective-permute-start(bf16[2,256,256]{2,1,0:T(8,128)(2,1)S(1)} %slice_select_fusion), channel_id=1, source_target_pairs={{0,3},{1,2},{2,1},{3,0},{4,7},{5,6},{6,5},{7,4},{8,11},{9,10},{10,... | collective-permute-start | bytes 786440 | tf_op jit(solution)/shard_map/ppermute | solution.py:430
  128.3 14.1 %collective-permute-start.30 = (bf16[2,4,256,256]{3,2,1,0:T(8,128)(2,1)S(1)}, bf16[2,4,256,256]{3,2,1,0:T(8,128)(2,1)}, u32[]{:S(2)}, u32[]{:S(2)}) collective-permute-start(bf16[2,4,256,256]{3,2,1,0:T(8,128)(2,1)S(1)} %pad_maximum_fusion.3.refs_8_.refs_13_.refs_9_.refs_14_), channel_id=1, source_target_pairs={{0,4},{1,5},{2,6},{3,7},{4,0},{5,1},{6,2},{7,3},{8,12},{9,13},{10,... | collective-permute-start | bytes 3145736 | tf_op jit(solution)/shard_map/ppermute | solution.py:454
  143.5 25.9 %collective-permute-start.32 = (bf16[2,4,256,256]{3,2,1,0:T(8,128)(2,1)}, bf16[2,4,256,256]{3,2,1,0:T(8,128)(2,1)}, u32[]{:S(2)}, u32[]{:S(2)}) collective-permute-start(bf16[2,4,256,256]{3,2,1,0:T(8,128)(2,1)} %collective-permute-done.30.refs_9_.refs_14_.refs_10_.refs_15_), channel_id=1, source_target_pairs={{0,16},{16,0},{1,17},{17,1},{2,18},{18,2},{3,19},{19,3},{4,20},{20... | collective-permute-start | bytes 3145736 | tf_op jit(solution)/shard_map/ppermute | solution.py:435
  145.3 24.2 %collective-permute-start.36 = (bf16[2,4,256,256]{3,2,1,0:T(8,128)(2,1)S(1)}, bf16[2,4,256,256]{3,2,1,0:T(8,128)(2,1)S(1)}, u32[]{:S(2)}, u32[]{:S(2)}) collective-permute-start(bf16[2,4,256,256]{3,2,1,0:T(8,128)(2,1)S(1)} %pad_maximum_fusion.4.refs_7_.refs_2_), channel_id=1, source_target_pairs={{0,4},{1,5},{2,6},{3,7},{4,0},{5,1},{6,2},{7,3},{8,12},{9,13},{10,... | collective-permute-start | bytes 3145736 | tf_op jit(solution)/shard_map/ppermute | solution.py:454
  147.0 22.5 %collective-permute-start.28 = (bf16[320,1024]{1,0:T(8,128)(2,1)}, bf16[320,1024]{1,0:T(8,128)(2,1)}, u32[]{:S(2)}, u32[]{:S(2)}) collective-permute-start(bf16[320,1024]{1,0:T(8,128)(2,1)} %get-tuple-element.205), channel_id=1, source_target_pairs={{0,1},{1,0},{2,3},{3,2},{4,5},{5,4},{6,7},{7,6},{8,9},{9,8},{10,11... | collective-permute-start | bytes 1966088 | tf_op jit(solution)/shard_map/ppermute | solution.py:442
  148.3 14.2 %collective-permute-start.33 = (bf16[4,256,256]{2,1,0:T(8,128)(2,1)S(1)}, bf16[4,256,256]{2,1,0:T(8,128)(2,1)}, u32[]{:S(2)}, u32[]{:S(2)}) collective-permute-start(bf16[4,256,256]{2,1,0:T(8,128)(2,1)S(1)} %select_bitcast_fusion.2), channel_id=1, source_target_pairs={{0,8},{1,9},{2,10},{3,11},{4,12},{5,13},{6,14},{7,15},{8,0},{9,1},... | collective-permute-start | bytes 1572872 | tf_op jit(solution)/shard_map/ppermute | solution.py:454
  148.8 19.4 %collective-permute-start.37 = (bf16[2,256,256]{2,1,0:T(8,128)(2,1)S(1)}, bf16[2,256,256]{2,1,0:T(8,128)(2,1)S(1)}, u32[]{:S(2)}, u32[]{:S(2)}) collective-permute-start(bf16[2,256,256]{2,1,0:T(8,128)(2,1)S(1)} %bitcast.218), channel_id=1, source_target_pairs={{0,3},{1,2},{2,1},{3,0},{4,7},{5,6},{6,5},{7,4},{8,11},{9,10},{10,... | collective-permute-start | bytes 786440 | tf_op jit(solution)/shard_map/ppermute | solution.py:430
  170.3 15.2 %collective-permute-start.38 = (f32[320,256]{1,0:T(8,128)S(1)}, f32[320,256]{1,0:T(8,128)S(1)}, u32[]{:S(2)}, u32[]{:S(2)}) collective-permute-start(f32[320,256]{1,0:T(8,128)S(1)} %get-tuple-element.215), channel_id=1, source_target_pairs={{0,3},{1,2},{2,1},{3,0},{4,7},{5,6},{6,5},{7,4},{8,11},{9,10},{10,... | collective-permute-start | bytes 983048 | tf_op jit(solution)/shard_map/ppermute | solution.py:430
  172.9 19.3 %collective-permute-start.43 = (bf16[2,4,256,256]{3,2,1,0:T(8,128)(2,1)S(1)}, bf16[2,4,256,256]{3,2,1,0:T(8,128)(2,1)S(1)}, u32[]{:S(2)}, u32[]{:S(2)}) collective-permute-start(bf16[2,4,256,256]{3,2,1,0:T(8,128)(2,1)S(1)} %pad_maximum_fusion.5.refs_12_.refs_7_), channel_id=1, source_target_pairs={{0,4},{1,5},{2,6},{3,7},{4,0},{5,1},{6,2},{7,3},{8,12},{9,13},{10,... | collective-permute-start | bytes 3145736 | tf_op jit(solution)/shard_map/ppermute | solution.py:454
  192.8 18.7 %collective-permute-start.45 = (bf16[2,4,256,256]{3,2,1,0:T(8,128)(2,1)S(1)}, bf16[2,4,256,256]{3,2,1,0:T(8,128)(2,1)S(1)}, u32[]{:S(2)}, u32[]{:S(2)}) collective-permute-start(bf16[2,4,256,256]{3,2,1,0:T(8,128)(2,1)S(1)} %collective-permute-done.43.refs_13_.refs_8_), channel_id=1, source_target_pairs={{0,16},{16,0},{1,17},{17,1},{2,18},{18,2},{3,19},{19,3},{4,20},{20... | collective-permute-start | bytes 3145736 | tf_op jit(solution)/shard_map/ppermute | solution.py:435
  193.4 16.6 %collective-permute-start.39 = (bf16[320,1024]{1,0:T(8,128)(2,1)}, bf16[320,1024]{1,0:T(8,128)(2,1)S(1)}, u32[]{:S(2)}, u32[]{:S(2)}) collective-permute-start(bf16[320,1024]{1,0:T(8,128)(2,1)} %get-tuple-element.216), channel_id=1, source_target_pairs={{0,1},{1,0},{2,3},{3,2},{4,5},{5,4},{6,7},{7,6},{8,9},{9,8},{10,11... | collective-permute-start | bytes 1966088 | tf_op jit(solution)/shard_map/ppermute | solution.py:442
  193.4 18.0 %collective-permute-start.44 = (bf16[4,256,256]{2,1,0:T(8,128)(2,1)S(1)}, bf16[4,256,256]{2,1,0:T(8,128)(2,1)S(1)}, u32[]{:S(2)}, u32[]{:S(2)}) collective-permute-start(bf16[4,256,256]{2,1,0:T(8,128)(2,1)S(1)} %collective-permute-done.41.refs_10_.refs_5_), channel_id=1, source_target_pairs={{0,16},{16,0},{1,17},{17,1},{2,18},{18,2},{3,19},{19,3},{4,20},{20... | collective-permute-start | bytes 1572872 | tf_op jit(solution)/shard_map/ppermute | solution.py:435
  210.0 14.7 %collective-permute-start.48 = (f32[320,256]{1,0:T(8,128)S(1)}, f32[320,256]{1,0:T(8,128)S(1)}, u32[]{:S(2)}, u32[]{:S(2)}) collective-permute-start(f32[320,256]{1,0:T(8,128)S(1)} %get-tuple-element.225.refs_0_), channel_id=1, source_target_pairs={{0,1},{1,0},{2,3},{3,2},{4,5},{5,4},{6,7},{7,6},{8,9},{9,8},{10,11... | collective-permute-start | bytes 983048 | tf_op jit(solution)/shard_map/ppermute | solution.py:442
  210.2 15.3 %collective-permute-start.49 = (f32[320,256]{1,0:T(8,128)S(1)}, f32[320,256]{1,0:T(8,128)S(1)}, u32[]{:S(2)}, u32[]{:S(2)}) collective-permute-start(f32[320,256]{1,0:T(8,128)S(1)} %collective-permute-done.38.refs_1_), channel_id=1, source_target_pairs={{0,1},{1,0},{2,3},{3,2},{4,5},{5,4},{6,7},{7,6},{8,9},{9,8},{10,11... | collective-permute-start | bytes 983048 | tf_op jit(solution)/shard_map/ppermute | solution.py:442
  225.5 14.8 %collective-permute-start.50 = (bf16[320,1024]{1,0:T(8,128)(2,1)}, bf16[320,1024]{1,0:T(8,128)(2,1)S(1)}, u32[]{:S(2)}, u32[]{:S(2)}) collective-permute-start(bf16[320,1024]{1,0:T(8,128)(2,1)} %get-tuple-element.227), channel_id=1, source_target_pairs={{0,1},{1,0},{2,3},{3,2},{4,5},{5,4},{6,7},{7,6},{8,9},{9,8},{10,11... | collective-permute-start | bytes 1966088 | tf_op jit(solution)/shard_map/ppermute | solution.py:442
  267.0 19.3 %collective-permute-start.53 = (bf16[2,8,256,256]{3,2,1,0:T(8,128)(2,1)}, bf16[2,8,256,256]{3,2,1,0:T(8,128)(2,1)S(1)}, u32[]{:S(2)}, u32[]{:S(2)}) collective-permute-start(bf16[2,8,256,256]{3,2,1,0:T(8,128)(2,1)} %get-tuple-element.241), channel_id=1, source_target_pairs={{0,16},{16,0},{1,17},{17,1},{2,18},{18,2},{3,19},{19,3},{4,20},{20... | collective-permute-start | bytes 6291464 | tf_op jit(solution)/shard_map/ppermute | solution.py:435
  270.1 16.2 %collective-permute-start.52 = (bf16[320,1024]{1,0:T(8,128)(2,1)}, bf16[320,1024]{1,0:T(8,128)(2,1)}, u32[]{:S(2)}, u32[]{:S(2)}) collective-permute-start(bf16[320,1024]{1,0:T(8,128)(2,1)} %get-tuple-element.233), channel_id=1, source_target_pairs={{0,1},{1,0},{2,3},{3,2},{4,5},{5,4},{6,7},{7,6},{8,9},{9,8},{10,11... | collective-permute-start | bytes 1966088 | tf_op jit(solution)/shard_map/ppermute | solution.py:442
  302.4 16.3 %collective-permute-start.57 = (bf16[320,1024]{1,0:T(8,128)(2,1)}, bf16[320,1024]{1,0:T(8,128)(2,1)S(1)}, u32[]{:S(2)}, u32[]{:S(2)}) collective-permute-start(bf16[320,1024]{1,0:T(8,128)(2,1)} %get-tuple-element.255), channel_id=1, source_target_pairs={{0,1},{1,0},{2,3},{3,2},{4,5},{5,4},{6,7},{7,6},{8,9},{9,8},{10,11... | collective-permute-start | bytes 1966088 | tf_op jit(solution)/shard_map/ppermute | solution.py:442
  315.0 33.7 %collective-permute-start.64 = (bf16[2,8,256,256]{3,2,1,0:T(8,128)(2,1)}, bf16[2,8,256,256]{3,2,1,0:T(8,128)(2,1)}, u32[]{:S(2)}, u32[]{:S(2)}) collective-permute-start(bf16[2,8,256,256]{3,2,1,0:T(8,128)(2,1)} %shard_map.246), channel_id=1, source_target_pairs={{0,4},{1,5},{2,6},{3,7},{4,0},{5,1},{6,2},{7,3},{8,12},{9,13},{10,... | collective-permute-start | bytes 6291464 | tf_op jit(solution)/shard_map/ppermute | solution.py:454
  318.7 15.0 %collective-permute-start.60 = (bf16[4,256,256]{2,1,0:T(8,128)(2,1)S(1)}, bf16[4,256,256]{2,1,0:T(8,128)(2,1)S(1)}, u32[]{:S(2)}, u32[]{:S(2)}) collective-permute-start(bf16[4,256,256]{2,1,0:T(8,128)(2,1)S(1)} %add_convert_fusion.11), channel_id=1, source_target_pairs={{0,8},{1,9},{2,10},{3,11},{4,12},{5,13},{6,14},{7,15},{8,0},{9,1},... | collective-permute-start | bytes 1572872 | tf_op jit(solution)/shard_map/ppermute | solution.py:454
  337.6 19.6 %collective-permute-start.70 = (bf16[2,4,256,256]{3,2,1,0:T(8,128)(2,1)}, bf16[2,4,256,256]{3,2,1,0:T(8,128)(2,1)S(1)}, u32[]{:S(2)}, u32[]{:S(2)}) collective-permute-start(bf16[2,4,256,256]{3,2,1,0:T(8,128)(2,1)} %shard_map.250), channel_id=1, source_target_pairs={{0,4},{1,5},{2,6},{3,7},{4,0},{5,1},{6,2},{7,3},{8,12},{9,13},{10,... | collective-permute-start | bytes 3145736 | tf_op jit(solution)/shard_map/ppermute | solution.py:454
  348.7 19.1 %collective-permute-start.62 = (bf16[2,8,256,256]{3,2,1,0:T(8,128)(2,1)}, bf16[2,8,256,256]{3,2,1,0:T(8,128)(2,1)S(1)}, u32[]{:S(2)}, u32[]{:S(2)}) collective-permute-start(bf16[2,8,256,256]{3,2,1,0:T(8,128)(2,1)} %get-tuple-element.281), channel_id=1, source_target_pairs={{0,16},{16,0},{1,17},{17,1},{2,18},{18,2},{3,19},{19,3},{4,20},{20... | collective-permute-start | bytes 6291464 | tf_op jit(solution)/shard_map/ppermute | solution.py:435
  352.0 15.8 %collective-permute-start.61 = (bf16[320,1024]{1,0:T(8,128)(2,1)S(1)}, bf16[320,1024]{1,0:T(8,128)(2,1)S(1)}, u32[]{:S(2)}, u32[]{:S(2)}) collective-permute-start(bf16[320,1024]{1,0:T(8,128)(2,1)S(1)} %copy-done.67), channel_id=1, source_target_pairs={{0,1},{1,0},{2,3},{3,2},{4,5},{5,4},{6,7},{7,6},{8,9},{9,8},{10,11... | collective-permute-start | bytes 1966088 | tf_op jit(solution)/shard_map/ppermute | solution.py:442
  358.5 43.7 %collective-permute-start.71 = (bf16[2,2,256,256]{3,2,1,0:T(8,128)(2,1)}, bf16[2,2,256,256]{3,2,1,0:T(8,128)(2,1)}, u32[]{:S(2)}, u32[]{:S(2)}) collective-permute-start(bf16[2,2,256,256]{3,2,1,0:T(8,128)(2,1)} %broadcast_select_fusion.3), channel_id=1, source_target_pairs={{0,16},{16,0},{1,17},{17,1},{2,18},{18,2},{3,19},{19,3},{4,20},{20... | collective-permute-start | bytes 1572872 | tf_op jit(solution)/shard_map/ppermute | solution.py:435
  367.8 35.7 %collective-permute-start.72 = (bf16[4,256,256]{2,1,0:T(8,128)(2,1)}, bf16[4,256,256]{2,1,0:T(8,128)(2,1)}, u32[]{:S(2)}, u32[]{:S(2)}) collective-permute-start(bf16[4,256,256]{2,1,0:T(8,128)(2,1)} %slice_bitcast_fusion.2), channel_id=1, source_target_pairs={{0,3},{1,2},{2,1},{3,0},{4,7},{5,6},{6,5},{7,4},{8,11},{9,10},{10,... | collective-permute-start | bytes 1572872 | tf_op jit(solution)/shard_map/ppermute | solution.py:430
  388.6 30.7 %collective-permute-start.74 = (bf16[2,8,256,256]{3,2,1,0:T(8,128)(2,1)}, bf16[2,8,256,256]{3,2,1,0:T(8,128)(2,1)}, u32[]{:S(2)}, u32[]{:S(2)}) collective-permute-start(bf16[2,8,256,256]{3,2,1,0:T(8,128)(2,1)} %shard_map.252), channel_id=1, source_target_pairs={{0,4},{1,5},{2,6},{3,7},{4,0},{5,1},{6,2},{7,3},{8,12},{9,13},{10,... | collective-permute-start | bytes 6291464 | tf_op jit(solution)/shard_map/ppermute | solution.py:454
  394.5 24.0 %collective-permute-start.68 = (bf16[2,4,256,256]{3,2,1,0:T(8,128)(2,1)}, bf16[2,4,256,256]{3,2,1,0:T(8,128)(2,1)}, u32[]{:S(2)}, u32[]{:S(2)}) collective-permute-start(bf16[2,4,256,256]{3,2,1,0:T(8,128)(2,1)} %get-tuple-element.302), channel_id=1, source_target_pairs={{0,16},{16,0},{1,17},{17,1},{2,18},{18,2},{3,19},{19,3},{4,20},{20... | collective-permute-start | bytes 3145736 | tf_op jit(solution)/shard_map/ppermute | solution.py:435
  402.1 16.4 %collective-permute-start.67 = (bf16[320,1024]{1,0:T(8,128)(2,1)S(1)}, bf16[320,1024]{1,0:T(8,128)(2,1)S(1)}, u32[]{:S(2)}, u32[]{:S(2)}) collective-permute-start(bf16[320,1024]{1,0:T(8,128)(2,1)S(1)} %copy-done.66), channel_id=1, source_target_pairs={{0,1},{1,0},{2,3},{3,2},{4,5},{5,4},{6,7},{7,6},{8,9},{9,8},{10,11... | collective-permute-start | bytes 1966088 | tf_op jit(solution)/shard_map/ppermute | solution.py:442
  422.6 41.4 %collective-permute-start.91 = (bf16[4,256,256]{2,1,0:T(8,128)(2,1)}, bf16[4,256,256]{2,1,0:T(8,128)(2,1)}, u32[]{:S(2)}, u32[]{:S(2)}) collective-permute-start(bf16[4,256,256]{2,1,0:T(8,128)(2,1)} %fusion.1.refs_2_), channel_id=1, source_target_pairs={{0,16},{16,0},{1,17},{17,1},{2,18},{18,2},{3,19},{19,3},{4,20},{20... | collective-permute-start | bytes 1572872 | tf_op jit(solution)/shard_map/ppermute | solution.py:435
  423.0 25.9 %collective-permute-start.87 = (bf16[2,256,256]{2,1,0:T(8,128)(2,1)S(1)}, bf16[2,256,256]{2,1,0:T(8,128)(2,1)}, u32[]{:S(2)}, u32[]{:S(2)}) collective-permute-start(bf16[2,256,256]{2,1,0:T(8,128)(2,1)S(1)} %slice_bitcast_fusion.8), channel_id=1, source_target_pairs={{0,3},{1,2},{2,1},{3,0},{4,7},{5,6},{6,5},{7,4},{8,11},{9,10},{10,... | collective-permute-start | bytes 786440 | tf_op jit(solution)/shard_map/ppermute | solution.py:430
  431.9 14.2 %collective-permute-start.76 = (bf16[2,4,256,256]{3,2,1,0:T(8,128)(2,1)}, bf16[2,4,256,256]{3,2,1,0:T(8,128)(2,1)S(1)}, u32[]{:S(2)}, u32[]{:S(2)}) collective-permute-start(bf16[2,4,256,256]{3,2,1,0:T(8,128)(2,1)} %shard_map.255), channel_id=1, source_target_pairs={{0,4},{1,5},{2,6},{3,7},{4,0},{5,1},{6,2},{7,3},{8,12},{9,13},{10,... | collective-permute-start | bytes 3145736 | tf_op jit(solution)/shard_map/ppermute | solution.py:454
  437.9 15.6 %collective-permute-start.89 = (bf16[4,256,256]{2,1,0:T(8,128)(2,1)S(1)}, bf16[4,256,256]{2,1,0:T(8,128)(2,1)S(1)}, u32[]{:S(2)}, u32[]{:S(2)}) collective-permute-start(bf16[4,256,256]{2,1,0:T(8,128)(2,1)S(1)} %slice_bitcast_fusion), channel_id=1, source_target_pairs={{0,3},{1,2},{2,1},{3,0},{4,7},{5,6},{6,5},{7,4},{8,11},{9,10},{10,... | collective-permute-start | bytes 1572872 | tf_op jit(solution)/shard_map/ppermute | solution.py:430
  450.0 46.8 %collective-permute-start.88 = (bf16[2,256,256]{2,1,0:T(8,128)(2,1)S(1)}, bf16[2,256,256]{2,1,0:T(8,128)(2,1)}, u32[]{:S(2)}, u32[]{:S(2)}) collective-permute-start(bf16[2,256,256]{2,1,0:T(8,128)(2,1)S(1)} %fusion.8.refs_2_), channel_id=1, source_target_pairs={{0,16},{16,0},{1,17},{17,1},{2,18},{18,2},{3,19},{19,3},{4,20},{20... | collective-permute-start | bytes 786440 | tf_op jit(solution)/shard_map/ppermute | solution.py:435
  468.9 19.4 %collective-permute-start.84 = (f32[25,256]{1,0:T(8,128)S(1)}, f32[25,256]{1,0:T(8,128)S(1)}, u32[]{:S(2)}, u32[]{:S(2)}) collective-permute-start(f32[25,256]{1,0:T(8,128)S(1)} %bitcast.222), channel_id=1, source_target_pairs={{0,3},{1,2},{2,1},{3,0},{4,7},{5,6},{6,5},{7,4},{8,11},{9,10},{10,... | collective-permute-start | bytes 76808 | tf_op jit(solution)/shard_map/ppermute | solution.py:430
  470.8 17.6 %collective-permute-start.85 = (bf16[2,256,256]{2,1,0:T(8,128)(2,1)S(1)}, bf16[2,256,256]{2,1,0:T(8,128)(2,1)S(1)}, u32[]{:S(2)}, u32[]{:S(2)}) collective-permute-start(bf16[2,256,256]{2,1,0:T(8,128)(2,1)S(1)} %slice_bitcast_fusion.10), channel_id=1, source_target_pairs={{0,3},{1,2},{2,1},{3,0},{4,7},{5,6},{6,5},{7,4},{8,11},{9,10},{10,... | collective-permute-start | bytes 786440 | tf_op jit(solution)/shard_map/ppermute | solution.py:430
  (130 other events, 1078.3 us)

commit v5 on v4

--- a/solution.py
+++ b/solution.py
@@ -968,8 +968,9 @@
                 feed_weight_kernel, 8, 9.0, normed_two, gated(pre), hidden, masked_low
             )
             way.append(scatter_first(tiles))
-            gate = [arrived, *tiles, *way[-1]]
+            gate = [arrived, *tiles]
             if layer < LAYERS - 1:
+                gate = gate + list(way[-1])
                 own, near_part, near_arrived, far_part = way[-2]
                 near_sent = near_add(near_part, near_arrived, far_moved)
                 part = scatter_third(way[-3][0], near_moved, first_core)
@@ -992,13 +993,13 @@
         if layer == LAYERS - 1:
             output_halves.append(flip_col(gated(output_other[rows // 2 :])))
         if tiled:
-            gate = [low, far_moved] + (output_halves[1:] if layer == LAYERS - 1 else [])
+            gate = [low, *output_halves[1:]] if layer == LAYERS - 1 else [low, far_moved]
         wide, arrived = group_total(wide, gated(low))
         if tiled:
             own, near_part, near_arrived, far_part = way[-1]
             near_sent = near_add(near_part, near_arrived, far_moved)
             if layer < LAYERS - 1:
-                gate = [*gate, near_sent]
+                pass
             else:
                 received = gated(jnp.concatenate(output_halves))
             tiles = weight_tiles(
@@ -1015,7 +1016,7 @@
                 feed_parts = [add(part[0], flip_moved)]
                 part = scatter_third(way[-3][0], near_moved, first_core)
                 gate = gate + [part, *feed_parts]
-                flip_moved = flip_col(after(part[1], *gate))
+                flip_moved = flip_col(part[1])
             near_moved = cross_row(near_sent, 1, 2)
             arrived = gated(arrived)
             far_moved = cross_row(gated(way[-1][3]), 2, 1)
@@ -1076,13 +1077,17 @@
 
     if tiled:
         gate = [grad, far_moved]
-        input_share = share_rows(gated(grad), low_type)
         own, near_part, near_arrived, far_part = way[-1]
         near_sent = near_add(near_part, near_arrived, far_moved)
         attend_parts = [add(part[0], flip_moved)]
         part = scatter_third(way[-2][0], near_moved, first_core)
-        last_moved = cross_row(after(near_sent, part), 1, 2)
-        feed_parts.append(add(part[0], flip_col(part[1])))
+        last_moved = cross_row(after(near_sent, part, *attend_parts), 1, 2)
+        other = lax.dynamic_slice_in_dim(grad, (col_count - 1 - col_index) * width, width, 1)
+        count = part[1].shape[0] * 256
+        moved = jnp.concatenate([part[1].reshape(count, 256), other.astype(low_type)])
+        moved = flip_col(moved)
+        feed_parts.append(add(part[0], moved[:count].reshape(part[0].shape)))
+        input_share = join_rows(grad, moved[count:].astype(wide_type))
         part = scatter_third(way[-1][0], last_moved, first_core)
         gate = [part]
         attend_parts.append(add(part[0], flip_col(part[1])))

time: 512 us -> 500 us (0.977)
  waiting for transfers between devices: 164 us -> 130 us
  starting transfers between devices: 107 us -> 132 us
    ppermute x13, waiting for transfers between devices: 72.5 us -> 53.3 us  [group_shift(): return lax.ppermute(value, 'col', pairs)]
    ppermute x20, starting transfers between devices: 12.4 us -> 21.1 us  [cross_row(): return lax.ppermute(value, ('dp', 'row', 'col'), pairs)]
    ppermute x20, waiting for transfers between devices: 48.7 us -> 41.4 us  [cross_row(): return lax.ppermute(value, ('dp', 'row', 'col'), pairs)]
    ppermute x13, starting transfers between devices: 7.26 us -> 12.7 us  [group_shift(): return lax.ppermute(value, 'col', pairs)]
    ppermute x17 -> x16, waiting for transfers between devices: 29.5 us -> 24.7 us  [flip_col(): lax.ppermute(value, 'col', [(i, count - 1 - i) for i in range(count)])]
    unnamed x188 -> x170, local copies, waits for them, and re-layouts: 15.8 us -> 14.2 us
    ppermute x17 -> x16, starting transfers between devices: 33.4 us -> 32.6 us  [flip_col(): lax.ppermute(value, 'col', [(i, count - 1 - i) for i in range(count)])]
  transfers between devices with their start and end apart: 92 -> 91, of which waited for: 35 -> 34; matrix products, arithmetic and copies ran while one was open for 10% -> 10% of each run, Pallas kernels for 27% -> 30%
where the time goes in v5:
time: 500 us; the launch traced here: 490 us
  Pallas kernels  152 us (30%)
  starting transfers between devices  132 us (26%)
  waiting for transfers between devices  130 us (26%)
  local copies, waits for them, and re-layouts  34.4 us (7%)
  other arithmetic  32.6 us (7%)
  between operations  9.01 us (2%)
    pallas_call x17, Pallas kernels, call(): pl.pallas_call(kernel, out_shape=outs, in_specs=specs, out_specs=[VMEM] *...  137 us
    ppermute x13, waiting for transfers between devices, group_shift(): return lax.ppermute(value, 'col', pairs)  53.3 us
    ppermute x20, waiting for transfers between devices, cross_row(): return lax.ppermute(value, ('dp', 'row', 'col'), pairs)  41.4 us
    ppermute x34, starting transfers between devices, swap_core(): return lax.ppermute(value, 'dp', [(i, count - 1 - i) for i in range(count)])  40.5 us
    ppermute x16, starting transfers between devices, flip_col(): lax.ppermute(value, 'col', [(i, count - 1 - i) for i in range(count)])  32.6 us
    ppermute x16, waiting for transfers between devices, flip_col(): lax.ppermute(value, 'col', [(i, count - 1 - i) for i in range(count)])  24.7 us
    ppermute x20, starting transfers between devices, cross_row(): return lax.ppermute(value, ('dp', 'row', 'col'), pairs)  21.1 us
    ppermute x5, starting transfers between devices, butterfly_sum(): lax.ppermute(value, axis, [(i, i ^ step) for i in range(count)])  16.1 us
  transfers between devices with their start and end apart: 91, of which 34 were waited for; matrix products, arithmetic and copies ran while one was open for 10% of the time, Pallas kernels for 30%

profile of v5, /device:TPU:1, one launch (start us, length us, event | category | flops | bytes accessed | tf_op | source)
XLA Modules:
  0.0 490.5 jit_solution(6147911032089737145)
XLA Ops:
  3.8 4.2 collective-permute-start
  8.0 6.1 %collective-permute-done = bf16[2,256,256]{2,1,0:T(8,128)(2,1)S(1)} collective-permute-done((bf16[2,256,256]{2,1,0:T(8,128)(2,1)S(1)}, bf16[2,256,256]{2,1,0:T(8,128)(2,1)S(1)}, u32[]{:S(2)}, u32[]{:S(2)}) %collective-permute-start) | collective-permute-done | bytes 262176 | tf_op jit(solution)/shard_map/ppermute | solution.py:430
  22.1 3.3 collective-permute-start.1
  25.4 3.0 collective-permute-start.2
  35.9 4.2 collective-permute-done.5
  46.9 5.9 %collective-permute-start.12 = (s32[]{:T(128)}, s32[]{:T(128)}, u32[]{:S(2)}, u32[]{:S(2)}) collective-permute-start(s32[]{:T(128)} %add.145), channel_id=1, source_target_pairs={{0,4},{4,0},{8,12},{12,8},{1,5},{5,1},{9,13},{13,9},{2,6},{6,2},{1... | collective-permute-start | bytes 20 | tf_op jit(solution)/shard_map/ppermute | solution.py:639
  53.9 3.3 collective-permute-start.11
  58.5 3.4 collective-permute-done.11
  71.0 10.4 %shard_map.237 = (f32[320,1024]{1,0:T(8,128)}, bf16[320,1024]{1,0:T(8,128)(2,1)}, bf16[320,512]{1,0:T(8,128)(2,1)}, bf16[320,512]{1,0:T(8,128)(2,1)}, bf16[320,5...) custom-call(s32[10]{0:T(128)} %concatenate.32.meta, ...), custom_call_target="tpu_custom_call" | custom-call | flops 96599998464 | bytes 1048576 | tf_op jit(solution)/shard_map/pallas_call | solution.py:748
  88.8 3.5 collective-permute-start.14
  96.5 10.6 %collective-permute-done.14.refs_2_ = bf16[320,1024]{1,0:T(8,128)(2,1)} collective-permute-done((bf16[320,1024]{1,0:T(8,128)(2,1)}, bf16[320,1024]{1,0:T(8,128)(2,1)}, u32[]{:S(2)}, u32[]{:S(2)}) %collective-permute-start.14) | collective-permute-done | bytes 655392 | tf_op jit(solution)/shard_map/ppermute | solution.py:442
  107.1 5.8 %collective-permute-done.23 = bf16[2,256,256]{2,1,0:T(8,128)(2,1)S(1)} collective-permute-done((bf16[2,256,256]{2,1,0:T(8,128)(2,1)}, bf16[2,256,256]{2,1,0:T(8,128)(2,1)S(1)}, u32[]{:S(2)}, u32[]{:S(2)}) %collective-permute-start.23) | collective-permute-done | bytes 262176 | tf_op jit(solution)/shard_map/ppermute | solution.py:430
  119.1 4.5 collective-permute-done.26.refs_15_.refs_10_
  128.6 12.1 %shard_map.238 = (f32[320,1024]{1,0:T(8,128)}, bf16[320,1024]{1,0:T(8,128)(2,1)}, bf16[320,2048]{1,0:T(8,128)(2,1)}, bf16[320,2048]{1,0:T(8,128)(2,1)}, f32[320,1024]{1,0:T(8,128)}, /*index=5*/bf16[320,1024]{1,0:T(8,128)(2,1)}) custom-call(s32[10]{0:T(128)} %concatenate.32.meta, f32[320,1024]{1,0:T(8,128)} %get-tuple-element.188.refs_0_.inputs, ...), custom_call_target="tpu_custom_call" | custom-call | flops 110399995904 | bytes 1048576 | tf_op jit(solution)/shard_map/pallas_call | solution.py:748
  150.9 10.8 %collective-permute-done.33.refs_11_.refs_16_.refs_12_.refs_17_ = bf16[4,256,256]{2,1,0:T(8,128)(2,1)} collective-permute-done((bf16[4,256,256]{2,1,0:T(8,128)(2,1)S(1)}, bf16[4,256,256]{2,1,0:T(8,128)(2,1)}, u32[]{:S(2)}, u32[]{:S(2)}) %collective-permute-start.33) | collective-permute-done | bytes 524320 | tf_op jit(solution)/shard_map/ppermute | solution.py:454
  166.1 3.4 collective-permute-start.42
  175.0 11.1 %shard_map.239 = (f32[320,1024]{1,0:T(8,128)}, bf16[320,1024]{1,0:T(8,128)(2,1)}, bf16[320,512]{1,0:T(8,128)(2,1)}, bf16[320,512]{1,0:T(8,128)(2,1)}, bf16[320,5...) custom-call(s32[10]{0:T(128)} %concatenate.32.meta, ...), custom_call_target="tpu_custom_call" | custom-call | flops 96599998464 | bytes 1048576 | tf_op jit(solution)/shard_map/pallas_call | solution.py:748
  186.1 5.5 %collective-permute-done.43.refs_13_.refs_8_ = bf16[2,4,256,256]{3,2,1,0:T(8,128)(2,1)S(1)} collective-permute-done((bf16[2,4,256,256]{3,2,1,0:T(8,128)(2,1)S(1)}, bf16[2,4,256,256]{3,2,1,0:T(8,128)(2,1)S(1)}, u32[]{:S(2)}, u32[]{:S(2)}) %collective-permute-start.43) | collective-permute-done | bytes 1048608 | tf_op jit(solution)/shard_map/ppermute | solution.py:454
  193.3 6.7 %collective-permute-done.46.refs_15_.refs_10_ = bf16[4,256,256]{2,1,0:T(8,128)(2,1)S(1)} collective-permute-done((bf16[4,256,256]{2,1,0:T(8,128)(2,1)S(1)}, bf16[4,256,256]{2,1,0:T(8,128)(2,1)S(1)}, u32[]{:S(2)}, u32[]{:S(2)}) %collective-permute-start.46) | collective-permute-done | bytes 524320 | tf_op jit(solution)/shard_map/ppermute | solution.py:454
  201.6 8.3 %collective-permute-done.39.refs_2_ = bf16[320,1024]{1,0:T(8,128)(2,1)S(1)} collective-permute-done((bf16[320,1024]{1,0:T(8,128)(2,1)}, bf16[320,1024]{1,0:T(8,128)(2,1)S(1)}, u32[]{:S(2)}, u32[]{:S(2)}) %collective-permute-start.39) | collective-permute-done | bytes 655392 | tf_op jit(solution)/shard_map/ppermute | solution.py:442
  212.7 11.9 %shard_map.240 = (f32[320,1024]{1,0:T(8,128)}, bf16[320,1024]{1,0:T(8,128)(2,1)}, bf16[320,2048]{1,0:T(8,128)(2,1)}, bf16[320,2048]{1,0:T(8,128)(2,1)}, f32[320,1024]{1,0:T(8,128)}, /*index=5*/bf16[320,1024]{1,0:T(8,128)(2,1)}) custom-call(s32[10]{0:T(128)} %concatenate.32.meta, f32[320,1024]{1,0:T(8,128)} %get-tuple-element.208.refs_0_.inputs, ...), custom_call_target="tpu_custom_call" | custom-call | flops 110399995904 | bytes 1048576 | tf_op jit(solution)/shard_map/pallas_call | solution.py:748
  227.1 12.9 %collective-permute-done.50.arrived = bf16[320,1024]{1,0:T(8,128)(2,1)S(1)} collective-permute-done((bf16[320,1024]{1,0:T(8,128)(2,1)}, bf16[320,1024]{1,0:T(8,128)(2,1)S(1)}, u32[]{:S(2)}, u32[]{:S(2)}) %collective-permute-start.50) | collective-permute-done | bytes 655392 | tf_op jit(solution)/shard_map/ppermute | solution.py:442
  240.8 4.4 shard_map.241
  248.4 9.8 %shard_map.242 = (f32[320,1024]{1,0:T(8,128)}, bf16[320,1024]{1,0:T(8,128)(2,1)}, bf16[320,2048]{1,0:T(8,128)(2,1)}, f32[1,1024]{1,0:T(1,128)}, f32[1,2048]{1,0:...) custom-call(s32[10]{0:T(128)} %concatenate.32.meta, f32[320,1024]{1,0:T(8,128)} %get-tuple-element.226.refs_0_, ...), custom_call_target="tpu_custom_call" | custom-call | flops 92000002048 | bytes 1048576 | tf_op jit(solution)/shard_map/pallas_call | solution.py:748
  258.3 9.0 %shard_map.243 = (bf16[2,8,256,256]{3,2,1,0:T(8,128)(2,1)}, bf16[2,8,256,256]{3,2,1,0:T(8,128)(2,1)}, bf16[2,8,256,256]{3,2,1,0:T(8,128)(2,1)}, bf16[8,256,256]{2,1,0:T(8,128)(2,1)}, bf16[8,256,256]{2,1,0:T(8,128)(2,1)}) custom-call(s32[10]{0:T(128)} %concatenate.32.meta, bf16[320,1024]{1,0:T(8,128)(2,1)} %get-tuple-element.232.normed, ...), custom_call_target="tpu_custom_call" | custom-call | flops 82800001024 | bytes 1048576 | tf_op jit(solution)/shard_map/pallas_call | solution.py:748
  273.5 11.8 %shard_map.244 = (f32[320,1024]{1,0:T(8,128)}, bf16[320,1024]{1,0:T(8,128)(2,1)}, f32[1,1024]{1,0:T(1,128)}, f32[1,1024]{1,0:T(1,128)}, f32[1,1024]{1,0:T(1,128)...) custom-call(s32[10]{0:T(128)} %concatenate.32.meta, ...), custom_call_target="tpu_custom_call" | custom-call | flops 110399995904 | bytes 1048576 | tf_op jit(solution)/shard_map/pallas_call | solution.py:748
  286.9 5.4 %shard_map.245 = (bf16[2,4,256,256]{3,2,1,0:T(8,128)(2,1)}, bf16[2,4,256,256]{3,2,1,0:T(8,128)(2,1)}, bf16[2,4,256,256]{3,2,1,0:T(8,128)(2,1)}, bf16[4,256,256]{2,1,0:T(8,128)(2,1)}, bf16[4,256,256]{2,1,0:T(8,128)(2,1)}) custom-call(s32[10]{0:T(128)} %concatenate.32.meta, bf16[320,1024]{1,0:T(8,128)(2,1)} %get-tuple-element.253.normed, ...), custom_call_target="tpu_custom_call" | custom-call | flops 50600001536 | bytes 1048576 | tf_op jit(solution)/shard_map/pallas_call | solution.py:748
  292.3 3.0 collective-permute-start.55
  300.7 4.3 shard_map.246
  306.9 4.3 shard_map.247
  311.3 9.8 %shard_map.248 = (f32[320,1024]{1,0:T(8,128)}, bf16[320,1024]{1,0:T(8,128)(2,1)}, bf16[320,2048]{1,0:T(8,128)(2,1)}, f32[1,1024]{1,0:T(1,128)}, f32[1,2048]{1,0:...) custom-call(s32[10]{0:T(128)} %concatenate.32.meta, f32[320,1024]{1,0:T(8,128)} %get-tuple-element.266.refs_0_, ...), custom_call_target="tpu_custom_call" | custom-call | flops 92000002048 | bytes 1048576 | tf_op jit(solution)/shard_map/pallas_call | solution.py:748
  321.9 3.1 shard_map.250
  325.8 9.1 %shard_map.249 = (bf16[2,8,256,256]{3,2,1,0:T(8,128)(2,1)}, bf16[2,8,256,256]{3,2,1,0:T(8,128)(2,1)}, bf16[2,8,256,256]{3,2,1,0:T(8,128)(2,1)}, bf16[8,256,256]{2,1,0:T(8,128)(2,1)}, bf16[8,256,256]{2,1,0:T(8,128)(2,1)}) custom-call(s32[10]{0:T(128)} %concatenate.32.meta, bf16[320,1024]{1,0:T(8,128)(2,1)} %get-tuple-element.272.normed, ...), custom_call_target="tpu_custom_call" | custom-call | flops 82800001024 | bytes 1048576 | tf_op jit(solution)/shard_map/pallas_call | solution.py:748
  334.9 5.2 %collective-permute-start.62 = (bf16[2,8,256,256]{3,2,1,0:T(8,128)(2,1)}, bf16[2,8,256,256]{3,2,1,0:T(8,128)(2,1)S(1)}, u32[]{:S(2)}, u32[]{:S(2)}) collective-permute-start(bf16[2,8,256,256]{3,2,1,0:T(8,128)(2,1)} %get-tuple-element.279), channel_id=1, source_target_pairs={{0,16},{16,0},{1,17},{17,1},{2,18},{18,2},{3,19},{19,3},{4,20},{20... | collective-permute-start | bytes 6291464 | tf_op jit(solution)/shard_map/ppermute | solution.py:435
  352.1 7.6 %collective-permute-done.61.refs_1_ = bf16[320,1024]{1,0:T(8,128)(2,1)S(1)} collective-permute-done((bf16[320,1024]{1,0:T(8,128)(2,1)S(1)}, bf16[320,1024]{1,0:T(8,128)(2,1)S(1)}, u32[]{:S(2)}, u32[]{:S(2)}) %collective-permute-start.61) | collective-permute-done | bytes 655392 | tf_op jit(solution)/shard_map/ppermute | solution.py:442
  362.8 11.9 %shard_map.251 = (f32[320,1024]{1,0:T(8,128)}, bf16[320,1024]{1,0:T(8,128)(2,1)}, f32[1,1024]{1,0:T(1,128)}, f32[1,1024]{1,0:T(1,128)}, f32[1,1024]{1,0:T(1,128)...) custom-call(s32[10]{0:T(128)} %concatenate.32.meta, ...), custom_call_target="tpu_custom_call" | custom-call | flops 110399995904 | bytes 1048576 | tf_op jit(solution)/shard_map/pallas_call | solution.py:748
  375.7 4.1 shard_map.253
  380.9 5.4 %shard_map.252 = (bf16[2,4,256,256]{3,2,1,0:T(8,128)(2,1)}, bf16[2,4,256,256]{3,2,1,0:T(8,128)(2,1)}, bf16[2,4,256,256]{3,2,1,0:T(8,128)(2,1)}, bf16[4,256,256]{2,1,0:T(8,128)(2,1)}, bf16[4,256,256]{2,1,0:T(8,128)(2,1)}) custom-call(s32[10]{0:T(128)} %concatenate.32.meta, bf16[320,1024]{1,0:T(8,128)(2,1)} %get-tuple-element.293.normed, ...), custom_call_target="tpu_custom_call" | custom-call | flops 50600001536 | bytes 1048576 | tf_op jit(solution)/shard_map/pallas_call | solution.py:748
  394.7 10.8 %collective-permute-done.67.arrived = bf16[320,1024]{1,0:T(8,128)(2,1)S(1)} collective-permute-done((bf16[320,1024]{1,0:T(8,128)(2,1)S(1)}, bf16[320,1024]{1,0:T(8,128)(2,1)S(1)}, u32[]{:S(2)}, u32[]{:S(2)}) %collective-permute-start.67) | collective-permute-done | bytes 655392 | tf_op jit(solution)/shard_map/ppermute | solution.py:442
  408.9 3.5 collective-permute-done.76
  414.0 3.1 shard_map.255
  419.3 4.3 shard_map.254
  426.8 6.0 %collective-permute-done.77 = bf16[2,4,256,256]{3,2,1,0:T(8,128)(2,1)S(1)} collective-permute-done((bf16[2,4,256,256]{3,2,1,0:T(8,128)(2,1)S(1)}, bf16[2,4,256,256]{3,2,1,0:T(8,128)(2,1)S(1)}, u32[]{:S(2)}, u32[]{:S(2)}) %collective-permute-start.77) | collective-permute-done | bytes 1048608 | tf_op jit(solution)/shard_map/ppermute | solution.py:454
  433.9 3.1 collective-permute-start.78
  451.9 3.9 shard_map.257
  459.9 11.9 %collective-permute-start.82 = (f32[]{:T(128)}, f32[]{:T(128)}, u32[]{:S(2)}, u32[]{:S(2)}) collective-permute-start(f32[]{:T(128)} %bitcast.88), channel_id=1, source_target_pairs={{0,1},{1,0},{2,3},{3,2},{4,5},{5,4},{6,7},{7,6},{8,9},{9,8},{10,11... | collective-permute-start | bytes 20 | tf_op jit(solution)/shard_map/ppermute | solution.py:469
  474.0 3.0 collective-permute-start.83
  478.1 4.6 collective-permute-start.87
  (450 shorter events, 168.3 us)
Async XLA Ops:
  17.7 23.3 %collective-permute-start.4 = (bf16[2,4,256,256]{3,2,1,0:T(8,128)(2,1)}, bf16[2,4,256,256]{3,2,1,0:T(8,128)(2,1)}, u32[]{:S(2)}, u32[]{:S(2)}) collective-permute-start(bf16[2,4,256,256]{3,2,1,0:T(8,128)(2,1)} %pad_maximum_fusion.refs_8_.refs_13_.refs_9_.refs_14_), channel_id=1, source_target_pairs={{0,4},{1,5},{2,6},{3,7},{4,0},{5,1},{6,2},{7,3},{8,12},{9,13},{10,... | collective-permute-start | bytes 3145736 | tf_op jit(solution)/shard_map/ppermute | solution.py:454
  22.1 17.9 %collective-permute-start.1 = (f32[320,256]{1,0:T(8,128)}, f32[320,256]{1,0:T(8,128)}, u32[]{:S(2)}, u32[]{:S(2)}) collective-permute-start(f32[320,256]{1,0:T(8,128)} %get-tuple-element.177), channel_id=1, source_target_pairs={{0,3},{1,2},{2,1},{3,0},{4,7},{5,6},{6,5},{7,4},{8,11},{9,10},{10,... | collective-permute-start | bytes 983048 | tf_op jit(solution)/shard_map/ppermute | solution.py:430
  25.4 15.7 %collective-permute-start.2 = (f32[320,256]{1,0:T(8,128)S(1)}, f32[320,256]{1,0:T(8,128)S(1)}, u32[]{:S(2)}, u32[]{:S(2)}) collective-permute-start(f32[320,256]{1,0:T(8,128)S(1)} %get-tuple-element.178.refs_0_), channel_id=1, source_target_pairs={{0,1},{1,0},{2,3},{3,2},{4,5},{5,4},{6,7},{7,6},{8,9},{9,8},{10,11... | collective-permute-start | bytes 983048 | tf_op jit(solution)/shard_map/ppermute | solution.py:442
  41.0 20.9 %collective-permute-start.9 = (bf16[2,4,256,256]{3,2,1,0:T(8,128)(2,1)}, bf16[2,4,256,256]{3,2,1,0:T(8,128)(2,1)}, u32[]{:S(2)}, u32[]{:S(2)}) collective-permute-start(bf16[2,4,256,256]{3,2,1,0:T(8,128)(2,1)} %collective-permute-done.4.refs_9_.refs_14_.refs_10_.refs_15_), channel_id=1, source_target_pairs={{0,16},{16,0},{1,17},{17,1},{2,18},{18,2},{3,19},{19,3},{4,20},{20... | collective-permute-start | bytes 3145736 | tf_op jit(solution)/shard_map/ppermute | solution.py:435
  43.3 18.6 %collective-permute-start.7 = (f32[320,256]{1,0:T(8,128)}, f32[320,256]{1,0:T(8,128)}, u32[]{:S(2)}, u32[]{:S(2)}) collective-permute-start(f32[320,256]{1,0:T(8,128)} %collective-permute-done.1.refs_1_), channel_id=1, source_target_pairs={{0,1},{1,0},{2,3},{3,2},{4,5},{5,4},{6,7},{7,6},{8,9},{9,8},{10,11... | collective-permute-start | bytes 983048 | tf_op jit(solution)/shard_map/ppermute | solution.py:442
  45.5 16.4 %collective-permute-start.10 = (bf16[4,256,256]{2,1,0:T(8,128)(2,1)S(1)}, bf16[4,256,256]{2,1,0:T(8,128)(2,1)}, u32[]{:S(2)}, u32[]{:S(2)}) collective-permute-start(bf16[4,256,256]{2,1,0:T(8,128)(2,1)S(1)} %select_bitcast_fusion.5), channel_id=1, source_target_pairs={{0,8},{1,9},{2,10},{3,11},{4,12},{5,13},{6,14},{7,15},{8,0},{9,1},... | collective-permute-start | bytes 1572872 | tf_op jit(solution)/shard_map/ppermute | solution.py:454
  63.8 17.7 %collective-permute-start.17 = (bf16[2,256,256]{2,1,0:T(8,128)(2,1)}, bf16[2,256,256]{2,1,0:T(8,128)(2,1)S(1)}, u32[]{:S(2)}, u32[]{:S(2)}) collective-permute-start(bf16[2,256,256]{2,1,0:T(8,128)(2,1)} %bitcast.41), channel_id=1, source_target_pairs={{0,3},{1,2},{2,1},{3,0},{4,7},{5,6},{6,5},{7,4},{8,11},{9,10},{10,... | collective-permute-start | bytes 786440 | tf_op jit(solution)/shard_map/ppermute | solution.py:430
  85.8 27.1 %collective-permute-start.19 = (bf16[2,4,256,256]{3,2,1,0:T(8,128)(2,1)}, bf16[2,4,256,256]{3,2,1,0:T(8,128)(2,1)}, u32[]{:S(2)}, u32[]{:S(2)}) collective-permute-start(bf16[2,4,256,256]{3,2,1,0:T(8,128)(2,1)} %collective-permute-done.16.refs_8_.refs_3_), channel_id=1, source_target_pairs={{0,16},{16,0},{1,17},{17,1},{2,18},{18,2},{3,19},{19,3},{4,20},{20... | collective-permute-start | bytes 3145736 | tf_op jit(solution)/shard_map/ppermute | solution.py:435
  87.5 25.4 %collective-permute-start.22 = (bf16[2,4,256,256]{3,2,1,0:T(8,128)(2,1)S(1)}, bf16[2,4,256,256]{3,2,1,0:T(8,128)(2,1)}, u32[]{:S(2)}, u32[]{:S(2)}) collective-permute-start(bf16[2,4,256,256]{3,2,1,0:T(8,128)(2,1)S(1)} %pad_maximum_fusion.2.refs_12_.refs_7_), channel_id=1, source_target_pairs={{0,4},{1,5},{2,6},{3,7},{4,0},{5,1},{6,2},{7,3},{8,12},{9,13},{10,... | collective-permute-start | bytes 3145736 | tf_op jit(solution)/shard_map/ppermute | solution.py:454
  88.8 18.3 %collective-permute-start.14 = (bf16[320,1024]{1,0:T(8,128)(2,1)}, bf16[320,1024]{1,0:T(8,128)(2,1)}, u32[]{:S(2)}, u32[]{:S(2)}) collective-permute-start(bf16[320,1024]{1,0:T(8,128)(2,1)} %get-tuple-element.190), channel_id=1, source_target_pairs={{0,1},{1,0},{2,3},{3,2},{4,5},{5,4},{6,7},{7,6},{8,9},{9,8},{10,11... | collective-permute-start | bytes 1966088 | tf_op jit(solution)/shard_map/ppermute | solution.py:442
  93.6 19.4 %collective-permute-start.20 = (bf16[4,256,256]{2,1,0:T(8,128)(2,1)S(1)}, bf16[4,256,256]{2,1,0:T(8,128)(2,1)}, u32[]{:S(2)}, u32[]{:S(2)}) collective-permute-start(bf16[4,256,256]{2,1,0:T(8,128)(2,1)S(1)} %select_bitcast_fusion.4), channel_id=1, source_target_pairs={{0,8},{1,9},{2,10},{3,11},{4,12},{5,13},{6,14},{7,15},{8,0},{9,1},... | collective-permute-start | bytes 1572872 | tf_op jit(solution)/shard_map/ppermute | solution.py:454
  95.7 17.3 %collective-permute-start.23 = (bf16[2,256,256]{2,1,0:T(8,128)(2,1)}, bf16[2,256,256]{2,1,0:T(8,128)(2,1)S(1)}, u32[]{:S(2)}, u32[]{:S(2)}) collective-permute-start(bf16[2,256,256]{2,1,0:T(8,128)(2,1)} %fusion.11), channel_id=1, source_target_pairs={{0,3},{1,2},{2,1},{3,0},{4,7},{5,6},{6,5},{7,4},{8,11},{9,10},{10,... | collective-permute-start | bytes 786440 | tf_op jit(solution)/shard_map/ppermute | solution.py:430
  125.4 15.3 %collective-permute-start.31 = (bf16[2,256,256]{2,1,0:T(8,128)(2,1)S(1)}, bf16[2,256,256]{2,1,0:T(8,128)(2,1)S(1)}, u32[]{:S(2)}, u32[]{:S(2)}) collective-permute-start(bf16[2,256,256]{2,1,0:T(8,128)(2,1)S(1)} %slice_select_fusion), channel_id=1, source_target_pairs={{0,3},{1,2},{2,1},{3,0},{4,7},{5,6},{6,5},{7,4},{8,11},{9,10},{10,... | collective-permute-start | bytes 786440 | tf_op jit(solution)/shard_map/ppermute | solution.py:430
  128.3 14.1 %collective-permute-start.30 = (bf16[2,4,256,256]{3,2,1,0:T(8,128)(2,1)S(1)}, bf16[2,4,256,256]{3,2,1,0:T(8,128)(2,1)}, u32[]{:S(2)}, u32[]{:S(2)}) collective-permute-start(bf16[2,4,256,256]{3,2,1,0:T(8,128)(2,1)S(1)} %pad_maximum_fusion.3.refs_8_.refs_13_.refs_9_.refs_14_), channel_id=1, source_target_pairs={{0,4},{1,5},{2,6},{3,7},{4,0},{5,1},{6,2},{7,3},{8,12},{9,13},{10,... | collective-permute-start | bytes 3145736 | tf_op jit(solution)/shard_map/ppermute | solution.py:454
  143.5 22.5 %collective-permute-start.32 = (bf16[2,4,256,256]{3,2,1,0:T(8,128)(2,1)}, bf16[2,4,256,256]{3,2,1,0:T(8,128)(2,1)}, u32[]{:S(2)}, u32[]{:S(2)}) collective-permute-start(bf16[2,4,256,256]{3,2,1,0:T(8,128)(2,1)} %collective-permute-done.30.refs_9_.refs_14_.refs_10_.refs_15_), channel_id=1, source_target_pairs={{0,16},{16,0},{1,17},{17,1},{2,18},{18,2},{3,19},{19,3},{4,20},{20... | collective-permute-start | bytes 3145736 | tf_op jit(solution)/shard_map/ppermute | solution.py:435
  145.3 20.8 %collective-permute-start.36 = (bf16[2,4,256,256]{3,2,1,0:T(8,128)(2,1)S(1)}, bf16[2,4,256,256]{3,2,1,0:T(8,128)(2,1)S(1)}, u32[]{:S(2)}, u32[]{:S(2)}) collective-permute-start(bf16[2,4,256,256]{3,2,1,0:T(8,128)(2,1)S(1)} %pad_maximum_fusion.4.refs_7_.refs_2_), channel_id=1, source_target_pairs={{0,4},{1,5},{2,6},{3,7},{4,0},{5,1},{6,2},{7,3},{8,12},{9,13},{10,... | collective-permute-start | bytes 3145736 | tf_op jit(solution)/shard_map/ppermute | solution.py:454
  146.2 19.8 %collective-permute-start.28 = (bf16[320,1024]{1,0:T(8,128)(2,1)}, bf16[320,1024]{1,0:T(8,128)(2,1)}, u32[]{:S(2)}, u32[]{:S(2)}) collective-permute-start(bf16[320,1024]{1,0:T(8,128)(2,1)} %get-tuple-element.203), channel_id=1, source_target_pairs={{0,1},{1,0},{2,3},{3,2},{4,5},{5,4},{6,7},{7,6},{8,9},{9,8},{10,11... | collective-permute-start | bytes 1966088 | tf_op jit(solution)/shard_map/ppermute | solution.py:442
  147.5 14.2 %collective-permute-start.33 = (bf16[4,256,256]{2,1,0:T(8,128)(2,1)S(1)}, bf16[4,256,256]{2,1,0:T(8,128)(2,1)}, u32[]{:S(2)}, u32[]{:S(2)}) collective-permute-start(bf16[4,256,256]{2,1,0:T(8,128)(2,1)S(1)} %select_bitcast_fusion.2), channel_id=1, source_target_pairs={{0,8},{1,9},{2,10},{3,11},{4,12},{5,13},{6,14},{7,15},{8,0},{9,1},... | collective-permute-start | bytes 1572872 | tf_op jit(solution)/shard_map/ppermute | solution.py:454
  149.0 17.0 %collective-permute-start.37 = (bf16[2,256,256]{2,1,0:T(8,128)(2,1)S(1)}, bf16[2,256,256]{2,1,0:T(8,128)(2,1)S(1)}, u32[]{:S(2)}, u32[]{:S(2)}) collective-permute-start(bf16[2,256,256]{2,1,0:T(8,128)(2,1)S(1)} %bitcast.220), channel_id=1, source_target_pairs={{0,3},{1,2},{2,1},{3,0},{4,7},{5,6},{6,5},{7,4},{8,11},{9,10},{10,... | collective-permute-start | bytes 786440 | tf_op jit(solution)/shard_map/ppermute | solution.py:430
  169.5 16.5 %collective-permute-start.38 = (f32[320,256]{1,0:T(8,128)S(1)}, f32[320,256]{1,0:T(8,128)S(1)}, u32[]{:S(2)}, u32[]{:S(2)}) collective-permute-start(f32[320,256]{1,0:T(8,128)S(1)} %get-tuple-element.213), channel_id=1, source_target_pairs={{0,3},{1,2},{2,1},{3,0},{4,7},{5,6},{6,5},{7,4},{8,11},{9,10},{10,... | collective-permute-start | bytes 983048 | tf_op jit(solution)/shard_map/ppermute | solution.py:430
  171.3 14.8 %collective-permute-start.40 = (bf16[2,4,256,256]{3,2,1,0:T(8,128)(2,1)S(1)}, bf16[2,4,256,256]{3,2,1,0:T(8,128)(2,1)S(1)}, u32[]{:S(2)}, u32[]{:S(2)}) collective-permute-start(bf16[2,4,256,256]{3,2,1,0:T(8,128)(2,1)S(1)} %collective-permute-done.36.refs_8_.refs_3_), channel_id=1, source_target_pairs={{0,16},{16,0},{1,17},{17,1},{2,18},{18,2},{3,19},{19,3},{4,20},{20... | collective-permute-start | bytes 3145736 | tf_op jit(solution)/shard_map/ppermute | solution.py:435
  171.6 14.4 %collective-permute-start.41 = (bf16[4,256,256]{2,1,0:T(8,128)(2,1)S(1)}, bf16[4,256,256]{2,1,0:T(8,128)(2,1)S(1)}, u32[]{:S(2)}, u32[]{:S(2)}) collective-permute-start(bf16[4,256,256]{2,1,0:T(8,128)(2,1)S(1)} %select_bitcast_fusion.1), channel_id=1, source_target_pairs={{0,8},{1,9},{2,10},{3,11},{4,12},{5,13},{6,14},{7,15},{8,0},{9,1},... | collective-permute-start | bytes 1572872 | tf_op jit(solution)/shard_map/ppermute | solution.py:454
  173.1 18.5 %collective-permute-start.43 = (bf16[2,4,256,256]{3,2,1,0:T(8,128)(2,1)S(1)}, bf16[2,4,256,256]{3,2,1,0:T(8,128)(2,1)S(1)}, u32[]{:S(2)}, u32[]{:S(2)}) collective-permute-start(bf16[2,4,256,256]{3,2,1,0:T(8,128)(2,1)S(1)} %pad_maximum_fusion.5.refs_12_.refs_7_), channel_id=1, source_target_pairs={{0,4},{1,5},{2,6},{3,7},{4,0},{5,1},{6,2},{7,3},{8,12},{9,13},{10,... | collective-permute-start | bytes 3145736 | tf_op jit(solution)/shard_map/ppermute | solution.py:454
  192.8 18.5 %collective-permute-start.45 = (bf16[2,4,256,256]{3,2,1,0:T(8,128)(2,1)S(1)}, bf16[2,4,256,256]{3,2,1,0:T(8,128)(2,1)S(1)}, u32[]{:S(2)}, u32[]{:S(2)}) collective-permute-start(bf16[2,4,256,256]{3,2,1,0:T(8,128)(2,1)S(1)} %collective-permute-done.43.refs_13_.refs_8_), channel_id=1, source_target_pairs={{0,16},{16,0},{1,17},{17,1},{2,18},{18,2},{3,19},{19,3},{4,20},{20... | collective-permute-start | bytes 3145736 | tf_op jit(solution)/shard_map/ppermute | solution.py:435
  193.3 16.5 %collective-permute-start.39 = (bf16[320,1024]{1,0:T(8,128)(2,1)}, bf16[320,1024]{1,0:T(8,128)(2,1)S(1)}, u32[]{:S(2)}, u32[]{:S(2)}) collective-permute-start(bf16[320,1024]{1,0:T(8,128)(2,1)} %get-tuple-element.214), channel_id=1, source_target_pairs={{0,1},{1,0},{2,3},{3,2},{4,5},{5,4},{6,7},{7,6},{8,9},{9,8},{10,11... | collective-permute-start | bytes 1966088 | tf_op jit(solution)/shard_map/ppermute | solution.py:442
  193.3 18.0 %collective-permute-start.44 = (bf16[4,256,256]{2,1,0:T(8,128)(2,1)S(1)}, bf16[4,256,256]{2,1,0:T(8,128)(2,1)S(1)}, u32[]{:S(2)}, u32[]{:S(2)}) collective-permute-start(bf16[4,256,256]{2,1,0:T(8,128)(2,1)S(1)} %collective-permute-done.41.refs_10_.refs_5_), channel_id=1, source_target_pairs={{0,16},{16,0},{1,17},{17,1},{2,18},{18,2},{3,19},{19,3},{4,20},{20... | collective-permute-start | bytes 1572872 | tf_op jit(solution)/shard_map/ppermute | solution.py:435
  209.8 14.7 %collective-permute-start.48 = (f32[320,256]{1,0:T(8,128)S(1)}, f32[320,256]{1,0:T(8,128)S(1)}, u32[]{:S(2)}, u32[]{:S(2)}) collective-permute-start(f32[320,256]{1,0:T(8,128)S(1)} %get-tuple-element.223.refs_0_), channel_id=1, source_target_pairs={{0,1},{1,0},{2,3},{3,2},{4,5},{5,4},{6,7},{7,6},{8,9},{9,8},{10,11... | collective-permute-start | bytes 983048 | tf_op jit(solution)/shard_map/ppermute | solution.py:442
  210.0 15.2 %collective-permute-start.49 = (f32[320,256]{1,0:T(8,128)S(1)}, f32[320,256]{1,0:T(8,128)S(1)}, u32[]{:S(2)}, u32[]{:S(2)}) collective-permute-start(f32[320,256]{1,0:T(8,128)S(1)} %collective-permute-done.38.refs_1_), channel_id=1, source_target_pairs={{0,1},{1,0},{2,3},{3,2},{4,5},{5,4},{6,7},{7,6},{8,9},{9,8},{10,11... | collective-permute-start | bytes 983048 | tf_op jit(solution)/shard_map/ppermute | solution.py:442
  225.3 14.7 %collective-permute-start.50 = (bf16[320,1024]{1,0:T(8,128)(2,1)}, bf16[320,1024]{1,0:T(8,128)(2,1)S(1)}, u32[]{:S(2)}, u32[]{:S(2)}) collective-permute-start(bf16[320,1024]{1,0:T(8,128)(2,1)} %get-tuple-element.225), channel_id=1, source_target_pairs={{0,1},{1,0},{2,3},{3,2},{4,5},{5,4},{6,7},{7,6},{8,9},{9,8},{10,11... | collective-permute-start | bytes 1966088 | tf_op jit(solution)/shard_map/ppermute | solution.py:442
  267.4 31.3 %collective-permute-start.57 = (bf16[2,8,256,256]{3,2,1,0:T(8,128)(2,1)}, bf16[2,8,256,256]{3,2,1,0:T(8,128)(2,1)}, u32[]{:S(2)}, u32[]{:S(2)}) collective-permute-start(bf16[2,8,256,256]{3,2,1,0:T(8,128)(2,1)} %get-tuple-element.239), channel_id=1, source_target_pairs={{0,16},{16,0},{1,17},{17,1},{2,18},{18,2},{3,19},{19,3},{4,20},{20... | collective-permute-start | bytes 6291464 | tf_op jit(solution)/shard_map/ppermute | solution.py:435
  270.3 15.1 %collective-permute-start.58 = (bf16[8,256,256]{2,1,0:T(8,128)(2,1)}, bf16[8,256,256]{2,1,0:T(8,128)(2,1)S(1)}, u32[]{:S(2)}, u32[]{:S(2)}) collective-permute-start(bf16[8,256,256]{2,1,0:T(8,128)(2,1)} %get-tuple-element.241), channel_id=1, source_target_pairs={{0,16},{16,0},{1,17},{17,1},{2,18},{18,2},{3,19},{19,3},{4,20},{20... | collective-permute-start | bytes 3145736 | tf_op jit(solution)/shard_map/ppermute | solution.py:435
  285.3 20.4 %collective-permute-start.54 = (bf16[320,1024]{1,0:T(8,128)(2,1)}, bf16[320,1024]{1,0:T(8,128)(2,1)S(1)}, u32[]{:S(2)}, u32[]{:S(2)}) collective-permute-start(bf16[320,1024]{1,0:T(8,128)(2,1)} %get-tuple-element.252), channel_id=1, source_target_pairs={{0,1},{1,0},{2,3},{3,2},{4,5},{5,4},{6,7},{7,6},{8,9},{9,8},{10,11... | collective-permute-start | bytes 1966088 | tf_op jit(solution)/shard_map/ppermute | solution.py:442
  304.9 35.1 %collective-permute-start.64 = (bf16[2,8,256,256]{3,2,1,0:T(8,128)(2,1)}, bf16[2,8,256,256]{3,2,1,0:T(8,128)(2,1)}, u32[]{:S(2)}, u32[]{:S(2)}) collective-permute-start(bf16[2,8,256,256]{3,2,1,0:T(8,128)(2,1)} %shard_map.246), channel_id=1, source_target_pairs={{0,4},{1,5},{2,6},{3,7},{4,0},{5,1},{6,2},{7,3},{8,12},{9,13},{10,... | collective-permute-start | bytes 6291464 | tf_op jit(solution)/shard_map/ppermute | solution.py:454
  305.8 15.3 %collective-permute-start.60 = (bf16[4,256,256]{2,1,0:T(8,128)(2,1)S(1)}, bf16[4,256,256]{2,1,0:T(8,128)(2,1)S(1)}, u32[]{:S(2)}, u32[]{:S(2)}) collective-permute-start(bf16[4,256,256]{2,1,0:T(8,128)(2,1)S(1)} %add_convert_fusion.11), channel_id=1, source_target_pairs={{0,8},{1,9},{2,10},{3,11},{4,12},{5,13},{6,14},{7,15},{8,0},{9,1},... | collective-permute-start | bytes 1572872 | tf_op jit(solution)/shard_map/ppermute | solution.py:454
  325.0 22.2 %collective-permute-start.70 = (bf16[2,4,256,256]{3,2,1,0:T(8,128)(2,1)}, bf16[2,4,256,256]{3,2,1,0:T(8,128)(2,1)S(1)}, u32[]{:S(2)}, u32[]{:S(2)}) collective-permute-start(bf16[2,4,256,256]{3,2,1,0:T(8,128)(2,1)} %shard_map.250), channel_id=1, source_target_pairs={{0,4},{1,5},{2,6},{3,7},{4,0},{5,1},{6,2},{7,3},{8,12},{9,13},{10,... | collective-permute-start | bytes 3145736 | tf_op jit(solution)/shard_map/ppermute | solution.py:454
  334.9 24.8 %collective-permute-start.62 = (bf16[2,8,256,256]{3,2,1,0:T(8,128)(2,1)}, bf16[2,8,256,256]{3,2,1,0:T(8,128)(2,1)S(1)}, u32[]{:S(2)}, u32[]{:S(2)}) collective-permute-start(bf16[2,8,256,256]{3,2,1,0:T(8,128)(2,1)} %get-tuple-element.279), channel_id=1, source_target_pairs={{0,16},{16,0},{1,17},{17,1},{2,18},{18,2},{3,19},{19,3},{4,20},{20... | collective-permute-start | bytes 6291464 | tf_op jit(solution)/shard_map/ppermute | solution.py:435
  343.4 16.3 %collective-permute-start.61 = (bf16[320,1024]{1,0:T(8,128)(2,1)S(1)}, bf16[320,1024]{1,0:T(8,128)(2,1)S(1)}, u32[]{:S(2)}, u32[]{:S(2)}) collective-permute-start(bf16[320,1024]{1,0:T(8,128)(2,1)S(1)} %copy-done.58), channel_id=1, source_target_pairs={{0,1},{1,0},{2,3},{3,2},{4,5},{5,4},{6,7},{7,6},{8,9},{9,8},{10,11... | collective-permute-start | bytes 1966088 | tf_op jit(solution)/shard_map/ppermute | solution.py:442
  348.5 39.8 %collective-permute-start.71 = (bf16[2,2,256,256]{3,2,1,0:T(8,128)(2,1)}, bf16[2,2,256,256]{3,2,1,0:T(8,128)(2,1)}, u32[]{:S(2)}, u32[]{:S(2)}) collective-permute-start(bf16[2,2,256,256]{3,2,1,0:T(8,128)(2,1)} %broadcast_select_fusion.3), channel_id=1, source_target_pairs={{0,16},{16,0},{1,17},{17,1},{2,18},{18,2},{3,19},{19,3},{4,20},{20... | collective-permute-start | bytes 1572872 | tf_op jit(solution)/shard_map/ppermute | solution.py:435
  359.7 15.0 %collective-permute-start.66 = (bf16[8,256,256]{2,1,0:T(8,128)(2,1)S(1)}, bf16[8,256,256]{2,1,0:T(8,128)(2,1)S(1)}, u32[]{:S(2)}, u32[]{:S(2)}) collective-permute-start(bf16[8,256,256]{2,1,0:T(8,128)(2,1)S(1)} %add_convert_fusion.6), channel_id=1, source_target_pairs={{0,8},{1,9},{2,10},{3,11},{4,12},{5,13},{6,14},{7,15},{8,0},{9,1},... | collective-permute-start | bytes 3145736 | tf_op jit(solution)/shard_map/ppermute | solution.py:454
  360.8 29.7 %collective-permute-start.72 = (bf16[4,256,256]{2,1,0:T(8,128)(2,1)}, bf16[4,256,256]{2,1,0:T(8,128)(2,1)}, u32[]{:S(2)}, u32[]{:S(2)}) collective-permute-start(bf16[4,256,256]{2,1,0:T(8,128)(2,1)} %slice_bitcast_fusion.1), channel_id=1, source_target_pairs={{0,3},{1,2},{2,1},{3,0},{4,7},{5,6},{6,5},{7,4},{8,11},{9,10},{10,... | collective-permute-start | bytes 1572872 | tf_op jit(solution)/shard_map/ppermute | solution.py:430
  379.8 26.9 %collective-permute-start.74 = (bf16[2,8,256,256]{3,2,1,0:T(8,128)(2,1)}, bf16[2,8,256,256]{3,2,1,0:T(8,128)(2,1)S(1)}, u32[]{:S(2)}, u32[]{:S(2)}) collective-permute-start(bf16[2,8,256,256]{3,2,1,0:T(8,128)(2,1)} %shard_map.253), channel_id=1, source_target_pairs={{0,4},{1,5},{2,6},{3,7},{4,0},{5,1},{6,2},{7,3},{8,12},{9,13},{10,... | collective-permute-start | bytes 6291464 | tf_op jit(solution)/shard_map/ppermute | solution.py:454
  386.4 19.1 %collective-permute-start.68 = (bf16[2,4,256,256]{3,2,1,0:T(8,128)(2,1)}, bf16[2,4,256,256]{3,2,1,0:T(8,128)(2,1)S(1)}, u32[]{:S(2)}, u32[]{:S(2)}) collective-permute-start(bf16[2,4,256,256]{3,2,1,0:T(8,128)(2,1)} %get-tuple-element.300), channel_id=1, source_target_pairs={{0,16},{16,0},{1,17},{17,1},{2,18},{18,2},{3,19},{19,3},{4,20},{20... | collective-permute-start | bytes 3145736 | tf_op jit(solution)/shard_map/ppermute | solution.py:435
  389.7 15.8 %collective-permute-start.67 = (bf16[320,1024]{1,0:T(8,128)(2,1)S(1)}, bf16[320,1024]{1,0:T(8,128)(2,1)S(1)}, u32[]{:S(2)}, u32[]{:S(2)}) collective-permute-start(bf16[320,1024]{1,0:T(8,128)(2,1)S(1)} %copy-done.60), channel_id=1, source_target_pairs={{0,1},{1,0},{2,3},{3,2},{4,5},{5,4},{6,7},{7,6},{8,9},{9,8},{10,11... | collective-permute-start | bytes 1966088 | tf_op jit(solution)/shard_map/ppermute | solution.py:442
  390.6 21.8 %collective-permute-start.76 = (bf16[2,256,256]{2,1,0:T(8,128)(2,1)S(1)}, bf16[2,256,256]{2,1,0:T(8,128)(2,1)S(1)}, u32[]{:S(2)}, u32[]{:S(2)}) collective-permute-start(bf16[2,256,256]{2,1,0:T(8,128)(2,1)S(1)} %slice_bitcast_fusion.9), channel_id=1, source_target_pairs={{0,3},{1,2},{2,1},{3,0},{4,7},{5,6},{6,5},{7,4},{8,11},{9,10},{10,... | collective-permute-start | bytes 786440 | tf_op jit(solution)/shard_map/ppermute | solution.py:430
  424.8 19.9 %collective-permute-start.84 = (bf16[1344,256]{1,0:T(8,128)(2,1)S(1)}, bf16[1344,256]{1,0:T(8,128)(2,1)S(1)}, u32[]{:S(2)}, u32[]{:S(2)}) collective-permute-start(bf16[1344,256]{1,0:T(8,128)(2,1)S(1)} %pad_maximum_fusion.6), channel_id=1, source_target_pairs={{0,3},{1,2},{2,1},{3,0},{4,7},{5,6},{6,5},{7,4},{8,11},{9,10},{10,... | collective-permute-start | bytes 2064392 | tf_op jit(solution)/shard_map/ppermute | solution.py:430
  442.0 43.6 %collective-permute-start.88 = (bf16[2,256,256]{2,1,0:T(8,128)(2,1)}, bf16[2,256,256]{2,1,0:T(8,128)(2,1)}, u32[]{:S(2)}, u32[]{:S(2)}) collective-permute-start(bf16[2,256,256]{2,1,0:T(8,128)(2,1)} %fusion.9.refs_2_), channel_id=1, source_target_pairs={{0,16},{16,0},{1,17},{17,1},{2,18},{18,2},{3,19},{19,3},{4,20},{20... | collective-permute-start | bytes 786440 | tf_op jit(solution)/shard_map/ppermute | solution.py:435
  455.9 22.0 %collective-permute-start.85 = (f32[25,256]{1,0:T(8,128)S(1)}, f32[25,256]{1,0:T(8,128)S(1)}, u32[]{:S(2)}, u32[]{:S(2)}) collective-permute-start(f32[25,256]{1,0:T(8,128)S(1)} %bitcast.224), channel_id=1, source_target_pairs={{0,3},{1,2},{2,1},{3,0},{4,7},{5,6},{6,5},{7,4},{8,11},{9,10},{10,... | collective-permute-start | bytes 76808 | tf_op jit(solution)/shard_map/ppermute | solution.py:430
  458.0 20.1 %collective-permute-start.86 = (bf16[2,256,256]{2,1,0:T(8,128)(2,1)S(1)}, bf16[2,256,256]{2,1,0:T(8,128)(2,1)S(1)}, u32[]{:S(2)}, u32[]{:S(2)}) collective-permute-start(bf16[2,256,256]{2,1,0:T(8,128)(2,1)S(1)} %slice_bitcast_fusion.7), channel_id=1, source_target_pairs={{0,3},{1,2},{2,1},{3,0},{4,7},{5,6},{6,5},{7,4},{8,11},{9,10},{10,... | collective-permute-start | bytes 786440 | tf_op jit(solution)/shard_map/ppermute | solution.py:430
  (120 other events, 1025.4 us)
